TPU v7x, 32 devices: a whole 2x2x4 slice. The times are simulated.
32 devices in a mesh: lat: 8 (over z, x), lev: 4 (over y, core).
Axes of the slice: x: 2, y: 2, z: 4, core: 2. Of those that a mesh axis runs over, the one named last changes fastest.
Arguments:
- grid_field: bfloat16 [8, 1280, 128], P('lev', 'lat'), may hold values from -6 to 6
- send_blocks: int32 [8, 2, 32], P('lat'), may hold values from 0 to 159
- donor_index: int32 [1280, 2], P('lat'), may hold values from 0 to 223
- tile_choice: int32 [1280, 2], P('lat'), may hold values from 0 to 7
- kernel_tiles: bfloat16 [8, 128, 128], replicated, may hold values from -0.375 to 0.375
- circle_len: int32 [32], replicated, may hold values from 20 to 5120, as said below
- slot_wave: int32 [1280], replicated, may hold values from 0 to 1279, each once
- legendre: bfloat16 [1280, 32, 1280], P(('lat', 'lev')), may hold values from -0.01171875 to 0.01171875
Outputs:
- spectra: bfloat16 [8, 2, 1280, 1280], P(None, None, ('lat', 'lev'))
Inputs may be any that keep to these rules, and one draw needn't show every extreme that they name: `circle_len`: each circle has 4 i + 16 points for a whole i of 1 or more, and some circle has 5120.
All inputs are finite; a program needn't handle non-finite values.
Results may differ from a plain program's by a relative error of at most 0.007.
Values may be sent and summed in bfloat16 or wider, within the bound.
No kernel may reach another device: no remote copies, remote signals or barrier semaphores. Data moves between devices by JAX's collectives and lax.ppermute only.
A program may use at most 64 MiB of HBM per device.

v0:
```python
import math

import jax
import jax.numpy as jnp
from jax import lax
from jax.sharding import PartitionSpec as P

PTS = 5120


def extended(array, sides, width):
    for axis, dim in sides:
        size, length = (lax.axis_size(axis), array.shape[dim])
        up = [(i, (i + 1) % size) for i in range(size - 1)]
        down = [(j, i) for i, j in up]
        last = lax.slice_in_dim(array, length - width, length, axis=dim)
        leading = lax.slice_in_dim(array, 0, width, axis=dim)
        before = lax.ppermute(last, axis, up)
        after = lax.ppermute(leading, axis, down)
        array = jnp.concatenate([before, array, after], axis=dim)
    return array


def circle_table(length, waves, points, top_wave):
    live_slot = (waves >= 1) & (waves < top_wave) & (2 * waves < length)
    step_angle = 2.0 * math.pi / length.astype(jnp.float32)
    coarse = jnp.arange(points // 128, dtype=jnp.int32) * 128
    fine_pos = jnp.arange(128, dtype=jnp.int32)
    angle_hi = (coarse[:, None] * waves[None, :] % length).astype(jnp.float32) * step_angle
    lower_angle = (fine_pos[:, None] * waves[None, :] % length).astype(jnp.float32) * step_angle
    cos_hi = jnp.cos(angle_hi)[:, None, :]
    sin_hi = jnp.sin(angle_hi)[:, None, :]
    cos_lo = jnp.cos(lower_angle)[None]
    sin_lo = jnp.sin(lower_angle)[None]
    cosine = (cos_hi * cos_lo - sin_hi * sin_lo).reshape(points, -1)
    sine_part = (sin_hi * cos_lo + cos_hi * sin_lo).reshape(points, -1)
    keep_mask = (jnp.arange(points, dtype=jnp.int32) < length)[:, None] & live_slot[None, :]
    return jnp.concatenate(
        [jnp.where(keep_mask, cosine, 0.0), jnp.where(keep_mask, -sine_part, 0.0)], axis=1
    ).astype(jnp.bfloat16)


def transform(values, lengths, waves, top_wave):
    row_count = values.shape[0]
    points = values.shape[2]
    slot_count = waves.shape[0]
    blocks = slot_count // 128
    wave_blocks = waves.reshape(blocks, 128)

    def per_circle(operands):
        circle_vals, length = operands

        def per_block(wave_part):
            factors = circle_table(length, wave_part, points, top_wave)
            return jnp.dot(circle_vals, factors, preferred_element_type=jnp.float32).astype(
                jnp.bfloat16
            )

        pieces = lax.map(per_block, wave_blocks)
        return (
            pieces.reshape(blocks, row_count, 2, 128)
            .transpose(1, 2, 0, 3)
            .reshape(row_count, 2, slot_count)
        )

    result = lax.map(per_circle, (jnp.moveaxis(values, 1, 0), lengths))
    return result.transpose(1, 2, 0, 3)


def body(
    grid_field, send_blocks, donor_index, tile_choice, kernel_tiles, circle_len, slot_wave, legendre
):
    level_dev, band_blocks, lane_width = grid_field.shape
    send_count = send_blocks.shape[2]
    tile_count = kernel_tiles.shape[0]
    top_wave = legendre.shape[2]
    slot_per_device = legendre.shape[0]
    circ_band = band_blocks * lane_width // PTS
    band_index = lax.axis_index("lat")
    level_index = lax.axis_index("lev")
    level_groups = lax.axis_size("lev")
    outgoing = jnp.take(grid_field, send_blocks[0].reshape(-1), axis=1)
    widened_values = extended(outgoing, (("lat", 1),), send_count)
    donor_pool = jnp.concatenate(
        [grid_field, widened_values[:, :send_count], widened_values[:, 3 * send_count :]], axis=1
    )
    picked = jnp.take(donor_pool, donor_index.reshape(-1), axis=1).reshape(
        level_dev, band_blocks, 2, 1, lane_width
    )
    chosen = tile_choice[:, :, None] == jnp.arange(tile_count, dtype=jnp.int32)
    spread = jnp.where(chosen[None, :, :, :, None], picked, jnp.zeros((), jnp.bfloat16))
    spread = spread.reshape(level_dev * band_blocks, 2 * tile_count * lane_width)
    stacked = jnp.broadcast_to(kernel_tiles[None], (2, tile_count, lane_width, lane_width)).reshape(
        2 * tile_count * lane_width, lane_width
    )
    arrival = jnp.dot(spread, stacked, preferred_element_type=jnp.float32)
    squared = (arrival * arrival).astype(jnp.bfloat16).reshape(level_dev, circ_band, PTS)
    grouped = lax.all_to_all(squared, "lev", split_axis=1, concat_axis=0, tiled=True)
    circ_dev = circ_band // level_groups
    first_circle = band_index * circ_band + level_index * circ_dev
    lengths = lax.dynamic_slice_in_dim(circle_len, first_circle, circ_dev)
    coeffs = transform(grouped, lengths, slot_wave, top_wave)
    levels = coeffs.shape[0]
    slot_count = coeffs.shape[3]
    coeffs = coeffs.reshape(levels, 2, 1, 1, circ_dev, slot_count)
    arrived = lax.all_to_all(
        lax.all_to_all(coeffs, "lat", split_axis=5, concat_axis=2, tiled=True),
        "lev",
        split_axis=5,
        concat_axis=3,
        tiled=True,
    )
    gathered = arrived.reshape(levels, 2, -1, slot_per_device)
    spectra = jnp.einsum("lcgs,sgn->lcsn", gathered, legendre, preferred_element_type=jnp.float32)
    first_slot = (band_index * level_groups + level_index) * slot_per_device
    my_waves = lax.dynamic_slice_in_dim(slot_wave, first_slot, slot_per_device)
    allowed = jnp.arange(top_wave, dtype=jnp.int32)[None, :] >= my_waves[:, None]
    return jnp.where(allowed[None, None], spectra, 0.0).astype(jnp.bfloat16)


def solution(mesh):
    return jax.shard_map(
        body,
        mesh=mesh,
        in_specs=(
            P("lev", "lat", None),
            P("lat", None, None),
            P("lat", None),
            P("lat", None),
            P(),
            P(),
            P(),
            P(("lat", "lev"), None, None),
        ),
        out_specs=P(None, None, ("lat", "lev"), None),
        check_vma=False,
    )
```

profile of v0, /device:TPU:0, one launch (start us, length us, event | category | flops | bytes accessed | tf_op | source)
XLA Modules:
  0.0 153.1 jit_solution(6161142448545435737)
XLA Ops:
  3.5 4.8 %collective-permute-start = (bf16[2,32,128]{2,1,0:T(8,128)(2,1)S(1)}, bf16[2,32,128]{2,1,0:T(8,128)(2,1)S(1)}, u32[]{:S(2)}, u32[]{:S(2)}) collective-permute-start(bf16[2,32,128]{2,1,0:T(8,128)(2,1)S(1)} %get-tuple-element.122), channel_id=1, source_target_pairs={{0,4},{4,8},{8,12},{12,16},{16,20},{20,24},{24,28},{1,5},{5,9},{9,... | collective-permute-start | bytes 49160 | tf_op jit(solution)/shard_map/ppermute | solution.py:18
  15.5 2.1 %gather_fusion.1 = bf16[320,2,128]{2,1,0:T(2,128)(2,1)S(1)} fusion(bf16[2,224,128]{2,0,1:T(2,128)(2,1)S(1)} %pad_maximum_fusion, s32[1024]{0:T(1024)} %pad_clamp_fusion), kind=kCustom, calls=%fused_computation.1 | custom fusion | bytes 328960 | tf_op jit(solution)/shard_map/jit(_take)/gather | solution.py:87
  18.9 2.1 %broadcast_select_fusion = bf16[2,160,2,8,128]{4,3,2,1,0:T(8,128)(2,1)} fusion(pred[160,2,8]{2,1,0:T(4,128)(4,1)} %iota_compare_fusion.2, bf16[2,160,2,128]{3,2,1,0:T(2,128)(2,1)S(1)} %copy.31), kind=kLoop, calls=%fused_computation.45 | loop fusion | flops 655360 | bytes 1477120 | tf_op jit(solution)/shard_map/jit(_where)/select_n | solution.py:91
  21.0 3.3 %select_n.130 = bf16[320,2048]{1,0:T(8,128)(2,1)} reshape(bf16[2,160,2,8,128]{4,3,2,1,0:T(8,128)(2,1)} %broadcast_select_fusion) | data formatting | bytes 2621440 | tf_op jit(solution)/shard_map/jit(_where)/select_n | solution.py:91
  24.4 1.8 %fusion.40 = bf16[320,128]{1,0:T(8,128)(2,1)S(1)} fusion(bf16[320,2048]{1,0:T(8,128)(2,1)} %select_n.130, bf16[2048,128]{1,0:T(8,128)(2,1)S(1)} %bitcast.74), kind=kOutput, calls=%fused_computation.47 | convolution fusion | flops 167854080 | bytes 1916928 | tf_op jit(solution)/shard_map/dot_general | solution.py:96
  27.0 3.3 %all-to-all-start = ((bf16[2,4,5120]{2,0,1:T(2,128)(2,1)}), bf16[2,4,5120]{2,0,1:T(2,128)(2,1)S(1)}, u32[]{:S(2)}, u32[]{:S(2)}) async-start(bf16[2,4,5120]{2,0,1:T(2,128)(2,1)} %copy.32), calls=%async_computation | async-start | bytes 163840 | tf_op jit(solution)/shard_map/all_to_all | solution.py:98
  34.5 79.9 %while.19 = (s32[]{:T(128)}, bf16[10,8,256]{2,1,0:T(8,128)(2,1)S(1)}, s32[]{:T(128)}, s32[10,128]{1,0:T(8,128)}, s32[]{:T(128)}, /*index=5*/pred[]{:T(512)}, f32[]{:T(128)}, bf16[8,5120]{1,0:T(8,128)(2,1)S(1)}, s32[]{:T(128)}) while((s32[]{:T(128)}, bf16[10,8,256]{2,1,0:T(8,128)(2,1)S(1)}, s32[]{:T(128)}, s32[10,128]{1,0:T(8,128)}, s32[]{:T(128)}, ...), condition=%wide.region_1.2_spmd, body=%wide.region_0.1_spmd.sunk | while | flops 34301736 | bytes 10929347 | solution.py:59
  39.3 2.7 %fusion.60 = (bf16[5120,128]{1,0:T(8,128)(2,1)S(1)}, bf16[5120,128]{1,0:T(8,128)(2,1)S(1)}) fusion(bf16[40,128,128]{2,1,0:T(8,128)(2,1)S(1)} %get-tuple-element.185, pred[128]{0:T(512)(128)(4,1)S(1)} %and_bitcast_fusion.2, pred[5120]{0:T(1024)(128)(4,1)S(1)} %iota_compare_fusion.4, bf16[40,128,128]{2,1,0:T(8,128)(2,1)S(1)} %get-tuple-element.186), kind=kLoop, calls=%fused_computation.4.clone.1 | loop fusion | flops 1966080 | bytes 5248128 | tf_op jit(solution)/shard_map/convert
  47.3 2.7 %fusion.60 = (bf16[5120,128]{1,0:T(8,128)(2,1)S(1)}, bf16[5120,128]{1,0:T(8,128)(2,1)S(1)}) fusion(bf16[40,128,128]{2,1,0:T(8,128)(2,1)S(1)} %get-tuple-element.185, pred[128]{0:T(512)(128)(4,1)S(1)} %and_bitcast_fusion.2, pred[5120]{0:T(1024)(128)(4,1)S(1)} %iota_compare_fusion.4, bf16[40,128,128]{2,1,0:T(8,128)(2,1)S(1)} %get-tuple-element.186), kind=kLoop, calls=%fused_computation.4.clone.1 | loop fusion | flops 1966080 | bytes 5248128 | tf_op jit(solution)/shard_map/convert
  55.3 2.7 %fusion.60 = (bf16[5120,128]{1,0:T(8,128)(2,1)S(1)}, bf16[5120,128]{1,0:T(8,128)(2,1)S(1)}) fusion(bf16[40,128,128]{2,1,0:T(8,128)(2,1)S(1)} %get-tuple-element.185, pred[128]{0:T(512)(128)(4,1)S(1)} %and_bitcast_fusion.2, pred[5120]{0:T(1024)(128)(4,1)S(1)} %iota_compare_fusion.4, bf16[40,128,128]{2,1,0:T(8,128)(2,1)S(1)} %get-tuple-element.186), kind=kLoop, calls=%fused_computation.4.clone.1 | loop fusion | flops 1966080 | bytes 5248128 | tf_op jit(solution)/shard_map/convert
  63.3 2.7 %fusion.60 = (bf16[5120,128]{1,0:T(8,128)(2,1)S(1)}, bf16[5120,128]{1,0:T(8,128)(2,1)S(1)}) fusion(bf16[40,128,128]{2,1,0:T(8,128)(2,1)S(1)} %get-tuple-element.185, pred[128]{0:T(512)(128)(4,1)S(1)} %and_bitcast_fusion.2, pred[5120]{0:T(1024)(128)(4,1)S(1)} %iota_compare_fusion.4, bf16[40,128,128]{2,1,0:T(8,128)(2,1)S(1)} %get-tuple-element.186), kind=kLoop, calls=%fused_computation.4.clone.1 | loop fusion | flops 1966080 | bytes 5248128 | tf_op jit(solution)/shard_map/convert
  71.3 2.7 %fusion.60 = (bf16[5120,128]{1,0:T(8,128)(2,1)S(1)}, bf16[5120,128]{1,0:T(8,128)(2,1)S(1)}) fusion(bf16[40,128,128]{2,1,0:T(8,128)(2,1)S(1)} %get-tuple-element.185, pred[128]{0:T(512)(128)(4,1)S(1)} %and_bitcast_fusion.2, pred[5120]{0:T(1024)(128)(4,1)S(1)} %iota_compare_fusion.4, bf16[40,128,128]{2,1,0:T(8,128)(2,1)S(1)} %get-tuple-element.186), kind=kLoop, calls=%fused_computation.4.clone.1 | loop fusion | flops 1966080 | bytes 5248128 | tf_op jit(solution)/shard_map/convert
  79.3 2.7 %fusion.60 = (bf16[5120,128]{1,0:T(8,128)(2,1)S(1)}, bf16[5120,128]{1,0:T(8,128)(2,1)S(1)}) fusion(bf16[40,128,128]{2,1,0:T(8,128)(2,1)S(1)} %get-tuple-element.185, pred[128]{0:T(512)(128)(4,1)S(1)} %and_bitcast_fusion.2, pred[5120]{0:T(1024)(128)(4,1)S(1)} %iota_compare_fusion.4, bf16[40,128,128]{2,1,0:T(8,128)(2,1)S(1)} %get-tuple-element.186), kind=kLoop, calls=%fused_computation.4.clone.1 | loop fusion | flops 1966080 | bytes 5248128 | tf_op jit(solution)/shard_map/convert
  87.3 2.7 %fusion.60 = (bf16[5120,128]{1,0:T(8,128)(2,1)S(1)}, bf16[5120,128]{1,0:T(8,128)(2,1)S(1)}) fusion(bf16[40,128,128]{2,1,0:T(8,128)(2,1)S(1)} %get-tuple-element.185, pred[128]{0:T(512)(128)(4,1)S(1)} %and_bitcast_fusion.2, pred[5120]{0:T(1024)(128)(4,1)S(1)} %iota_compare_fusion.4, bf16[40,128,128]{2,1,0:T(8,128)(2,1)S(1)} %get-tuple-element.186), kind=kLoop, calls=%fused_computation.4.clone.1 | loop fusion | flops 1966080 | bytes 5248128 | tf_op jit(solution)/shard_map/convert
  95.3 2.7 %fusion.60 = (bf16[5120,128]{1,0:T(8,128)(2,1)S(1)}, bf16[5120,128]{1,0:T(8,128)(2,1)S(1)}) fusion(bf16[40,128,128]{2,1,0:T(8,128)(2,1)S(1)} %get-tuple-element.185, pred[128]{0:T(512)(128)(4,1)S(1)} %and_bitcast_fusion.2, pred[5120]{0:T(1024)(128)(4,1)S(1)} %iota_compare_fusion.4, bf16[40,128,128]{2,1,0:T(8,128)(2,1)S(1)} %get-tuple-element.186), kind=kLoop, calls=%fused_computation.4.clone.1 | loop fusion | flops 1966080 | bytes 5248128 | tf_op jit(solution)/shard_map/convert
  103.3 2.7 %fusion.60 = (bf16[5120,128]{1,0:T(8,128)(2,1)S(1)}, bf16[5120,128]{1,0:T(8,128)(2,1)S(1)}) fusion(bf16[40,128,128]{2,1,0:T(8,128)(2,1)S(1)} %get-tuple-element.185, pred[128]{0:T(512)(128)(4,1)S(1)} %and_bitcast_fusion.2, pred[5120]{0:T(1024)(128)(4,1)S(1)} %iota_compare_fusion.4, bf16[40,128,128]{2,1,0:T(8,128)(2,1)S(1)} %get-tuple-element.186), kind=kLoop, calls=%fused_computation.4.clone.1 | loop fusion | flops 1966080 | bytes 5248128 | tf_op jit(solution)/shard_map/convert
  111.3 2.7 %fusion.60 = (bf16[5120,128]{1,0:T(8,128)(2,1)S(1)}, bf16[5120,128]{1,0:T(8,128)(2,1)S(1)}) fusion(bf16[40,128,128]{2,1,0:T(8,128)(2,1)S(1)} %get-tuple-element.185, pred[128]{0:T(512)(128)(4,1)S(1)} %and_bitcast_fusion.2, pred[5120]{0:T(1024)(128)(4,1)S(1)} %iota_compare_fusion.4, bf16[40,128,128]{2,1,0:T(8,128)(2,1)S(1)} %get-tuple-element.186), kind=kLoop, calls=%fused_computation.4.clone.1 | loop fusion | flops 1966080 | bytes 5248128 | tf_op jit(solution)/shard_map/convert
  115.6 2.3 %reshape.325 = bf16[8,2,1280]{2,1,0:T(2,128)(2,1)} reshape(bf16[1280,1,1,1,2,8]{5,4,3,2,1,0:T(2,128)(2,1)} %bitcast.70) | data formatting | bytes 81920
  117.9 7.0 %all-to-all-start.1 = ((bf16[8,2,1280]{2,1,0:T(2,128)(2,1)}), bf16[8,2,1280]{2,1,0:T(2,128)(2,1)S(1)}, u32[]{:S(2)}, u32[]{:S(2)}) async-start(bf16[8,2,1280]{2,1,0:T(2,128)(2,1)} %reshape.325), calls=%async_computation.1 | async-start | bytes 81920 | tf_op jit(solution)/shard_map/all_to_all | solution.py:107
  125.7 6.0 %all-to-all-done.1 = bf16[8,2,1280]{2,1,0:T(2,128)(2,1)S(1)} async-done(((bf16[8,2,1280]{2,1,0:T(2,128)(2,1)}), bf16[8,2,1280]{2,1,0:T(2,128)(2,1)S(1)}, u32[]{:S(2)}, u32[]{:S(2)}) %all-to-all-start.1) | async-done | bytes 40992 | tf_op jit(solution)/shard_map/all_to_all | solution.py:107
  133.2 3.0 %copy.36 = bf16[8,2,8,1,1,160]{2,0,1,4,3,5:T(8,128)(2,1)} copy(bf16[8,2,8,1,1,160]{0,1,5,2,4,3:T(2,128)(2,1)} %bitcast.71) | data formatting | bytes 81920 | tf_op jit(solution)/shard_map/all_to_all | solution.py:107
  136.2 2.3 %reshape.327 = bf16[4,2,2560]{2,1,0:T(2,128)(2,1)} reshape(bf16[160,1,1,2,8,8]{5,4,3,2,1,0:T(8,128)(2,1)} %bitcast.72) | data formatting | bytes 81920
  138.6 3.3 %all-to-all-start.2 = ((bf16[4,2,2560]{2,1,0:T(2,128)(2,1)}), bf16[4,2,2560]{2,1,0:T(2,128)(2,1)S(1)}, u32[]{:S(2)}, u32[]{:S(2)}) async-start(bf16[4,2,2560]{2,1,0:T(2,128)(2,1)} %reshape.327), calls=%async_computation.2 | async-start | bytes 81920 | tf_op jit(solution)/shard_map/all_to_all | solution.py:106
  141.9 3.9 %all-to-all-done.2 = bf16[4,2,2560]{2,1,0:T(2,128)(2,1)S(1)} async-done(((bf16[4,2,2560]{2,1,0:T(2,128)(2,1)}), bf16[4,2,2560]{2,1,0:T(2,128)(2,1)S(1)}, u32[]{:S(2)}, u32[]{:S(2)}) %all-to-all-start.2) | async-done | bytes 40992 | tf_op jit(solution)/shard_map/all_to_all | solution.py:106
  (128 shorter events, 78.4 us)
Async XLA Ops:
  0.0 150.9 %copy-start = (bf16[40,32,1280]{2,1,0:T(8,128)(2,1)S(1)}, bf16[40,32,1280]{2,1,0:T(8,128)(2,1)}, u32[]{:S(2)}) copy-start(bf16[40,32,1280]{2,1,0:T(8,128)(2,1)} %param.17) | copy-start | bytes 9830404
  3.5 11.7 %collective-permute-start = (bf16[2,32,128]{2,1,0:T(8,128)(2,1)S(1)}, bf16[2,32,128]{2,1,0:T(8,128)(2,1)S(1)}, u32[]{:S(2)}, u32[]{:S(2)}) collective-permute-start(bf16[2,32,128]{2,1,0:T(8,128)(2,1)S(1)} %get-tuple-element.122), channel_id=1, source_target_pairs={{0,4},{4,8},{8,12},{12,16},{16,20},{20,24},{24,28},{1,5},{5,9},{9,... | collective-permute-start | bytes 49160 | tf_op jit(solution)/shard_map/ppermute | solution.py:18
  8.3 6.9 %collective-permute-start.1 = (bf16[2,32,128]{2,1,0:T(8,128)(2,1)S(1)}, bf16[2,32,128]{2,1,0:T(8,128)(2,1)S(1)}, u32[]{:S(2)}, u32[]{:S(2)}) collective-permute-start(bf16[2,32,128]{2,1,0:T(8,128)(2,1)S(1)} %get-tuple-element.123), channel_id=1, source_target_pairs={{4,0},{8,4},{12,8},{16,12},{20,16},{24,20},{28,24},{5,1},{9,5},{13... | collective-permute-start | bytes 49160 | tf_op jit(solution)/shard_map/ppermute | solution.py:19
  18.8 5.5 %copy-start.1 = (bf16[8,128,128]{2,1,0:T(8,128)(2,1)S(1)}, bf16[8,128,128]{2,1,0:T(8,128)(2,1)}, u32[]{:S(2)}) copy-start(bf16[8,128,128]{2,1,0:T(8,128)(2,1)} %param.14) | copy-start | bytes 786436
  21.0 9.2 %copy-start.2 = (s32[32]{0:T(128)S(1)}, s32[32]{0:T(128)}, u32[]{:S(2)}) copy-start(s32[32]{0:T(128)} %param.15) | copy-start | bytes 388
  27.0 7.5 %all-to-all-start = ((bf16[2,4,5120]{2,0,1:T(2,128)(2,1)}), bf16[2,4,5120]{2,0,1:T(2,128)(2,1)S(1)}, u32[]{:S(2)}, u32[]{:S(2)}) async-start(bf16[2,4,5120]{2,0,1:T(2,128)(2,1)} %copy.32), calls=%async_computation | async-start | bytes 163840 | tf_op jit(solution)/shard_map/all_to_all | solution.py:98
  117.9 13.7 %all-to-all-start.1 = ((bf16[8,2,1280]{2,1,0:T(2,128)(2,1)}), bf16[8,2,1280]{2,1,0:T(2,128)(2,1)S(1)}, u32[]{:S(2)}, u32[]{:S(2)}) async-start(bf16[8,2,1280]{2,1,0:T(2,128)(2,1)} %reshape.325), calls=%async_computation.1 | async-start | bytes 81920 | tf_op jit(solution)/shard_map/all_to_all | solution.py:107
  138.6 7.2 %all-to-all-start.2 = ((bf16[4,2,2560]{2,1,0:T(2,128)(2,1)}), bf16[4,2,2560]{2,1,0:T(2,128)(2,1)S(1)}, u32[]{:S(2)}, u32[]{:S(2)}) async-start(bf16[4,2,2560]{2,1,0:T(2,128)(2,1)} %reshape.327), calls=%async_computation.2 | async-start | bytes 81920 | tf_op jit(solution)/shard_map/all_to_all | solution.py:106
where the time goes:
time: 155 us; the launch traced here: 153 us
  other arithmetic  74 us (48%)
  local copies, waits for them, and re-layouts  38.7 us (25%)
  starting transfers between devices  19.7 us (13%)
  waiting for transfers between devices  11.4 us (7%)
  matrix products  6.93 us (4%)
  between operations  2.16 us (1%)
    another operation x11, other arithmetic  27 us
    and x10, other arithmetic, circle_table(): (jnp.arange(points, dtype=jnp.int32) < length)[:, None] & live_slot[None, :]  13.3 us
    unnamed x13, local copies, waits for them, and re-layouts  10.4 us
    cos x10, other arithmetic, circle_table(): cos_lo = jnp.cos(lower_angle)[None]  9.2 us
    sub x10, other arithmetic, circle_table(): cosine = (cos_hi * cos_lo - sin_hi * sin_lo).reshape(points, -1)  8.11 us
    mul x10, local copies, waits for them, and re-layouts, circle_table(): coarse[:, None] * waves[None, :] % length  7 us
    all_to_all x1, starting transfers between devices, body(): lax.all_to_all(coeffs, 'lat', split_axis=5, concat_axis=2, tiled=True)  6.96 us
    lt x10, other arithmetic, circle_table(): jnp.arange(points, dtype=jnp.int32) < length  6.35 us
  transfers between devices with their start and end apart: 5, of which 3 were waited for; matrix products, arithmetic and copies ran while one was open for 5% of the time, Pallas kernels for 0%

commit v1 on v0

v1 whole, which is shorter than its diff:
```python
import functools
import math

import jax
import jax.numpy as jnp
from jax import lax
from jax.experimental import pallas as pl
from jax.experimental.pallas import tpu as pltpu
from jax.sharding import PartitionSpec as P

PTS = 5120
LANES = 128
BF16 = jnp.bfloat16
F32 = jnp.float32
VMEM = pl.BlockSpec(memory_space=pltpu.VMEM)
SMEM = pl.BlockSpec(memory_space=pltpu.SMEM)
CONTRACT_ROWS = (((0,), (0,)), ((), ()))


def params(mebibytes):
    return pltpu.CompilerParams(vmem_limit_bytes=mebibytes << 20)


def one_hot(condition):
    return jnp.where(condition, 1.0, 0.0).astype(BF16)


def side_by_side(field_ref):
    return jnp.concatenate([field_ref[l] for l in range(field_ref.shape[0])], axis=1)


def outgoing_kernel(send_ref, field_ref, first_ref, second_ref):
    even = lax.rem(lax.axis_index("lat"), 2) == 0
    own = side_by_side(field_ref)
    blocks, count = own.shape[0], send_ref.shape[2]
    rows = lax.broadcasted_iota(jnp.int32, (blocks, count), 0)
    below, above = send_ref[0, 0:1, :], send_ref[0, 1:2, :]
    for ref, listed in (
        (first_ref, jnp.where(even, above, below)),
        (second_ref, jnp.where(even, below, above)),
    ):
        picked = lax.dot_general(
            one_hot(rows == listed), own, CONTRACT_ROWS, preferred_element_type=F32
        )
        ref[...] = picked.astype(BF16)


def turn(steps, waves, length, inverse):
    phase = steps * waves
    rest = phase - jnp.round(phase * inverse) * length
    f = rest * inverse
    x = f * f
    s = math.pi ** 11 / -math.factorial(11)
    for k in (9, 7, 5, 3, 1):
        s = s * x + (-1) ** (k // 2) * math.pi**k / math.factorial(k)
    s = s * f
    c = math.pi ** 10 / -math.factorial(10)
    for k in (8, 6, 4, 2, 0):
        c = c * x + (-1) ** (k // 2) * math.pi**k / math.factorial(k)
    return 1.0 - 2.0 * (s * s), 2.0 * (s * c)


def times(a, b):
    return a[0] * b[0] - a[1] * b[1], a[0] * b[1] + a[1] * b[0]


def table_kernel(length_ref, wave_ref, fine_ref, coarse_ref):
    circles, tiles = fine_ref.shape[:2]
    coarse = coarse_ref.shape[2]
    band = lax.axis_index("lat")
    step = lax.broadcasted_iota(jnp.int32, (8, LANES), 0).astype(F32)

    def doubled(base, factor_of, groups):
        out = [base]
        while len(out) < groups:
            out += [times(e, factor_of(len(out))) for e in out[: groups - len(out)]]
        return out

    def one(index, _):
        g, t = index // tiles, lax.rem(index, tiles)
        length = jnp.full((8, LANES), length_ref[band * circles + g], jnp.int32).astype(F32)
        inverse = 1.0 / length
        waves = jnp.broadcast_to(wave_ref[pl.ds(t, 1), :], (8, LANES)).astype(F32)
        hop_steps = jnp.left_shift(8, lax.broadcasted_iota(jnp.int32, (8, LANES), 0)).astype(F32)
        hops = turn(hop_steps, waves, length, inverse)
        far = turn(hop_steps * float(LANES), waves, length, inverse)

        def hop(table):
            def factor(groups):
                k = groups.bit_length() - 1
                return tuple(jnp.broadcast_to(x[k : k + 1], (8, LANES)) for x in table)

            return factor

        fine = doubled(turn(step, waves, length, inverse), hop(hops), LANES // 8)
        fine_ref[g, t] = jnp.concatenate(
            [jnp.concatenate([e[p] for e in fine], axis=0) for p in range(2)], axis=1
        ).astype(BF16)
        wide = doubled(turn(step * float(LANES), waves, length, inverse), hop(far), coarse // 8)
        coarse_ref[g, t] = jnp.concatenate(
            [jnp.concatenate([e[p] for e in wide], axis=0) for p in range(2)], axis=1
        )
        return 0

    lax.fori_loop(0, circles * tiles, one, 0, unroll=2)


def transform_kernel(
    length_ref, donor_ref, tile_ref, field_ref, first_ref, second_ref, kernels_ref, wave_ref,
    fine_ref, coarse_ref, out_ref, points_ref, coeff_ref, *, top_wave,
):
    levels, blocks = field_ref.shape[:2]
    circles, tiles = fine_ref.shape[:2]
    coarse = coarse_ref.shape[2]
    kinds = kernels_ref.shape[0]
    band = lax.axis_index("lat")
    even = lax.rem(band, 2) == 0

    first, second = first_ref[...], second_ref[...]
    below, above = jnp.where(even, second, first), jnp.where(even, first, second)
    pool = jnp.concatenate([side_by_side(field_ref), below, above], axis=0)

    listed = jnp.concatenate(
        [donor_ref[...], tile_ref[...], jnp.zeros((4, blocks), jnp.int32)], axis=0
    )
    columns = jnp.transpose(listed.astype(F32))
    lane = lax.broadcasted_iota(jnp.int32, (blocks, pool.shape[0]), 1).astype(F32)
    stacked = jnp.concatenate([kernels_ref[k] for k in range(kinds)], axis=1)
    arrival = [jnp.zeros((blocks, LANES), F32) for _ in range(levels)]
    for k in range(2):
        picked = jnp.dot(
            one_hot(lane == columns[:, k : k + 1]), pool, preferred_element_type=F32
        ).astype(BF16)
        kind = jnp.broadcast_to(columns[:, 2 + k : 3 + k], (blocks, LANES))
        for l in range(levels):
            every = jnp.dot(
                picked[:, l * LANES : (l + 1) * LANES], stacked, preferred_element_type=F32
            )
            value = every[:, :LANES]
            for q in range(1, kinds):
                value = jnp.where(kind == float(q), every[:, q * LANES : (q + 1) * LANES], value)
            arrival[l] = arrival[l] + value

    position = lax.broadcasted_iota(jnp.int32, (coarse, LANES), 0) * LANES
    position = position + lax.broadcasted_iota(jnp.int32, (coarse, LANES), 1)
    for g in range(circles):
        inside = position < length_ref[band * circles + g]
        for l in range(levels):
            part = arrival[l][g * coarse : (g + 1) * coarse]
            points_ref[g, l * coarse : (l + 1) * coarse] = jnp.where(inside, part * part, 0.0)

    def circle(g, _):
        length = length_ref[band * circles + g]
        points = points_ref[g].astype(BF16)
        for t in range(tiles):
            near = jnp.dot(points, fine_ref[g, t], preferred_element_type=F32)
            c, s = coarse_ref[g, t, :, :LANES], coarse_ref[g, t, :, LANES:]
            waves = wave_ref[t : t + 1, :]
            live = (waves >= 1) & (waves < top_wave) & (2 * waves < length)
            for l in range(levels):
                here = near[l * coarse : (l + 1) * coarse]
                a, b = here[:, :LANES], here[:, LANES:]
                real = jnp.sum(a * c - b * s, axis=0, keepdims=True)
                imag = jnp.sum(a * s + b * c, axis=0, keepdims=True)
                for part, value in ((0, real), (1, -imag)):
                    row = (l * 2 + part) * circles + g
                    coeff_ref[t, pl.ds(row, 1), :LANES] = jnp.where(live, value, 0.0)
        return 0

    lax.fori_loop(0, circles, circle, 0, unroll=circles * tiles <= 64)

    devices, height, _ = out_ref.shape
    width = tiles * LANES // devices
    packs = coeff_ref.shape[1] // height
    step = LANES // packs
    lane = lax.broadcasted_iota(jnp.int32, (height, LANES), 1)
    for d in range(devices):
        t, shift = divmod(d * width, LANES)
        chunk = jnp.zeros((height, LANES), F32)
        for p in range(packs):
            rows = slice(p * height, (p + 1) * height)
            at = p * step
            value = pltpu.roll(coeff_ref[t, rows, :LANES], (at - shift) % LANES, 1)
            if shift + width > LANES:
                after = pltpu.roll(coeff_ref[t + 1, rows, :LANES], (at - shift) % LANES, 1)
                value = jnp.where(lane < at + LANES - shift, value, after)
            chunk = value if p == 0 else jnp.where(lane < at, chunk, value)
        out_ref[d] = chunk.astype(BF16)


def legendre_kernel(wave_ref, arrived_ref, legendre_ref, out_ref, *, lat, lev, packs):
    outputs, slots, top_wave = out_ref.shape
    circles = legendre_ref.shape[0] // slots
    own = circles // lat
    per_tile = LANES // circles
    device = lax.axis_index("lat") * lev + lax.axis_index("lev")

    total = arrived_ref.shape[0]
    row = lax.broadcasted_iota(jnp.int32, (total, total), 0)
    col = lax.broadcasted_iota(jnp.int32, (total, total), 1)
    log = lambda n: n.bit_length() - 1
    inner = row & (own - 1)
    group = (row >> log(own)) & (2 * lev - 1)
    outer = row >> log(own * 2 * lev)
    target = (group << log(circles)) | (outer << log(own)) | inner
    turned = lax.dot_general(
        arrived_ref[...], one_hot(col == target), CONTRACT_ROWS, preferred_element_type=F32
    )

    sub = lax.broadcasted_iota(jnp.int32, (8, LANES), 0)
    block = lax.broadcasted_iota(jnp.int32, (8, LANES), 1) >> log(circles)
    chosen = [(block == b) & ((sub & (per_tile - 1)) == b) for b in range(per_tile)]
    halves = 8 // per_tile
    in_half = [(sub >> log(per_tile)) == h for h in range(halves)]
    step = LANES // packs
    spread, limits = [], []
    for k in range(slots // 8):
        pieces = [None] * outputs
        for l in range(packs):
            for j in range(total // LANES):
                at = l * step + 8 * k
                v = turned[at : at + 8, j * LANES : (j + 1) * LANES]
                rolled = [v] + [pltpu.roll(v, circles * d, 1) for d in range(1, per_tile)]
                for i in range(per_tile):
                    a = jnp.zeros((8, LANES), F32)
                    for b in range(per_tile):
                        a = jnp.where(chosen[b], rolled[(b - i) % per_tile], a)
                    group_lev, part = divmod(j * per_tile + i, 2)
                    pieces[(group_lev * packs + l) * 2 + part] = jnp.concatenate(
                        [jnp.where(in_half[h], a, 0.0) for h in range(halves)], axis=1
                    )
        spread.append(jnp.concatenate(pieces, axis=0).astype(BF16))
        limit = jnp.zeros((8, LANES), jnp.int32)
        for s in range(8):
            limit = jnp.where(sub == s, wave_ref[device * slots + 8 * k + s], limit)
        limits.append(limit)

    wide = 2 * LANES
    lane = lax.broadcasted_iota(jnp.int32, (8, wide), 1)
    for n in range(0, top_wave, wide):
        sums = [
            jnp.dot(
                spread[k],
                legendre_ref[8 * k * circles : 8 * (k + 1) * circles, n : n + wide],
                preferred_element_type=F32,
            )
            for k in range(slots // 8)
        ]
        keep = [lane + n >= jnp.concatenate([m, m], axis=1) for m in limits]
        for o in range(outputs):
            out_ref[o, :, n : n + wide] = jnp.concatenate(
                [jnp.where(keep[k], sums[k][8 * o : 8 * o + 8], 0.0) for k in range(slots // 8)],
                axis=0,
            ).astype(BF16)


def other_neighbours(size):
    pairs = [(i, i + 1) for i in range(1, size - 1, 2)]
    return pairs + [(j, i) for i, j in pairs]


def body(
    grid_field, send_blocks, donor_index, tile_choice, kernel_tiles, circle_len, slot_wave, legendre
):
    levels, blocks, _ = grid_field.shape
    send_count = send_blocks.shape[2]
    slots, circles, top_wave = legendre.shape
    lat, lev = lax.axis_size("lat"), lax.axis_size("lev")
    devices = lat * lev
    coarse = PTS // LANES
    own = blocks // coarse
    tiles = slot_wave.shape[0] // LANES
    waves = slot_wave.reshape(tiles, LANES)

    halo = jax.ShapeDtypeStruct((send_count, levels * LANES), BF16)
    to_first, to_second = pl.pallas_call(
        outgoing_kernel, out_shape=(halo, halo), in_specs=[VMEM] * 2, out_specs=(VMEM, VMEM),
        compiler_params=params(4), name="outgoing",
    )(send_blocks, grid_field)
    first = lax.ppermute(to_first, "lat", [(i, i ^ 1) for i in range(lat)])
    second = lax.ppermute(to_second, "lat", other_neighbours(lat))

    entries = own * tiles * (LANES + coarse) * 2 * LANES
    fine, wide = pl.pallas_call(
        table_kernel,
        out_shape=(
            jax.ShapeDtypeStruct((own, tiles, LANES, 2 * LANES), BF16),
            jax.ShapeDtypeStruct((own, tiles, coarse, 2 * LANES), F32),
        ),
        in_specs=[SMEM, VMEM], out_specs=(VMEM, VMEM), compiler_params=params(26), name="tables",
        cost_estimate=pl.CostEstimate(flops=8 * entries, bytes_accessed=3 * entries, transcendentals=0),
    )(circle_len, waves)

    rows = levels * 2 * own
    packs = 1
    while rows % (16 * packs) == 0 and 2 * packs * slots <= LANES:
        packs *= 2
    coeffs = pl.pallas_call(
        functools.partial(transform_kernel, top_wave=top_wave),
        out_shape=jax.ShapeDtypeStruct((devices, rows // packs, LANES), BF16),
        in_specs=[SMEM] + [VMEM] * 9, out_specs=VMEM,
        scratch_shapes=[
            pltpu.VMEM((own, levels * coarse, LANES), F32),
            pltpu.VMEM((tiles, rows, LANES), F32),
        ],
        compiler_params=params(40), name="transform",
    )(
        circle_len, donor_index.T, tile_choice.T, grid_field, first, second, kernel_tiles, waves,
        fine, wide,
    )
    arrived = lax.all_to_all(coeffs, ("lat", "lev"), 0, 0, tiled=True)

    outputs = lev * levels * 2
    height = rows // packs
    if packs == levels and height == 2 * own == 8 and LANES == 4 * circles and slots % 8 == 0:
        spectra = pl.pallas_call(
            functools.partial(legendre_kernel, lat=lat, lev=lev, packs=packs),
            out_shape=jax.ShapeDtypeStruct((outputs, slots, top_wave), BF16),
            in_specs=[SMEM, VMEM, VMEM], out_specs=VMEM, compiler_params=params(32), name="legendre",
        )(
            slot_wave,
            arrived.reshape(devices * height, LANES),
            legendre.reshape(slots * circles, top_wave),
        )
        return spectra.reshape(outputs // 2, 2, slots, top_wave)

    gathered = arrived.reshape(lat, lev, height, packs, LANES // packs)[..., :slots]
    gathered = gathered.swapaxes(2, 3).reshape(lat, lev, levels, 2, own, slots)
    gathered = gathered.transpose(1, 2, 3, 0, 4, 5).reshape(outputs // 2, 2, circles, slots)
    spectra = jnp.einsum("lcgs,sgn->lcsn", gathered, legendre, preferred_element_type=F32)
    first_slot = (lax.axis_index("lat") * lev + lax.axis_index("lev")) * slots
    mine = lax.dynamic_slice_in_dim(slot_wave, first_slot, slots)
    allowed = jnp.arange(top_wave, dtype=jnp.int32)[None, :] >= mine[:, None]
    return jnp.where(allowed[None, None], spectra, 0.0).astype(BF16)


def solution(mesh):
    return jax.shard_map(
        body,
        mesh=mesh,
        in_specs=(
            P("lev", "lat", None),
            P("lat", None, None),
            P("lat", None),
            P("lat", None),
            P(),
            P(),
            P(),
            P(("lat", "lev"), None, None),
        ),
        out_specs=P(None, None, ("lat", "lev"), None),
        check_vma=False,
    )
```

time: 155 us -> 33.4 us (0.22)
  other arithmetic: 74 us -> 0 us
  local copies, waits for them, and re-layouts: 38.7 us -> 6.81 us
  starting transfers between devices: 19.7 us -> 3.6 us
  blocking collectives: 0 us -> 14.8 us
  waiting for transfers between devices: 11.4 us -> 0.01 us
  Pallas kernels: 0 us -> 7.64 us
  matrix products: 6.93 us -> 0 us
  between operations: 2.16 us -> 0.07 us
    another operation x11 -> x0, other arithmetic: 27 us -> none
    all_to_all x0 -> x1, blocking collectives: none -> 14.8 us  [body(): arrived = lax.all_to_all(coeffs, ('lat', 'lev'), 0, 0, tiled=True)]
    and x12 -> x0, other arithmetic: 14 us -> none  [the longest x10 13.3 us: circle_table(): (jnp.arange(points, dtype=jnp.int32) < length)[:, None] & live_slot[None, :]]
    all_to_all x3 -> x0, starting transfers between devices: 13.5 us -> none  [the longest x1 6.96 us: body(): lax.all_to_all(coeffs, 'lat', split_axis=5, concat_axis=2, tiled=True)]
    cos x20 -> x0, other arithmetic: 13.3 us -> none  [the longest x10 9.2 us: circle_table(): cos_lo = jnp.cos(lower_angle)[None]]
    all_to_all x3 -> x0, waiting for transfers between devices: 11.4 us -> none  [the longest x1 5.97 us: body(): lax.all_to_all(coeffs, 'lat', split_axis=5, concat_axis=2, tiled=True)]
    sub x10 -> x0, other arithmetic: 8.11 us -> none  [circle_table(): cosine = (cos_hi * cos_lo - sin_hi * sin_lo).reshape(points, -1)]
    pallas_call x0 -> x4, Pallas kernels: none -> 7.64 us  [the longest x1 2.61 us: body(): pl.pallas_call(functools.partial(legendre_kernel, lat=lat, lev=lev, packs...]
  transfers between devices with their start and end apart: 5 -> 2, of which waited for: 3 -> 0; matrix products, arithmetic and copies ran while one was open for 5% -> 0% of each run, Pallas kernels for 0% -> 8%
where the time goes in v1:
time: 33.4 us; the launch traced here: 33 us
  blocking collectives  14.8 us (44%)
  Pallas kernels  7.64 us (23%)
  local copies, waits for them, and re-layouts  6.81 us (20%)
  starting transfers between devices  3.6 us (11%)
    all_to_all x1, blocking collectives, body(): arrived = lax.all_to_all(coeffs, ('lat', 'lev'), 0, 0, tiled=True)  14.8 us
    unnamed x20, local copies, waits for them, and re-layouts  6.81 us
    ppermute x1, starting transfers between devices, body(): first = lax.ppermute(to_first, 'lat', [(i, i ^ 1) for i in range(lat)])  2.95 us
    pallas_call x1, Pallas kernels, body(): pl.pallas_call(functools.partial(legendre_kernel, lat=lat, lev=lev, packs...  2.61 us
    pallas_call x1, Pallas kernels, body(): pl.pallas_call(table_kernel, out_shape=(jax.ShapeDtypeStruct((own, tiles,...  2.49 us
    pallas_call x1, Pallas kernels, body(): pl.pallas_call(functools.partial(transform_kernel, top_wave=top_wave), ou...  2.36 us
  transfers between devices with their start and end apart: 2, of which 0 were waited for; matrix products, arithmetic and copies ran while one was open for 0% of the time, Pallas kernels for 8%

profile of v1, /device:TPU:0, one launch (start us, length us, event | category | flops | bytes accessed | tf_op | source)
XLA Modules:
  0.0 33.0 jit_solution(6206149866144515176)
XLA Ops:
  0.0 0.9 %copy-done.1 = bf16[2,160,128]{2,1,0:T(8,128)(2,1)S(1)} copy-done((bf16[2,160,128]{2,1,0:T(8,128)(2,1)S(1)}, bf16[2,160,128]{2,1,0:T(8,128)(2,1)}, u32[]{:S(2)}) %copy-start.1) | copy-done | bytes 81944
  0.9 0.0 copy-start.8
  0.9 0.7 %copy-done.8 = s32[1,2,32]{2,1,0:T(2,128)S(1)} copy-done((s32[1,2,32]{2,1,0:T(2,128)S(1)}, s32[1,2,32]{2,1,0:T(2,128)}, u32[]{:S(2)}) %copy-start.8) | copy-done | bytes 280
  1.6 0.0 copy-start
  1.6 0.2 outgoing.1
  1.8 3.0 %collective-permute-start = (bf16[32,256]{1,0:T(8,128)(2,1)S(1)}, bf16[32,256]{1,0:T(8,128)(2,1)S(1)}, u32[]{:S(2)}, u32[]{:S(2)}) collective-permute-start(bf16[32,256]{1,0:T(8,128)(2,1)S(1)} %get-tuple-element.9), channel_id=1, source_target_pairs={{0,4},{4,0},{8,12},{12,8},{16,20},{20,16},{24,28},{28,24},{1,5},{5... | collective-permute-start | bytes 49160 | tf_op jit(solution)/shard_map/ppermute | solution.py:280
  4.7 0.7 %collective-permute-start.1 = (bf16[32,256]{1,0:T(8,128)(2,1)S(1)}, bf16[32,256]{1,0:T(8,128)(2,1)S(1)}, u32[]{:S(2)}, u32[]{:S(2)}) collective-permute-start(bf16[32,256]{1,0:T(8,128)(2,1)S(1)} %get-tuple-element.10), channel_id=1, source_target_pairs={{4,8},{12,16},{20,24},{8,4},{16,12},{24,20},{5,9},{13,17},{21,25},... | collective-permute-start | bytes 49160 | tf_op jit(solution)/shard_map/ppermute | solution.py:281
  5.4 0.0 copy-start.4
  5.4 0.7 %copy-done.4 = s32[1280]{0:T(1024)S(1)} copy-done((s32[1280]{0:T(1024)S(1)}, s32[1280]{0:T(1024)}, u32[]{:S(2)}) %copy-start.4) | copy-done | bytes 5144
  6.1 0.0 copy-start.9
  6.1 0.7 %copy-done.9 = s32[32]{0:T(128)S(1)} copy-done((s32[32]{0:T(128)S(1)}, s32[32]{0:T(128)}, u32[]{:S(2)}) %copy-start.9) | copy-done | bytes 152
  6.7 2.5 %tables.1 = (bf16[4,10,128,256]{3,2,1,0:T(8,128)(2,1)S(1)}, f32[4,10,40,256]{3,2,1,0:T(8,128)S(1)}) custom-call(s32[32]{0:T(128)S(1)} %copy-done.9, s32[10,128]{1,0:T(8,128)S(1)} %bitcast.8), custom_call_target="tpu_custom_call" | custom-call | flops 13762560 | bytes 5160960 | tf_op jit(solution)/shard_map/tables/pallas_call | solution.py:284
  9.2 0.0 collective-permute-done.first_ref
  9.2 0.0 collective-permute-done.1.second_ref
  9.2 0.0 copy-start.2
  9.2 0.9 %copy-done.2 = bf16[2,160,128]{2,1,0:T(8,128)(2,1)S(1)} copy-done((bf16[2,160,128]{2,1,0:T(8,128)(2,1)S(1)}, bf16[2,160,128]{2,1,0:T(8,128)(2,1)}, u32[]{:S(2)}) %copy-start.2) | copy-done | bytes 81944
  10.1 0.9 %copy-done.3 = bf16[8,128,128]{2,1,0:T(8,128)(2,1)S(1)} copy-done((bf16[8,128,128]{2,1,0:T(8,128)(2,1)S(1)}, bf16[8,128,128]{2,1,0:T(8,128)(2,1)}, u32[]{:S(2)}) %copy-start.3) | copy-done | bytes 262168
  11.1 0.7 %copy-done.5 = s32[1280]{0:T(1024)S(1)} copy-done((s32[1280]{0:T(1024)S(1)}, s32[1280]{0:T(1024)}, u32[]{:S(2)}) %copy-start.5) | copy-done | bytes 5144
  11.8 0.7 %copy-done.6 = s32[160,2]{0,1:T(2,128)S(1)} copy-done((s32[160,2]{0,1:T(2,128)S(1)}, s32[160,2]{0,1:T(2,128)}, u32[]{:S(2)}) %copy-start.6) | copy-done | bytes 1304
  12.5 0.7 %copy-done.7 = s32[160,2]{0,1:T(2,128)S(1)} copy-done((s32[160,2]{0,1:T(2,128)S(1)}, s32[160,2]{0,1:T(2,128)}, u32[]{:S(2)}) %copy-start.7) | copy-done | bytes 1304
  13.1 2.4 %transform.1 = bf16[32,8,128]{2,1,0:T(8,128)(2,1)S(1)} custom-call(s32[32]{0:T(128)S(1)} %copy-done.9, s32[2,160]{1,0:T(2,128)S(1)} %bitcast.10, s32[2,160]{1,0:T(2,128)S(1)} %bitcast.11, bf16[2,160,128]{2,1,0:T(8,128)(2,1)S(1)} %copy-done.2, bf16[32,256]{1,0:T(8,128)(2,1)S(1)} %collective-permute-done.first_ref, ...), custom_call_target="tpu_custom_call" | custom-call | tf_op jit(solution)/shard_map/transform/pallas_call | solution.py:298
  15.5 14.8 %all_to_all.5 = bf16[32,8,128]{2,1,0:T(8,128)(2,1)S(1)} all-to-all(bf16[32,8,128]{2,1,0:T(8,128)(2,1)S(1)} %transform.1), channel_id=1, replica_groups=mesh['lat'=8,'lev'=4] {'lat','lev'}, dimensions={0} | all-to-all | bytes 131072 | tf_op jit(solution)/shard_map/all_to_all | solution.py:311
  30.3 0.0 copy-done
  30.4 2.6 %legendre.1 = bf16[16,40,1280]{2,1,0:T(8,128)(2,1)} custom-call(s32[1280]{0:T(1024)S(1)} %copy-done.5, bf16[256,128]{1,0:T(8,128)(2,1)S(1)} %bitcast.7, bf16[1280,1280]{1,0:T(8,128)(2,1)S(1)} %bitcast.6), custom_call_target="tpu_custom_call" | custom-call | tf_op jit(solution)/shard_map/legendre/pallas_call | solution.py:316
  (5 shorter events, 0.0 us)
Async XLA Ops:
  0.0 0.9 %copy-start.1 = (bf16[2,160,128]{2,1,0:T(8,128)(2,1)S(1)}, bf16[2,160,128]{2,1,0:T(8,128)(2,1)}, u32[]{:S(2)}) copy-start(bf16[2,160,128]{2,1,0:T(8,128)(2,1)} %field_ref.3) | copy-start | bytes 245764
  0.9 0.7 %copy-start.8 = (s32[1,2,32]{2,1,0:T(2,128)S(1)}, s32[1,2,32]{2,1,0:T(2,128)}, u32[]{:S(2)}) copy-start(s32[1,2,32]{2,1,0:T(2,128)} %send_ref.1) | copy-start | bytes 772
  1.6 28.8 %copy-start = (bf16[40,32,1280]{2,1,0:T(8,128)(2,1)S(1)}, bf16[40,32,1280]{2,1,0:T(8,128)(2,1)}, u32[]{:S(2)}) copy-start(bf16[40,32,1280]{2,1,0:T(8,128)(2,1)} %param.15) | copy-start | bytes 9830404
  1.8 7.5 %collective-permute-start = (bf16[32,256]{1,0:T(8,128)(2,1)S(1)}, bf16[32,256]{1,0:T(8,128)(2,1)S(1)}, u32[]{:S(2)}, u32[]{:S(2)}) collective-permute-start(bf16[32,256]{1,0:T(8,128)(2,1)S(1)} %get-tuple-element.9), channel_id=1, source_target_pairs={{0,4},{4,0},{8,12},{12,8},{16,20},{20,16},{24,28},{28,24},{1,5},{5... | collective-permute-start | bytes 49160 | tf_op jit(solution)/shard_map/ppermute | solution.py:280
  4.7 4.5 %collective-permute-start.1 = (bf16[32,256]{1,0:T(8,128)(2,1)S(1)}, bf16[32,256]{1,0:T(8,128)(2,1)S(1)}, u32[]{:S(2)}, u32[]{:S(2)}) collective-permute-start(bf16[32,256]{1,0:T(8,128)(2,1)S(1)} %get-tuple-element.10), channel_id=1, source_target_pairs={{4,8},{12,16},{20,24},{8,4},{16,12},{24,20},{5,9},{13,17},{21,25},... | collective-permute-start | bytes 49160 | tf_op jit(solution)/shard_map/ppermute | solution.py:281
  5.4 0.7 %copy-start.4 = (s32[1280]{0:T(1024)S(1)}, s32[1280]{0:T(1024)}, u32[]{:S(2)}) copy-start(s32[1280]{0:T(1024)} %wave_ref.1) | copy-start | bytes 15364
  6.1 0.7 %copy-start.9 = (s32[32]{0:T(128)S(1)}, s32[32]{0:T(128)}, u32[]{:S(2)}) copy-start(s32[32]{0:T(128)} %length_ref.3) | copy-start | bytes 388
  9.2 0.9 %copy-start.2 = (bf16[2,160,128]{2,1,0:T(8,128)(2,1)S(1)}, bf16[2,160,128]{2,1,0:T(8,128)(2,1)}, u32[]{:S(2)}) copy-start(bf16[2,160,128]{2,1,0:T(8,128)(2,1)} %field_ref.3) | copy-start | bytes 245764
  10.1 0.9 %copy-start.3 = (bf16[8,128,128]{2,1,0:T(8,128)(2,1)S(1)}, bf16[8,128,128]{2,1,0:T(8,128)(2,1)}, u32[]{:S(2)}) copy-start(bf16[8,128,128]{2,1,0:T(8,128)(2,1)} %kernels_ref.1) | copy-start | bytes 786436
  11.1 0.7 %copy-start.5 = (s32[1280]{0:T(1024)S(1)}, s32[1280]{0:T(1024)}, u32[]{:S(2)}) copy-start(s32[1280]{0:T(1024)} %wave_ref.1) | copy-start | bytes 15364
  11.8 0.7 %copy-start.6 = (s32[160,2]{0,1:T(2,128)S(1)}, s32[160,2]{0,1:T(2,128)}, u32[]{:S(2)}) copy-start(s32[160,2]{0,1:T(2,128)} %param.10) | copy-start | bytes 3844
  12.5 0.7 %copy-start.7 = (s32[160,2]{0,1:T(2,128)S(1)}, s32[160,2]{0,1:T(2,128)}, u32[]{:S(2)}) copy-start(s32[160,2]{0,1:T(2,128)} %param.11) | copy-start | bytes 3844

commit v2 on v1

--- a/solution.py
+++ b/solution.py
@@ -13,7 +13,7 @@
 BF16 = jnp.bfloat16
 F32 = jnp.float32
 VMEM = pl.BlockSpec(memory_space=pltpu.VMEM)
-SMEM = pl.BlockSpec(memory_space=pltpu.SMEM)
+HBM = pl.BlockSpec(memory_space=pltpu.HBM)
 CONTRACT_ROWS = (((0,), (0,)), ((), ()))
 
 
@@ -29,8 +29,31 @@
     return jnp.concatenate([field_ref[l] for l in range(field_ref.shape[0])], axis=1)
 
 
-def outgoing_kernel(send_ref, field_ref, first_ref, second_ref):
-    even = lax.rem(lax.axis_index("lat"), 2) == 0
+def outgoing_kernel(
+    send_hbm, field_hbm, length_hbm, donor_hbm, tile_hbm, kernels_hbm, wave_hbm,
+    first_ref, second_ref, field_ref, lengths_ref, donor_ref, tile_ref, kernels_ref, wave_ref,
+    send_ref, length_ref, sems,
+):
+    copies = [
+        pltpu.make_async_copy(source, target, sems.at[i])
+        for i, (source, target) in enumerate(
+            (
+                (send_hbm, send_ref),
+                (field_hbm, field_ref),
+                (length_hbm, length_ref),
+                (donor_hbm, donor_ref),
+                (tile_hbm, tile_ref),
+                (kernels_hbm, kernels_ref),
+                (wave_hbm, wave_ref),
+            )
+        )
+    ]
+    for copy in copies:
+        copy.start()
+    copies[0].wait()
+    copies[1].wait()
+    band = lax.axis_index("lat")
+    even = lax.rem(band, 2) == 0
     own = side_by_side(field_ref)
     blocks, count = own.shape[0], send_ref.shape[2]
     rows = lax.broadcasted_iota(jnp.int32, (blocks, count), 0)
@@ -43,6 +66,12 @@
             one_hot(rows == listed), own, CONTRACT_ROWS, preferred_element_type=F32
         )
         ref[...] = picked.astype(BF16)
+    copies[2].wait()
+    circles = lengths_ref.shape[0]
+    for g in range(circles):
+        lengths_ref[g] = jnp.full((8, LANES), length_ref[band * circles + g], jnp.int32)
+    for copy in copies[3:]:
+        copy.wait()
 
 
 def turn(steps, waves, length, inverse):
@@ -64,10 +93,11 @@
     return a[0] * b[0] - a[1] * b[1], a[0] * b[1] + a[1] * b[0]
 
 
-def table_kernel(length_ref, wave_ref, fine_ref, coarse_ref):
+def table_kernel(lengths_ref, wave_ref, slot_hbm, fine_ref, coarse_ref, limits_ref, slot_ref, sem, *, lev):
     circles, tiles = fine_ref.shape[:2]
     coarse = coarse_ref.shape[2]
-    band = lax.axis_index("lat")
+    fetch = pltpu.make_async_copy(slot_hbm, slot_ref, sem)
+    fetch.start()
     step = lax.broadcasted_iota(jnp.int32, (8, LANES), 0).astype(F32)
 
     def doubled(base, factor_of, groups):
@@ -78,7 +108,7 @@
 
     def one(index, _):
         g, t = index // tiles, lax.rem(index, tiles)
-        length = jnp.full((8, LANES), length_ref[band * circles + g], jnp.int32).astype(F32)
+        length = lengths_ref[g].astype(F32)
         inverse = 1.0 / length
         waves = jnp.broadcast_to(wave_ref[pl.ds(t, 1), :], (8, LANES)).astype(F32)
         hop_steps = jnp.left_shift(8, lax.broadcasted_iota(jnp.int32, (8, LANES), 0)).astype(F32)
@@ -104,17 +134,22 @@
 
     lax.fori_loop(0, circles * tiles, one, 0, unroll=2)
 
+    fetch.wait()
+    slots = limits_ref.shape[0]
+    first = (lax.axis_index("lat") * lev + lax.axis_index("lev")) * slots
+    for s in range(slots):
+        limits_ref[s : s + 1] = jnp.full((1, LANES), slot_ref[first + s], jnp.int32)
+
 
 def transform_kernel(
-    length_ref, donor_ref, tile_ref, field_ref, first_ref, second_ref, kernels_ref, wave_ref,
+    lengths_ref, donor_ref, tile_ref, field_ref, first_ref, second_ref, kernels_ref, wave_ref,
     fine_ref, coarse_ref, out_ref, points_ref, coeff_ref, *, top_wave,
 ):
     levels, blocks = field_ref.shape[:2]
     circles, tiles = fine_ref.shape[:2]
     coarse = coarse_ref.shape[2]
     kinds = kernels_ref.shape[0]
-    band = lax.axis_index("lat")
-    even = lax.rem(band, 2) == 0
+    even = lax.rem(lax.axis_index("lat"), 2) == 0
 
     first, second = first_ref[...], second_ref[...]
     below, above = jnp.where(even, second, first), jnp.where(even, first, second)
@@ -144,13 +179,13 @@
     position = lax.broadcasted_iota(jnp.int32, (coarse, LANES), 0) * LANES
     position = position + lax.broadcasted_iota(jnp.int32, (coarse, LANES), 1)
     for g in range(circles):
-        inside = position < length_ref[band * circles + g]
+        inside = position < jnp.broadcast_to(lengths_ref[g, 0:1], (coarse, LANES))
         for l in range(levels):
             part = arrival[l][g * coarse : (g + 1) * coarse]
             points_ref[g, l * coarse : (l + 1) * coarse] = jnp.where(inside, part * part, 0.0)
 
     def circle(g, _):
-        length = length_ref[band * circles + g]
+        length = lengths_ref[g, 0:1]
         points = points_ref[g].astype(BF16)
         for t in range(tiles):
             near = jnp.dot(points, fine_ref[g, t], preferred_element_type=F32)
@@ -188,12 +223,11 @@
         out_ref[d] = chunk.astype(BF16)
 
 
-def legendre_kernel(wave_ref, arrived_ref, legendre_ref, out_ref, *, lat, lev, packs):
+def legendre_kernel(limits_ref, arrived_ref, legendre_ref, out_hbm, out_ref, sems, *, lat, lev, packs):
     outputs, slots, top_wave = out_ref.shape
     circles = legendre_ref.shape[0] // slots
     own = circles // lat
     per_tile = LANES // circles
-    device = lax.axis_index("lat") * lev + lax.axis_index("lev")
 
     total = arrived_ref.shape[0]
     row = lax.broadcasted_iota(jnp.int32, (total, total), 0)
@@ -213,7 +247,7 @@
     halves = 8 // per_tile
     in_half = [(sub >> log(per_tile)) == h for h in range(halves)]
     step = LANES // packs
-    spread, limits = [], []
+    spread = []
     for k in range(slots // 8):
         pieces = [None] * outputs
         for l in range(packs):
@@ -230,13 +264,12 @@
                         [jnp.where(in_half[h], a, 0.0) for h in range(halves)], axis=1
                     )
         spread.append(jnp.concatenate(pieces, axis=0).astype(BF16))
-        limit = jnp.zeros((8, LANES), jnp.int32)
-        for s in range(8):
-            limit = jnp.where(sub == s, wave_ref[device * slots + 8 * k + s], limit)
-        limits.append(limit)
 
     wide = 2 * LANES
     lane = lax.broadcasted_iota(jnp.int32, (8, wide), 1)
+    limits = [limits_ref[8 * k : 8 * k + 8] for k in range(slots // 8)]
+    limits = [jnp.concatenate([m, m], axis=1) for m in limits]
+    copies = []
     for n in range(0, top_wave, wide):
         sums = [
             jnp.dot(
@@ -246,12 +279,21 @@
             )
             for k in range(slots // 8)
         ]
-        keep = [lane + n >= jnp.concatenate([m, m], axis=1) for m in limits]
+        keep = [lane + n >= m for m in limits]
         for o in range(outputs):
             out_ref[o, :, n : n + wide] = jnp.concatenate(
                 [jnp.where(keep[k], sums[k][8 * o : 8 * o + 8], 0.0) for k in range(slots // 8)],
                 axis=0,
             ).astype(BF16)
+        columns = (slice(None), slice(None), pl.ds(n, wide))
+        copies.append(
+            pltpu.make_async_copy(
+                out_ref.at[columns], out_hbm.at[columns], sems.at[n // wide]
+            )
+        )
+        copies[-1].start()
+    for copy in copies:
+        copy.wait()
 
 
 def other_neighbours(size):
@@ -272,24 +314,40 @@
     tiles = slot_wave.shape[0] // LANES
     waves = slot_wave.reshape(tiles, LANES)
 
+    def like(x):
+        return jax.ShapeDtypeStruct(x.shape, x.dtype)
+
+    donors, kinds = donor_index.T, tile_choice.T
     halo = jax.ShapeDtypeStruct((send_count, levels * LANES), BF16)
-    to_first, to_second = pl.pallas_call(
-        outgoing_kernel, out_shape=(halo, halo), in_specs=[VMEM] * 2, out_specs=(VMEM, VMEM),
+    lengths = jax.ShapeDtypeStruct((own, 8, LANES), jnp.int32)
+    small = (send_blocks, grid_field, circle_len, donors, kinds, kernel_tiles, waves)
+    to_first, to_second, field, lengths, donors, kinds, kernels, waves = pl.pallas_call(
+        outgoing_kernel,
+        out_shape=(halo, halo, like(grid_field), lengths, *map(like, small[3:])),
+        in_specs=[HBM] * 7, out_specs=(VMEM,) * 8,
+        scratch_shapes=[
+            pltpu.VMEM(send_blocks.shape, jnp.int32),
+            pltpu.SMEM(circle_len.shape, jnp.int32),
+            pltpu.SemaphoreType.DMA((7,)),
+        ],
         compiler_params=params(4), name="outgoing",
-    )(send_blocks, grid_field)
+    )(*small)
     first = lax.ppermute(to_first, "lat", [(i, i ^ 1) for i in range(lat)])
     second = lax.ppermute(to_second, "lat", other_neighbours(lat))
 
     entries = own * tiles * (LANES + coarse) * 2 * LANES
-    fine, wide = pl.pallas_call(
-        table_kernel,
+    fine, wide, limits = pl.pallas_call(
+        functools.partial(table_kernel, lev=lev),
         out_shape=(
             jax.ShapeDtypeStruct((own, tiles, LANES, 2 * LANES), BF16),
             jax.ShapeDtypeStruct((own, tiles, coarse, 2 * LANES), F32),
+            jax.ShapeDtypeStruct((slots, LANES), jnp.int32),
         ),
-        in_specs=[SMEM, VMEM], out_specs=(VMEM, VMEM), compiler_params=params(26), name="tables",
+        in_specs=[VMEM, VMEM, HBM], out_specs=(VMEM,) * 3,
+        scratch_shapes=[pltpu.SMEM(slot_wave.shape, jnp.int32), pltpu.SemaphoreType.DMA],
+        compiler_params=params(26), name="tables",
         cost_estimate=pl.CostEstimate(flops=8 * entries, bytes_accessed=3 * entries, transcendentals=0),
-    )(circle_len, waves)
+    )(lengths, waves, slot_wave)
 
     rows = levels * 2 * own
     packs = 1
@@ -298,15 +356,14 @@
     coeffs = pl.pallas_call(
         functools.partial(transform_kernel, top_wave=top_wave),
         out_shape=jax.ShapeDtypeStruct((devices, rows // packs, LANES), BF16),
-        in_specs=[SMEM] + [VMEM] * 9, out_specs=VMEM,
+        in_specs=[VMEM] * 10, out_specs=VMEM,
         scratch_shapes=[
             pltpu.VMEM((own, levels * coarse, LANES), F32),
             pltpu.VMEM((tiles, rows, LANES), F32),
         ],
         compiler_params=params(40), name="transform",
     )(
-        circle_len, donor_index.T, tile_choice.T, grid_field, first, second, kernel_tiles, waves,
-        fine, wide,
+        lengths, donors, kinds, field, first, second, kernels, waves, fine, wide
     )
     arrived = lax.all_to_all(coeffs, ("lat", "lev"), 0, 0, tiled=True)
 
@@ -316,9 +373,14 @@
         spectra = pl.pallas_call(
             functools.partial(legendre_kernel, lat=lat, lev=lev, packs=packs),
             out_shape=jax.ShapeDtypeStruct((outputs, slots, top_wave), BF16),
-            in_specs=[SMEM, VMEM, VMEM], out_specs=VMEM, compiler_params=params(32), name="legendre",
+            in_specs=[VMEM] * 3, out_specs=HBM,
+            scratch_shapes=[
+                pltpu.VMEM((outputs, slots, top_wave), BF16),
+                pltpu.SemaphoreType.DMA((top_wave // (2 * LANES),)),
+            ],
+            compiler_params=params(32), name="legendre",
         )(
-            slot_wave,
+            limits,
             arrived.reshape(devices * height, LANES),
             legendre.reshape(slots * circles, top_wave),
         )

time: 33.4 us -> 31.5 us (0.943)
  Pallas kernels: 7.64 us -> 6.14 us
  local copies, waits for them, and re-layouts: 6.81 us -> 5.92 us
  blocking collectives: 14.8 us -> 15.3 us
    pallas_call x1, Pallas kernels: 2.61 us -> 1.69 us  [body(): pl.pallas_call(functools.partial(legendre_kernel, lat=lat, lev=lev, packs...]
    unnamed x20 -> x18, local copies, waits for them, and re-layouts: 6.81 us -> 5.92 us
    pallas_call x1, Pallas kernels: 2.36 us -> 1.79 us  [body(): pl.pallas_call(functools.partial(transform_kernel, top_wave=top_wave), ou...]
    all_to_all x1, blocking collectives: 14.8 us -> 15.3 us  [body(): arrived = lax.all_to_all(coeffs, ('lat', 'lev'), 0, 0, tiled=True)]
  transfers between devices with their start and end apart: 2 -> 2, of which waited for: 0 -> 0; matrix products, arithmetic and copies ran while one was open for 0% -> 0% of each run, Pallas kernels for 8% -> 6%
where the time goes in v2:
time: 31.5 us; the launch traced here: 31.1 us
  blocking collectives  15.3 us (49%)
  Pallas kernels  6.14 us (19%)
  local copies, waits for them, and re-layouts  5.92 us (19%)
  starting transfers between devices  3.65 us (12%)
    all_to_all x1, blocking collectives, body(): arrived = lax.all_to_all(coeffs, ('lat', 'lev'), 0, 0, tiled=True)  15.3 us
    unnamed x18, local copies, waits for them, and re-layouts  5.92 us
    ppermute x1, starting transfers between devices, body(): first = lax.ppermute(to_first, 'lat', [(i, i ^ 1) for i in range(lat)])  3 us
    pallas_call x1, Pallas kernels, body(): pl.pallas_call(functools.partial(table_kernel, lev=lev), out_shape=(jax.S...  1.97 us
    pallas_call x1, Pallas kernels, body(): pl.pallas_call(functools.partial(transform_kernel, top_wave=top_wave), ou...  1.79 us
    pallas_call x1, Pallas kernels, body(): pl.pallas_call(functools.partial(legendre_kernel, lat=lat, lev=lev, packs...  1.69 us
    pallas_call x1, Pallas kernels, body(): pl.pallas_call(outgoing_kernel, out_shape=(halo, halo, like(grid_field),...  0.7 us
    ppermute x1, starting transfers between devices, body(): second = lax.ppermute(to_second, 'lat', other_neighbours(lat))  0.65 us
  transfers between devices with their start and end apart: 2, of which 0 were waited for; matrix products, arithmetic and copies ran while one was open for 0% of the time, Pallas kernels for 6%

profile of v2, /device:TPU:0, one launch (start us, length us, event | category | flops | bytes accessed | tf_op | source)
XLA Modules:
  0.0 31.1 jit_solution(17141602569555469460)
XLA Ops:
  0.0 0.0 copy-start.1
  0.0 0.9 %copy-done.1 = bf16[8,128,128]{2,1,0:T(8,128)(2,1)S(1)} copy-done((bf16[8,128,128]{2,1,0:T(8,128)(2,1)S(1)}, bf16[8,128,128]{2,1,0:T(8,128)(2,1)}, u32[]{:S(2)}) %copy-start.1) | copy-done | bytes 262168
  1.0 0.0 copy-start.2
  1.0 0.9 %copy-done.2 = bf16[2,160,128]{2,1,0:T(8,128)(2,1)S(1)} copy-done((bf16[2,160,128]{2,1,0:T(8,128)(2,1)S(1)}, bf16[2,160,128]{2,1,0:T(8,128)(2,1)}, u32[]{:S(2)}) %copy-start.2) | copy-done | bytes 81944
  1.8 0.0 copy-start.3
  1.8 0.7 %copy-done.3 = s32[1280]{0:T(1024)S(1)} copy-done((s32[1280]{0:T(1024)S(1)}, s32[1280]{0:T(1024)}, u32[]{:S(2)}) %copy-start.3) | copy-done | bytes 5144
  2.5 0.0 copy-start.5
  2.5 0.7 %copy-done.5 = s32[160,2]{0,1:T(2,128)S(1)} copy-done((s32[160,2]{0,1:T(2,128)S(1)}, s32[160,2]{0,1:T(2,128)}, u32[]{:S(2)}) %copy-start.5) | copy-done | bytes 1304
  3.2 0.0 copy-start.6
  3.2 0.7 %copy-done.6 = s32[160,2]{0,1:T(2,128)S(1)} copy-done((s32[160,2]{0,1:T(2,128)S(1)}, s32[160,2]{0,1:T(2,128)}, u32[]{:S(2)}) %copy-start.6) | copy-done | bytes 1304
  3.9 0.7 %copy-done.7 = s32[1,2,32]{2,1,0:T(2,128)S(1)} copy-done((s32[1,2,32]{2,1,0:T(2,128)S(1)}, s32[1,2,32]{2,1,0:T(2,128)}, u32[]{:S(2)}) %copy-start.7) | copy-done | bytes 280
  4.6 0.7 %copy-done.8 = s32[32]{0:T(128)S(1)} copy-done((s32[32]{0:T(128)S(1)}, s32[32]{0:T(128)}, u32[]{:S(2)}) %copy-start.8) | copy-done | bytes 152
  5.2 0.7 %outgoing.1 = (bf16[32,256]{1,0:T(8,128)(2,1)S(1)}, bf16[32,256]{1,0:T(8,128)(2,1)S(1)}, bf16[2,160,128]{2,1,0:T(8,128)(2,1)S(1)}, s32[4,8,128]{2,1,0:T(8,128)S(...) custom-call(s32[1,2,32]{2,1,0:T(2,128)S(1)} %copy-done.7, ...), custom_call_target="tpu_custom_call" | custom-call | tf_op jit(solution)/shard_map/outgoing/pallas_call | solution.py:324
  5.9 3.0 %collective-permute-start = (bf16[32,256]{1,0:T(8,128)(2,1)S(1)}, bf16[32,256]{1,0:T(8,128)(2,1)S(1)}, u32[]{:S(2)}, u32[]{:S(2)}) collective-permute-start(bf16[32,256]{1,0:T(8,128)(2,1)S(1)} %get-tuple-element.22), channel_id=1, source_target_pairs={{0,4},{4,0},{8,12},{12,8},{16,20},{20,16},{24,28},{28,24},{1,5},{5... | collective-permute-start | bytes 49160 | tf_op jit(solution)/shard_map/ppermute | solution.py:335
  9.0 0.7 %collective-permute-start.1 = (bf16[32,256]{1,0:T(8,128)(2,1)S(1)}, bf16[32,256]{1,0:T(8,128)(2,1)S(1)}, u32[]{:S(2)}, u32[]{:S(2)}) collective-permute-start(bf16[32,256]{1,0:T(8,128)(2,1)S(1)} %get-tuple-element.23), channel_id=1, source_target_pairs={{4,8},{12,16},{20,24},{8,4},{16,12},{24,20},{5,9},{13,17},{21,25},... | collective-permute-start | bytes 49160 | tf_op jit(solution)/shard_map/ppermute | solution.py:336
  9.6 0.0 copy-start.4
  9.6 0.7 %copy-done.4 = s32[1280]{0:T(1024)S(1)} copy-done((s32[1280]{0:T(1024)S(1)}, s32[1280]{0:T(1024)}, u32[]{:S(2)}) %copy-start.4) | copy-done | bytes 5144
  10.3 2.0 %tables.1 = (bf16[4,10,128,256]{3,2,1,0:T(8,128)(2,1)S(1)}, f32[4,10,40,256]{3,2,1,0:T(8,128)S(1)}, s32[40,128]{1,0:T(8,128)S(1)}) custom-call(s32[4,8,128]{2,1,0:T(8,128)S(1)} %get-tuple-element.16.lengths_ref, s32[10,128]{1,0:T(8,128)S(1)} %get-tuple-element.17.wave_ref, s32[1280]{0:T(1024)S(1)} %copy-done.4), custom_call_target="tpu_custom_call" | custom-call | flops 13762560 | bytes 5160960 | tf_op jit(solution)/shard_map/tables/pallas_call | solution.py:339
  12.3 0.0 collective-permute-done.first_ref
  12.3 0.0 collective-permute-done.1.second_ref
  12.3 1.8 %transform.1 = bf16[32,8,128]{2,1,0:T(8,128)(2,1)S(1)} custom-call(s32[4,8,128]{2,1,0:T(8,128)S(1)} %get-tuple-element.16.lengths_ref, s32[2,160]{1,0:T(2,128)S(1)} %get-tuple-element.19.donor_ref, s32[2,160]{1,0:T(2,128)S(1)} %get-tuple-element.20.tile_ref, bf16[2,160,128]{2,1,0:T(8,128)(2,1)S(1)} %get-tuple-element.21.field_ref, ...), custom_call_target="tpu_custom_call" | custom-call | tf_op jit(solution)/shard_map/transform/pallas_call | solution.py:356
  14.1 15.3 %all_to_all.5 = bf16[32,8,128]{2,1,0:T(8,128)(2,1)S(1)} all-to-all(bf16[32,8,128]{2,1,0:T(8,128)(2,1)S(1)} %transform.1), channel_id=1, replica_groups=mesh['lat'=8,'lev'=4] {'lat','lev'}, dimensions={0} | all-to-all | bytes 131072 | tf_op jit(solution)/shard_map/all_to_all | solution.py:368
  29.4 0.0 copy-done
  29.4 1.7 %legendre.1 = bf16[16,40,1280]{2,1,0:T(8,128)(2,1)} custom-call(s32[40,128]{1,0:T(8,128)S(1)} %get-tuple-element.18.limits_ref, bf16[256,128]{1,0:T(8,128)(2,1)S(1)} %bitcast.7, bf16[1280,1280]{1,0:T(8,128)(2,1)S(1)} %bitcast.6), custom_call_target="tpu_custom_call" | custom-call | tf_op jit(solution)/shard_map/legendre/pallas_call | solution.py:373
  (3 shorter events, 0.0 us)
Async XLA Ops:
  0.0 0.9 %copy-start.1 = (bf16[8,128,128]{2,1,0:T(8,128)(2,1)S(1)}, bf16[8,128,128]{2,1,0:T(8,128)(2,1)}, u32[]{:S(2)}) copy-start(bf16[8,128,128]{2,1,0:T(8,128)(2,1)} %kernels_hbm.1) | copy-start | bytes 786436
  1.0 0.9 %copy-start.2 = (bf16[2,160,128]{2,1,0:T(8,128)(2,1)S(1)}, bf16[2,160,128]{2,1,0:T(8,128)(2,1)}, u32[]{:S(2)}) copy-start(bf16[2,160,128]{2,1,0:T(8,128)(2,1)} %field_hbm.1) | copy-start | bytes 245764
  1.8 0.7 %copy-start.3 = (s32[1280]{0:T(1024)S(1)}, s32[1280]{0:T(1024)}, u32[]{:S(2)}) copy-start(s32[1280]{0:T(1024)} %slot_hbm.1) | copy-start | bytes 15364
  2.5 0.7 %copy-start.5 = (s32[160,2]{0,1:T(2,128)S(1)}, s32[160,2]{0,1:T(2,128)}, u32[]{:S(2)}) copy-start(s32[160,2]{0,1:T(2,128)} %param.10) | copy-start | bytes 3844
  3.2 0.7 %copy-start.6 = (s32[160,2]{0,1:T(2,128)S(1)}, s32[160,2]{0,1:T(2,128)}, u32[]{:S(2)}) copy-start(s32[160,2]{0,1:T(2,128)} %param.11) | copy-start | bytes 3844
  3.9 0.7 %copy-start.7 = (s32[1,2,32]{2,1,0:T(2,128)S(1)}, s32[1,2,32]{2,1,0:T(2,128)}, u32[]{:S(2)}) copy-start(s32[1,2,32]{2,1,0:T(2,128)} %send_hbm.1) | copy-start | bytes 772
  4.6 0.7 %copy-start.8 = (s32[32]{0:T(128)S(1)}, s32[32]{0:T(128)}, u32[]{:S(2)}) copy-start(s32[32]{0:T(128)} %length_hbm.1) | copy-start | bytes 388
  5.2 24.2 %copy-start = (bf16[40,32,1280]{2,1,0:T(8,128)(2,1)S(1)}, bf16[40,32,1280]{2,1,0:T(8,128)(2,1)}, u32[]{:S(2)}) copy-start(bf16[40,32,1280]{2,1,0:T(8,128)(2,1)} %param.15) | copy-start | bytes 9830404
  5.9 6.3 %collective-permute-start = (bf16[32,256]{1,0:T(8,128)(2,1)S(1)}, bf16[32,256]{1,0:T(8,128)(2,1)S(1)}, u32[]{:S(2)}, u32[]{:S(2)}) collective-permute-start(bf16[32,256]{1,0:T(8,128)(2,1)S(1)} %get-tuple-element.22), channel_id=1, source_target_pairs={{0,4},{4,0},{8,12},{12,8},{16,20},{20,16},{24,28},{28,24},{1,5},{5... | collective-permute-start | bytes 49160 | tf_op jit(solution)/shard_map/ppermute | solution.py:335
  9.0 3.3 %collective-permute-start.1 = (bf16[32,256]{1,0:T(8,128)(2,1)S(1)}, bf16[32,256]{1,0:T(8,128)(2,1)S(1)}, u32[]{:S(2)}, u32[]{:S(2)}) collective-permute-start(bf16[32,256]{1,0:T(8,128)(2,1)S(1)} %get-tuple-element.23), channel_id=1, source_target_pairs={{4,8},{12,16},{20,24},{8,4},{16,12},{24,20},{5,9},{13,17},{21,25},... | collective-permute-start | bytes 49160 | tf_op jit(solution)/shard_map/ppermute | solution.py:336
  9.6 0.7 %copy-start.4 = (s32[1280]{0:T(1024)S(1)}, s32[1280]{0:T(1024)}, u32[]{:S(2)}) copy-start(s32[1280]{0:T(1024)} %slot_hbm.1) | copy-start | bytes 15364

commit v3 on v2

--- a/solution.py
+++ b/solution.py
@@ -317,6 +317,9 @@
     def like(x):
         return jax.ShapeDtypeStruct(x.shape, x.dtype)
 
+    def in_hbm(x):
+        return pltpu.with_memory_space_constraint(x, pltpu.HBM)
+
     donors, kinds = donor_index.T, tile_choice.T
     halo = jax.ShapeDtypeStruct((send_count, levels * LANES), BF16)
     lengths = jax.ShapeDtypeStruct((own, 8, LANES), jnp.int32)
@@ -331,7 +334,7 @@
             pltpu.SemaphoreType.DMA((7,)),
         ],
         compiler_params=params(4), name="outgoing",
-    )(*small)
+    )(*map(in_hbm, small))
     first = lax.ppermute(to_first, "lat", [(i, i ^ 1) for i in range(lat)])
     second = lax.ppermute(to_second, "lat", other_neighbours(lat))
 
@@ -347,7 +350,7 @@
         scratch_shapes=[pltpu.SMEM(slot_wave.shape, jnp.int32), pltpu.SemaphoreType.DMA],
         compiler_params=params(26), name="tables",
         cost_estimate=pl.CostEstimate(flops=8 * entries, bytes_accessed=3 * entries, transcendentals=0),
-    )(lengths, waves, slot_wave)
+    )(lengths, waves, in_hbm(slot_wave))
 
     rows = levels * 2 * own
     packs = 1

time: 31.5 us -> 26.7 us (0.85)
  local copies, waits for them, and re-layouts: 5.92 us -> 0.01 us
  blocking collectives: 15.3 us -> 16 us
  Pallas kernels: 6.14 us -> 6.79 us
    unnamed x18 -> x2, local copies, waits for them, and re-layouts: 5.92 us -> 0.01 us
    all_to_all x1, blocking collectives: 15.3 us -> 16 us  [body(): arrived = lax.all_to_all(coeffs, ('lat', 'lev'), 0, 0, tiled=True)]
    pallas_call x1, Pallas kernels: 0.7 us -> 1.33 us  [body(): pl.pallas_call(outgoing_kernel, out_shape=(halo, halo, like(grid_field),...]
  transfers between devices with their start and end apart: 2 -> 2, of which waited for: 0 -> 0; matrix products, arithmetic and copies ran while one was open for 0% -> 0% of each run, Pallas kernels for 6% -> 7%
where the time goes in v3:
time: 26.7 us; the launch traced here: 26.5 us
  blocking collectives  16 us (60%)
  Pallas kernels  6.79 us (25%)
  starting transfers between devices  3.65 us (14%)
    all_to_all x1, blocking collectives, body(): arrived = lax.all_to_all(coeffs, ('lat', 'lev'), 0, 0, tiled=True)  16 us
    ppermute x1, starting transfers between devices, body(): first = lax.ppermute(to_first, 'lat', [(i, i ^ 1) for i in range(lat)])  3 us
    pallas_call x1, Pallas kernels, body(): pl.pallas_call(functools.partial(table_kernel, lev=lev), out_shape=(jax.S...  1.98 us
    pallas_call x1, Pallas kernels, body(): pl.pallas_call(functools.partial(transform_kernel, top_wave=top_wave), ou...  1.8 us
    pallas_call x1, Pallas kernels, body(): pl.pallas_call(functools.partial(legendre_kernel, lat=lat, lev=lev, packs...  1.69 us
    pallas_call x1, Pallas kernels, body(): pl.pallas_call(outgoing_kernel, out_shape=(halo, halo, like(grid_field),...  1.33 us
    ppermute x1, starting transfers between devices, body(): second = lax.ppermute(to_second, 'lat', other_neighbours(lat))  0.65 us
  transfers between devices with their start and end apart: 2, of which 0 were waited for; matrix products, arithmetic and copies ran while one was open for 0% of the time, Pallas kernels for 7%

profile of v3, /device:TPU:0, one launch (start us, length us, event | category | flops | bytes accessed | tf_op | source)
XLA Modules:
  0.0 26.5 jit_solution(7237097660635667629)
XLA Ops:
  0.0 0.0 copy-start
  0.0 1.3 %outgoing.1 = (bf16[32,256]{1,0:T(8,128)(2,1)S(1)}, bf16[32,256]{1,0:T(8,128)(2,1)S(1)}, bf16[2,160,128]{2,1,0:T(8,128)(2,1)S(1)}, s32[4,8,128]{2,1,0:T(8,128)S(...) custom-call(s32[1,2,32]{2,1,0:T(2,128)} %send_hbm.1, ...), custom_call_target="tpu_custom_call" | custom-call | tf_op jit(solution)/shard_map/outgoing/pallas_call | solution.py:327
  1.3 3.0 %collective-permute-start = (bf16[32,256]{1,0:T(8,128)(2,1)S(1)}, bf16[32,256]{1,0:T(8,128)(2,1)S(1)}, u32[]{:S(2)}, u32[]{:S(2)}) collective-permute-start(bf16[32,256]{1,0:T(8,128)(2,1)S(1)} %get-tuple-element.22), channel_id=1, source_target_pairs={{0,4},{4,0},{8,12},{12,8},{16,20},{20,16},{24,28},{28,24},{1,5},{5... | collective-permute-start | bytes 49160 | tf_op jit(solution)/shard_map/ppermute | solution.py:338
  4.3 0.7 %collective-permute-start.1 = (bf16[32,256]{1,0:T(8,128)(2,1)S(1)}, bf16[32,256]{1,0:T(8,128)(2,1)S(1)}, u32[]{:S(2)}, u32[]{:S(2)}) collective-permute-start(bf16[32,256]{1,0:T(8,128)(2,1)S(1)} %get-tuple-element.23), channel_id=1, source_target_pairs={{4,8},{12,16},{20,24},{8,4},{16,12},{24,20},{5,9},{13,17},{21,25},... | collective-permute-start | bytes 49160 | tf_op jit(solution)/shard_map/ppermute | solution.py:339
  5.0 2.0 %tables.1 = (bf16[4,10,128,256]{3,2,1,0:T(8,128)(2,1)S(1)}, f32[4,10,40,256]{3,2,1,0:T(8,128)S(1)}, s32[40,128]{1,0:T(8,128)S(1)}) custom-call(s32[4,8,128]{2,1,0:T(8,128)S(1)} %get-tuple-element.16.lengths_ref, s32[10,128]{1,0:T(8,128)S(1)} %get-tuple-element.17.wave_ref, s32[1280]{0:T(1024)} %slot_hbm.1), custom_call_target="tpu_custom_call" | custom-call | flops 13762560 | bytes 5160960 | tf_op jit(solution)/shard_map/tables/pallas_call | solution.py:342
  7.0 0.0 collective-permute-done.first_ref
  7.0 0.0 collective-permute-done.1.second_ref
  7.0 1.8 %transform.1 = bf16[32,8,128]{2,1,0:T(8,128)(2,1)S(1)} custom-call(s32[4,8,128]{2,1,0:T(8,128)S(1)} %get-tuple-element.16.lengths_ref, s32[2,160]{1,0:T(2,128)S(1)} %get-tuple-element.19.donor_ref, s32[2,160]{1,0:T(2,128)S(1)} %get-tuple-element.20.tile_ref, bf16[2,160,128]{2,1,0:T(8,128)(2,1)S(1)} %get-tuple-element.21.field_ref, ...), custom_call_target="tpu_custom_call" | custom-call | tf_op jit(solution)/shard_map/transform/pallas_call | solution.py:359
  8.8 16.0 %all_to_all.5 = bf16[32,8,128]{2,1,0:T(8,128)(2,1)S(1)} all-to-all(bf16[32,8,128]{2,1,0:T(8,128)(2,1)S(1)} %transform.1), channel_id=1, replica_groups=mesh['lat'=8,'lev'=4] {'lat','lev'}, dimensions={0} | all-to-all | bytes 131072 | tf_op jit(solution)/shard_map/all_to_all | solution.py:371
  24.8 0.0 copy-done
  24.8 1.7 %legendre.1 = bf16[16,40,1280]{2,1,0:T(8,128)(2,1)} custom-call(s32[40,128]{1,0:T(8,128)S(1)} %get-tuple-element.18.limits_ref, bf16[256,128]{1,0:T(8,128)(2,1)S(1)} %bitcast.7, bf16[1280,1280]{1,0:T(8,128)(2,1)S(1)} %bitcast.6), custom_call_target="tpu_custom_call" | custom-call | tf_op jit(solution)/shard_map/legendre/pallas_call | solution.py:376
Async XLA Ops:
  0.0 24.8 %copy-start = (bf16[40,32,1280]{2,1,0:T(8,128)(2,1)S(1)}, bf16[40,32,1280]{2,1,0:T(8,128)(2,1)}, u32[]{:S(2)}) copy-start(bf16[40,32,1280]{2,1,0:T(8,128)(2,1)} %param.15) | copy-start | bytes 9830404
  1.3 5.7 %collective-permute-start = (bf16[32,256]{1,0:T(8,128)(2,1)S(1)}, bf16[32,256]{1,0:T(8,128)(2,1)S(1)}, u32[]{:S(2)}, u32[]{:S(2)}) collective-permute-start(bf16[32,256]{1,0:T(8,128)(2,1)S(1)} %get-tuple-element.22), channel_id=1, source_target_pairs={{0,4},{4,0},{8,12},{12,8},{16,20},{20,16},{24,28},{28,24},{1,5},{5... | collective-permute-start | bytes 49160 | tf_op jit(solution)/shard_map/ppermute | solution.py:338
  4.3 2.7 %collective-permute-start.1 = (bf16[32,256]{1,0:T(8,128)(2,1)S(1)}, bf16[32,256]{1,0:T(8,128)(2,1)S(1)}, u32[]{:S(2)}, u32[]{:S(2)}) collective-permute-start(bf16[32,256]{1,0:T(8,128)(2,1)S(1)} %get-tuple-element.23), channel_id=1, source_target_pairs={{4,8},{12,16},{20,24},{8,4},{16,12},{24,20},{5,9},{13,17},{21,25},... | collective-permute-start | bytes 49160 | tf_op jit(solution)/shard_map/ppermute | solution.py:339

commit v4 on v3

v4 whole, which is shorter than its diff:
```python
import functools
import math

import jax
import jax.numpy as jnp
from jax import lax
from jax.experimental import pallas as pl
from jax.experimental.pallas import tpu as pltpu
from jax.sharding import PartitionSpec as P

PTS = 5120
LANES = 128
BF16 = jnp.bfloat16
F32 = jnp.float32
VMEM = pl.BlockSpec(memory_space=pltpu.VMEM)
HBM = pl.BlockSpec(memory_space=pltpu.HBM)
CONTRACT_ROWS = (((0,), (0,)), ((), ()))


def params(mebibytes):
    return pltpu.CompilerParams(vmem_limit_bytes=mebibytes << 20)


def one_hot(condition):
    return jnp.where(condition, 1.0, 0.0).astype(BF16)


def side_by_side(field_ref):
    return jnp.concatenate([field_ref[l] for l in range(field_ref.shape[0])], axis=1)


def outgoing_kernel(
    send_hbm, field_hbm, length_hbm, wave_hbm, far_ref, near_ref, field_ref, lengths_ref, wave_ref,
    send_ref, length_ref, sems,
):
    pairs = (
        (send_hbm, send_ref), (field_hbm, field_ref), (length_hbm, length_ref), (wave_hbm, wave_ref)
    )
    copies = [pltpu.make_async_copy(*pair, sems.at[i]) for i, pair in enumerate(pairs)]
    for copy in copies:
        copy.start()
    copies[0].wait()
    copies[1].wait()
    band = lax.axis_index("lat")
    even = lax.rem(band, 2) == 0
    own = side_by_side(field_ref)
    blocks, count = own.shape[0], send_ref.shape[2]
    rows = lax.broadcasted_iota(jnp.int32, (blocks, count), 0)
    below, above = send_ref[0, 0:1, :], send_ref[0, 1:2, :]
    for ref, listed in (
        (far_ref, jnp.where(even, below, above)),
        (near_ref, jnp.where(even, above, below)),
    ):
        picked = lax.dot_general(
            one_hot(rows == listed), own, CONTRACT_ROWS, preferred_element_type=F32
        )
        ref[...] = picked.astype(BF16)
    copies[2].wait()
    circles = lengths_ref.shape[0] // 2
    for i in range(2 * circles):
        length = length_ref[band * circles + i % circles]
        lengths_ref[i : i + 1] = jnp.full((1, LANES), length, jnp.int32)
    copies[3].wait()


def turn(steps, waves, length, inverse):
    phase = steps * waves
    rest = phase - jnp.round(phase * inverse) * length
    f = rest * inverse
    x = f * f
    s = math.pi ** 11 / -math.factorial(11)
    for k in (9, 7, 5, 3, 1):
        s = s * x + (-1) ** (k // 2) * math.pi**k / math.factorial(k)
    s = s * f
    c = math.pi ** 10 / -math.factorial(10)
    for k in (8, 6, 4, 2, 0):
        c = c * x + (-1) ** (k // 2) * math.pi**k / math.factorial(k)
    return 1.0 - 2.0 * (s * s), 2.0 * (s * c)


def log(n):
    return n.bit_length() - 1


def times(a, b):
    return a[0] * b[0] - a[1] * b[1], a[0] * b[1] + a[1] * b[0]


def table_kernel(
    lengths_ref, wave_ref, field_ref, slot_hbm, donor_hbm, tile_hbm, kernels_hbm, legendre_hbm,
    fine_ref, coarse_ref, limits_ref, hot_ref, own_ref, kind_ref, kernels_ref, legendre_ref,
    order_ref, slot_ref, donor_ref, tile_ref, sems, *, lat, lev,
):
    circles, tiles = fine_ref.shape[:2]
    coarse = coarse_ref.shape[2]
    pairs = (
        (slot_hbm, slot_ref), (donor_hbm, donor_ref), (tile_hbm, tile_ref),
        (kernels_hbm, kernels_ref), (legendre_hbm, legendre_ref),
    )
    copies = [pltpu.make_async_copy(*pair, sems.at[i]) for i, pair in enumerate(pairs)]
    for copy in copies:
        copy.start()
    step = lax.broadcasted_iota(jnp.int32, (8, LANES), 0).astype(F32)

    def doubled(base, factor_of, groups):
        out = [base]
        while len(out) < groups:
            out += [times(e, factor_of(len(out))) for e in out[: groups - len(out)]]
        return out

    def one(index, _):
        g, t = index // tiles, lax.rem(index, tiles)
        length = jnp.broadcast_to(lengths_ref[pl.ds(g, 1)], (8, LANES)).astype(F32)
        inverse = 1.0 / length
        waves = jnp.broadcast_to(wave_ref[pl.ds(t, 1), :], (8, LANES)).astype(F32)
        hop_steps = jnp.left_shift(8, lax.broadcasted_iota(jnp.int32, (8, LANES), 0)).astype(F32)
        hops = turn(hop_steps, waves, length, inverse)
        far = turn(hop_steps * float(LANES), waves, length, inverse)

        def hop(table):
            def factor(groups):
                k = groups.bit_length() - 1
                return tuple(jnp.broadcast_to(x[k : k + 1], (8, LANES)) for x in table)

            return factor

        fine = doubled(turn(step, waves, length, inverse), hop(hops), LANES // 8)
        fine_ref[g, t] = jnp.concatenate(
            [jnp.concatenate([e[p] for e in fine], axis=0) for p in range(2)], axis=1
        ).astype(BF16)
        wide = doubled(turn(step * float(LANES), waves, length, inverse), hop(far), coarse // 8)
        coarse_ref[g, t] = jnp.concatenate(
            [jnp.concatenate([e[p] for e in wide], axis=0) for p in range(2)], axis=1
        )
        return 0

    lax.fori_loop(0, circles * tiles, one, 0, unroll=2)

    copies[0].wait()
    slots = limits_ref.shape[0]
    first = (lax.axis_index("lat") * lev + lax.axis_index("lev")) * slots
    for s in range(slots):
        limits_ref[s : s + 1] = jnp.full((1, LANES), slot_ref[first + s], jnp.int32)

    copies[1].wait()
    copies[2].wait()
    own = side_by_side(field_ref)
    blocks = own.shape[0]
    listed = jnp.concatenate(
        [donor_ref[...], tile_ref[...], jnp.zeros((4, blocks), jnp.int32)], axis=0
    )
    columns = jnp.transpose(listed.astype(F32))
    lane = lax.broadcasted_iota(jnp.int32, (blocks, blocks), 1).astype(F32)
    halo_lane = lax.broadcasted_iota(jnp.int32, hot_ref.shape[1:], 1).astype(F32) + float(blocks)
    for k in range(2):
        donor = columns[:, k : k + 1]
        own_ref[k] = jnp.dot(one_hot(lane == donor), own, preferred_element_type=F32)
        hot_ref[k] = one_hot(halo_lane == donor)
        kind_ref[k] = jnp.broadcast_to(columns[:, 2 + k : 3 + k], (blocks, LANES))

    total = order_ref.shape[0]
    if total == lat * lev * 2 * circles:
        row = lax.broadcasted_iota(jnp.int32, (total, total), 0)
        col = lax.broadcasted_iota(jnp.int32, (total, total), 1)
        group = (row >> log(circles)) & (2 * lev - 1)
        outer = row >> log(circles * 2 * lev)
        target = (group << log(lat * circles)) | (outer << log(circles)) | (row & (circles - 1))
        order_ref[...] = one_hot(col == target)
    else:
        order_ref[...] = jnp.zeros(order_ref.shape, BF16)
    copies[3].wait()
    copies[4].wait()


def fold(parts):
    row = lax.broadcasted_iota(jnp.int32, (8, LANES), 0)
    for half in (4, 2, 1):
        low = (row & half) == 0
        count = len(parts) // 2
        parts = [
            jnp.where(low, a, pltpu.roll(b, half, 0)) + jnp.where(low, pltpu.roll(a, 8 - half, 0), b)
            for a, b in zip(parts[:count], parts[count:])
        ]
    return parts[0]


def transform_kernel(
    lengths_ref, wave_ref, far_ref, near_ref, hot_ref, own_ref, kind_ref, kernels_ref, fine_ref,
    coarse_ref, out_ref, points_ref, coeff_ref, *, top_wave,
):
    blocks = own_ref.shape[1]
    levels = own_ref.shape[2] // LANES
    circles, tiles = fine_ref.shape[:2]
    coarse = coarse_ref.shape[2]
    kinds = kernels_ref.shape[0]
    band = lax.axis_index("lat")
    even = lax.rem(band, 2) == 0

    near, far = near_ref[...], far_ref[...]
    at_end = (band == 0) | (band == lax.axis_size("lat") - 1)
    far = jnp.where(at_end, jnp.zeros_like(far), far)
    halo = jnp.concatenate([jnp.where(even, far, near), jnp.where(even, near, far)], axis=0)
    stacked = jnp.concatenate([kernels_ref[k] for k in range(kinds)], axis=1)
    arrival = [jnp.zeros((blocks, LANES), F32) for _ in range(levels)]
    for k in range(2):
        picked = jnp.dot(hot_ref[k], halo, preferred_element_type=F32)
        picked = (picked + own_ref[k]).astype(BF16)
        kind = kind_ref[k]
        for l in range(levels):
            every = jnp.dot(
                picked[:, l * LANES : (l + 1) * LANES], stacked, preferred_element_type=F32
            )
            value = every[:, :LANES]
            for q in range(1, kinds):
                value = jnp.where(kind == float(q), every[:, q * LANES : (q + 1) * LANES], value)
            arrival[l] = arrival[l] + value

    position = lax.broadcasted_iota(jnp.int32, (coarse, LANES), 0) * LANES
    position = position + lax.broadcasted_iota(jnp.int32, (coarse, LANES), 1)
    for g in range(circles):
        inside = position < jnp.broadcast_to(lengths_ref[g : g + 1], (coarse, LANES))
        parts = [arrival[l][g * coarse : (g + 1) * coarse] for l in range(levels)]
        parts = [jnp.where(inside, part * part, 0.0) for part in parts]
        points_ref[g] = jnp.concatenate(parts, axis=0).astype(BF16)

    height = 2 * circles
    lengths = lengths_ref[...]
    sine = lax.broadcasted_iota(jnp.int32, (height, LANES), 0) >= circles

    def tile(t, _):
        sums = [[] for _ in range(levels)]
        for g in range(circles):
            turned = jnp.dot(points_ref[g], fine_ref[g, t], preferred_element_type=F32)
            c, s = coarse_ref[g, t, :, :LANES], coarse_ref[g, t, :, LANES:]
            for l in range(levels):
                here = turned[l * coarse : (l + 1) * coarse]
                a, b = here[:, :LANES], here[:, LANES:]
                for value in (a * c - b * s, a * s + b * c):
                    sums[l].append(jnp.sum(value.reshape(coarse // 8, 8, LANES), axis=0))
        waves = jnp.broadcast_to(wave_ref[pl.ds(t, 1), :], (height, LANES))
        live = (waves >= 1) & (waves < top_wave) & (2 * waves < lengths)
        for l in range(levels):
            ordered = sums[l][0::2] + sums[l][1::2]
            rows = [fold(ordered[i : i + 8]) for i in range(0, height, 8)]
            rows = jnp.concatenate(rows, axis=0)
            coeff_ref[t, l * height : (l + 1) * height] = jnp.where(
                live, jnp.where(sine, -rows, rows), 0.0
            )
        return 0

    lax.fori_loop(0, tiles, tile, 0, unroll=circles * tiles <= 64)

    devices, height, _ = out_ref.shape
    width = tiles * LANES // devices
    packs = coeff_ref.shape[1] // height
    step = LANES // packs
    lane = lax.broadcasted_iota(jnp.int32, (height, LANES), 1)
    for d in range(devices):
        t, shift = divmod(d * width, LANES)
        chunk = jnp.zeros((height, LANES), F32)
        for p in range(packs):
            rows = slice(p * height, (p + 1) * height)
            at = p * step
            value = pltpu.roll(coeff_ref[t, rows], (at - shift) % LANES, 1)
            if shift + width > LANES:
                after = pltpu.roll(coeff_ref[t + 1, rows], (at - shift) % LANES, 1)
                value = jnp.where(lane < at + LANES - shift, value, after)
            chunk = value if p == 0 else jnp.where(lane < at, chunk, value)
        out_ref[d] = chunk.astype(BF16)


def legendre_kernel(limits_ref, arrived_ref, order_ref, legendre_ref, out_hbm, out_ref, sems, *, packs):
    outputs, slots, top_wave = out_ref.shape
    circles = legendre_ref.shape[0] // slots
    per_tile = LANES // circles
    total = arrived_ref.shape[0]
    turned = lax.dot_general(
        arrived_ref[...], order_ref[...], CONTRACT_ROWS, preferred_element_type=F32
    )

    sub = lax.broadcasted_iota(jnp.int32, (8, LANES), 0)
    block = lax.broadcasted_iota(jnp.int32, (8, LANES), 1) >> log(circles)
    chosen = [(block == b) & ((sub & (per_tile - 1)) == b) for b in range(per_tile)]
    halves = 8 // per_tile
    in_half = [(sub >> log(per_tile)) == h for h in range(halves)]
    step = LANES // packs
    spread = []
    for k in range(slots // 8):
        pieces = [None] * outputs
        for l in range(packs):
            for j in range(total // LANES):
                at = l * step + 8 * k
                v = turned[at : at + 8, j * LANES : (j + 1) * LANES]
                rolled = [v] + [pltpu.roll(v, circles * d, 1) for d in range(1, per_tile)]
                for i in range(per_tile):
                    a = jnp.zeros((8, LANES), F32)
                    for b in range(per_tile):
                        a = jnp.where(chosen[b], rolled[(b - i) % per_tile], a)
                    group_lev, part = divmod(j * per_tile + i, 2)
                    pieces[(group_lev * packs + l) * 2 + part] = jnp.concatenate(
                        [jnp.where(in_half[h], a, 0.0) for h in range(halves)], axis=1
                    )
        spread.append(jnp.concatenate(pieces, axis=0).astype(BF16))

    wide = 2 * LANES
    lane = lax.broadcasted_iota(jnp.int32, (8, wide), 1)
    limits = [limits_ref[8 * k : 8 * k + 8] for k in range(slots // 8)]
    limits = [jnp.concatenate([m, m], axis=1) for m in limits]
    copies = []
    for n in range(0, top_wave, wide):
        sums = [
            jnp.dot(
                spread[k],
                legendre_ref[8 * k * circles : 8 * (k + 1) * circles, n : n + wide],
                preferred_element_type=F32,
            )
            for k in range(slots // 8)
        ]
        keep = [lane + n >= m for m in limits]
        for o in range(outputs):
            out_ref[o, :, n : n + wide] = jnp.concatenate(
                [jnp.where(keep[k], sums[k][8 * o : 8 * o + 8], 0.0) for k in range(slots // 8)],
                axis=0,
            ).astype(BF16)
        columns = (slice(None), slice(None), pl.ds(n, wide))
        copies.append(
            pltpu.make_async_copy(
                out_ref.at[columns], out_hbm.at[columns], sems.at[n // wide]
            )
        )
        copies[-1].start()
    for copy in copies:
        copy.wait()


def other_neighbours(lat, lev):
    inner = [(i, i + 1) for i in range(1, lat - 1, 2)]
    inner += [(j, i) for i, j in inner]
    pairs = [(i * lev + l, j * lev + l) for i, j in inner for l in range(lev)]
    return pairs + [(i * lev + l, i * lev + (l ^ 1)) for i in (0, lat - 1) for l in range(lev)]


def body(
    grid_field, send_blocks, donor_index, tile_choice, kernel_tiles, circle_len, slot_wave, legendre
):
    levels, blocks, _ = grid_field.shape
    send_count = send_blocks.shape[2]
    slots, circles, top_wave = legendre.shape
    lat, lev = lax.axis_size("lat"), lax.axis_size("lev")
    devices = lat * lev
    coarse = PTS // LANES
    own = blocks // coarse
    tiles = slot_wave.shape[0] // LANES
    waves = slot_wave.reshape(tiles, LANES)

    def like(x):
        return jax.ShapeDtypeStruct(x.shape, x.dtype)

    def in_hbm(x):
        return pltpu.with_memory_space_constraint(x, pltpu.HBM)

    halo = jax.ShapeDtypeStruct((send_count, levels * LANES), BF16)
    to_far, to_near, field, lengths, waves = pl.pallas_call(
        outgoing_kernel,
        out_shape=(
            halo, halo, like(grid_field), jax.ShapeDtypeStruct((2 * own, LANES), jnp.int32), like(waves)
        ),
        in_specs=[HBM] * 4, out_specs=(VMEM,) * 5,
        scratch_shapes=[
            pltpu.VMEM(send_blocks.shape, jnp.int32),
            pltpu.SMEM(circle_len.shape, jnp.int32),
            pltpu.SemaphoreType.DMA((4,)),
        ],
        compiler_params=params(4), name="outgoing",
    )(*map(in_hbm, (send_blocks, grid_field, circle_len, waves)))
    near = lax.ppermute(to_near, "lat", [(i, i ^ 1) for i in range(lat)])
    far = lax.ppermute(to_far, ("lat", "lev"), other_neighbours(lat, lev))

    direct = levels == 2 and 2 * own == 8 and 4 * circles == LANES and slots % 8 == 0
    direct = direct and 2 * slots <= LANES and lev & (lev - 1) == 0
    total = devices * 2 * own if direct else 16
    entries = own * tiles * (LANES + coarse) * 2 * LANES
    donors, kinds = donor_index.T, tile_choice.T
    fine, wide, limits, hot, own_part, kind, kernels, functions, order = pl.pallas_call(
        functools.partial(table_kernel, lat=lat, lev=lev),
        out_shape=(
            jax.ShapeDtypeStruct((own, tiles, LANES, 2 * LANES), BF16),
            jax.ShapeDtypeStruct((own, tiles, coarse, 2 * LANES), F32),
            jax.ShapeDtypeStruct((slots, LANES), jnp.int32),
            jax.ShapeDtypeStruct((2, blocks, 2 * send_count), BF16),
            jax.ShapeDtypeStruct((2, blocks, levels * LANES), F32),
            jax.ShapeDtypeStruct((2, blocks, LANES), F32),
            like(kernel_tiles),
            like(legendre),
            jax.ShapeDtypeStruct((total, total), BF16),
        ),
        in_specs=[VMEM] * 3 + [HBM] * 5, out_specs=(VMEM,) * 9,
        scratch_shapes=[
            pltpu.SMEM(slot_wave.shape, jnp.int32),
            pltpu.VMEM(donors.shape, jnp.int32),
            pltpu.VMEM(donors.shape, jnp.int32),
            pltpu.SemaphoreType.DMA((5,)),
        ],
        compiler_params=params(32), name="tables",
        cost_estimate=pl.CostEstimate(flops=8 * entries, bytes_accessed=3 * entries, transcendentals=0),
    )(lengths, waves, field, *map(in_hbm, (slot_wave, donors, kinds, kernel_tiles, legendre)))

    rows = levels * 2 * own
    packs = 1
    while rows % (16 * packs) == 0 and 2 * packs * slots <= LANES:
        packs *= 2
    coeffs = pl.pallas_call(
        functools.partial(transform_kernel, top_wave=top_wave),
        out_shape=jax.ShapeDtypeStruct((devices, rows // packs, LANES), BF16),
        in_specs=[VMEM] * 10, out_specs=VMEM,
        scratch_shapes=[
            pltpu.VMEM((own, levels * coarse, LANES), BF16),
            pltpu.VMEM((tiles, rows, LANES), F32),
        ],
        compiler_params=params(40), name="transform",
    )(lengths, waves, far, near, hot, own_part, kind, kernels, fine, wide)
    arrived = lax.all_to_all(coeffs, ("lat", "lev"), 0, 0, tiled=True)

    outputs = lev * levels * 2
    height = rows // packs
    if direct:
        spectra = pl.pallas_call(
            functools.partial(legendre_kernel, packs=packs),
            out_shape=jax.ShapeDtypeStruct((outputs, slots, top_wave), BF16),
            in_specs=[VMEM] * 4, out_specs=HBM,
            scratch_shapes=[
                pltpu.VMEM((outputs, slots, top_wave), BF16),
                pltpu.SemaphoreType.DMA((top_wave // (2 * LANES),)),
            ],
            compiler_params=params(32), name="legendre",
        )(
            limits,
            arrived.reshape(devices * height, LANES),
            order,
            functions.reshape(slots * circles, top_wave),
        )
        return spectra.reshape(outputs // 2, 2, slots, top_wave)

    gathered = arrived.reshape(lat, lev, height, packs, LANES // packs)[..., :slots]
    gathered = gathered.swapaxes(2, 3).reshape(lat, lev, levels, 2, own, slots)
    gathered = gathered.transpose(1, 2, 3, 0, 4, 5).reshape(outputs // 2, 2, circles, slots)
    spectra = jnp.einsum("lcgs,sgn->lcsn", gathered, functions, preferred_element_type=F32)
    first_slot = (lax.axis_index("lat") * lev + lax.axis_index("lev")) * slots
    mine = lax.dynamic_slice_in_dim(slot_wave, first_slot, slots)
    allowed = jnp.arange(top_wave, dtype=jnp.int32)[None, :] >= mine[:, None]
    return jnp.where(allowed[None, None], spectra, 0.0).astype(BF16)


def solution(mesh):
    return jax.shard_map(
        body,
        mesh=mesh,
        in_specs=(
            P("lev", "lat", None),
            P("lat", None, None),
            P("lat", None),
            P("lat", None),
            P(),
            P(),
            P(),
            P(("lat", "lev"), None, None),
        ),
        out_specs=P(None, None, ("lat", "lev"), None),
        check_vma=False,
    )
```

time: 26.7 us -> 23.5 us (0.88)
  blocking collectives: 16 us -> 11.9 us
  starting transfers between devices: 3.65 us -> 4.55 us
    all_to_all x1, blocking collectives: 16 us -> 11.9 us  [body(): arrived = lax.all_to_all(coeffs, ('lat', 'lev'), 0, 0, tiled=True)]
    ppermute x2, starting transfers between devices: 3.65 us -> 4.55 us  [the longest x1 4.03 us: body(): near = lax.ppermute(to_near, 'lat', [(i, i ^ 1) for i in range(lat)])]
    pallas_call x2, Pallas kernels: 3.66 us -> 4.07 us  [the longest x1 2.39 us: body(): pl.pallas_call(functools.partial(table_kernel, lat=lat, lev=lev), out_sha...]
  transfers between devices with their start and end apart: 2 -> 2, of which waited for: 0 -> 0; matrix products, arithmetic and copies ran while one was open for 0% -> 0% of each run, Pallas kernels for 7% -> 10%
where the time goes in v4:
time: 23.5 us; the launch traced here: 23.3 us
  blocking collectives  11.9 us (51%)
  Pallas kernels  6.78 us (29%)
  starting transfers between devices  4.55 us (19%)
    all_to_all x1, blocking collectives, body(): arrived = lax.all_to_all(coeffs, ('lat', 'lev'), 0, 0, tiled=True)  11.9 us
    ppermute x1, starting transfers between devices, body(): near = lax.ppermute(to_near, 'lat', [(i, i ^ 1) for i in range(lat)])  4.03 us
    pallas_call x1, Pallas kernels, body(): pl.pallas_call(functools.partial(table_kernel, lat=lat, lev=lev), out_sha...  2.39 us
    pallas_call x1, Pallas kernels, body(): pl.pallas_call(functools.partial(legendre_kernel, packs=packs), out_shape...  1.68 us
    pallas_call x1, Pallas kernels, body(): pl.pallas_call(functools.partial(transform_kernel, top_wave=top_wave), ou...  1.56 us
    pallas_call x1, Pallas kernels, body(): pl.pallas_call(outgoing_kernel, out_shape=(halo, halo, like(grid_field),...  1.15 us
    ppermute x1, starting transfers between devices, body(): far = lax.ppermute(to_far, ('lat', 'lev'), other_neighbours(lat, lev))  0.52 us
  transfers between devices with their start and end apart: 2, of which 0 were waited for; matrix products, arithmetic and copies ran while one was open for 0% of the time, Pallas kernels for 10%

profile of v4, /device:TPU:0, one launch (start us, length us, event | category | flops | bytes accessed | tf_op | source)
XLA Modules:
  0.0 23.3 jit_solution(14000592281344096995)
XLA Ops:
  0.0 1.2 %outgoing.1 = (bf16[32,256]{1,0:T(8,128)(2,1)S(1)}, bf16[32,256]{1,0:T(8,128)(2,1)S(1)}, bf16[2,160,128]{2,1,0:T(8,128)(2,1)S(1)}, s32[8,128]{1,0:T(8,128)S(1)}, s32[10,128]{1,0:T(8,128)S(1)}) custom-call(s32[1,2,32]{2,1,0:T(2,128)} %send_hbm.1, bf16[2,160,128]{2,1,0:T(8,128)(2,1)} %field_hbm.1, s32[32]{0:T(128)} %length_hbm.1, s32[10,128]{1,0:T(8,128)} %bitcast.8), custom_call_target="tpu_custom_call" | custom-call | tf_op jit(solution)/shard_map/outgoing/pallas_call | solution.py:363
  1.2 0.5 %collective-permute-start = (bf16[32,256]{1,0:T(8,128)(2,1)S(1)}, bf16[32,256]{1,0:T(8,128)(2,1)S(1)}, u32[]{:S(2)}, u32[]{:S(2)}) collective-permute-start(bf16[32,256]{1,0:T(8,128)(2,1)S(1)} %get-tuple-element.23), channel_id=1, source_target_pairs={{4,8},{5,9},{6,10},{7,11},{12,16},{13,17},{14,18},{15,19},{20,24},... | collective-permute-start | bytes 49160 | tf_op jit(solution)/shard_map/ppermute | solution.py:377
  1.7 4.0 %collective-permute-start.1 = (bf16[32,256]{1,0:T(8,128)(2,1)S(1)}, bf16[32,256]{1,0:T(8,128)(2,1)S(1)}, u32[]{:S(2)}, u32[]{:S(2)}) collective-permute-start(bf16[32,256]{1,0:T(8,128)(2,1)S(1)} %get-tuple-element.24), channel_id=1, source_target_pairs={{0,4},{4,0},{8,12},{12,8},{16,20},{20,16},{24,28},{28,24},{1,5},{5... | collective-permute-start | bytes 49160 | tf_op jit(solution)/shard_map/ppermute | solution.py:376
  5.7 2.4 %tables.1 = (bf16[4,10,128,256]{3,2,1,0:T(8,128)(2,1)S(1)}, f32[4,10,40,256]{3,2,1,0:T(8,128)S(1)}, s32[40,128]{1,0:T(8,128)S(1)}, bf16[2,160,64]{2,1,0:T(8,128)...) custom-call(s32[8,128]{1,0:T(8,128)S(1)} %get-tuple-element.19.lengt, ...), custom_call_target="tpu_custom_call" | custom-call | flops 13762560 | bytes 5160960 | tf_op jit(solution)/shard_map/tables/pallas_call | solution.py:384
  8.1 0.0 collective-permute-done.far_ref
  8.1 0.0 collective-permute-done.1.near_ref
  8.1 1.6 %transform.1 = bf16[32,8,128]{2,1,0:T(8,128)(2,1)S(1)} custom-call(s32[8,128]{1,0:T(8,128)S(1)} %get-tuple-element.19.lengths_ref, s32[10,128]{1,0:T(8,128)S(1)} %get-tuple-element.20.wave_ref, bf16[32,256]{1,0:T(8,128)(2,1)S(1)} %collective-permute-done.far_ref, bf16[32,256]{1,0:T(8,128)(2,1)S(1)} %collective-permute-done.1.near_ref, ...), custom_call_target="tpu_custom_call" | custom-call | tf_op jit(solution)/shard_map/transform/pallas_call | solution.py:412
  9.7 11.9 %all_to_all.5 = bf16[32,8,128]{2,1,0:T(8,128)(2,1)S(1)} all-to-all(bf16[32,8,128]{2,1,0:T(8,128)(2,1)S(1)} %transform.1), channel_id=1, replica_groups=mesh['lat'=8,'lev'=4] {'lat','lev'}, dimensions={0} | all-to-all | bytes 131072 | tf_op jit(solution)/shard_map/all_to_all | solution.py:422
  21.6 1.7 %legendre.1 = bf16[16,40,1280]{2,1,0:T(8,128)(2,1)} custom-call(s32[40,128]{1,0:T(8,128)S(1)} %get-tuple-element.22.limits_ref, bf16[256,128]{1,0:T(8,128)(2,1)S(1)} %bitcast.7, bf16[256,256]{1,0:T(8,128)(2,1)S(1)} %get-tuple-element.31.order_ref, bf16[1280,1280]{1,0:T(8,128)(2,1)S(1)} %bitcast.6), custom_call_target="tpu_custom_call" | custom-call | tf_op jit(solution)/shard_map/legendre/pallas_call | solution.py:427
Async XLA Ops:
  1.2 7.0 %collective-permute-start = (bf16[32,256]{1,0:T(8,128)(2,1)S(1)}, bf16[32,256]{1,0:T(8,128)(2,1)S(1)}, u32[]{:S(2)}, u32[]{:S(2)}) collective-permute-start(bf16[32,256]{1,0:T(8,128)(2,1)S(1)} %get-tuple-element.23), channel_id=1, source_target_pairs={{4,8},{5,9},{6,10},{7,11},{12,16},{13,17},{14,18},{15,19},{20,24},... | collective-permute-start | bytes 49160 | tf_op jit(solution)/shard_map/ppermute | solution.py:377
  1.7 6.4 %collective-permute-start.1 = (bf16[32,256]{1,0:T(8,128)(2,1)S(1)}, bf16[32,256]{1,0:T(8,128)(2,1)S(1)}, u32[]{:S(2)}, u32[]{:S(2)}) collective-permute-start(bf16[32,256]{1,0:T(8,128)(2,1)S(1)} %get-tuple-element.24), channel_id=1, source_target_pairs={{0,4},{4,0},{8,12},{12,8},{16,20},{20,16},{24,28},{28,24},{1,5},{5... | collective-permute-start | bytes 49160 | tf_op jit(solution)/shard_map/ppermute | solution.py:376

commit v5 on v4

--- a/solution.py
+++ b/solution.py
@@ -88,11 +88,12 @@
 
 def table_kernel(
     lengths_ref, wave_ref, field_ref, slot_hbm, donor_hbm, tile_hbm, kernels_hbm, legendre_hbm,
-    fine_ref, coarse_ref, limits_ref, hot_ref, own_ref, kind_ref, kernels_ref, legendre_ref,
-    order_ref, slot_ref, donor_ref, tile_ref, sems, *, lat, lev,
+    fine_ref, coarse_ref, limits_ref, choice_ref, arrival_ref, kernels_ref, legendre_ref, order_ref,
+    slot_ref, donor_ref, tile_ref, sems, *, lat, lev,
 ):
     circles, tiles = fine_ref.shape[:2]
-    coarse = coarse_ref.shape[2]
+    levels, blocks, _ = field_ref.shape
+    coarse = blocks // circles
     pairs = (
         (slot_hbm, slot_ref), (donor_hbm, donor_ref), (tile_hbm, tile_ref),
         (kernels_hbm, kernels_ref), (legendre_hbm, legendre_ref),
@@ -124,13 +125,17 @@
 
             return factor
 
-        fine = doubled(turn(step, waves, length, inverse), hop(hops), LANES // 8)
+        middle = float(LANES // 2 * (coarse - 1))
+        fine = doubled(turn(step + middle, waves, length, inverse), hop(hops), LANES // 8)
         fine_ref[g, t] = jnp.concatenate(
             [jnp.concatenate([e[p] for e in fine], axis=0) for p in range(2)], axis=1
         ).astype(BF16)
-        wide = doubled(turn(step * float(LANES), waves, length, inverse), hop(far), coarse // 8)
+        start = turn(step * float(LANES) + float(LANES // 2), waves, length, inverse)
+        half = coarse // 2
+        wide = doubled(start, hop(far), -(-half // 8))
+        wide = [jnp.concatenate([e[p] for e in wide], axis=0)[:half] for p in range(2)]
         coarse_ref[g, t] = jnp.concatenate(
-            [jnp.concatenate([e[p] for e in wide], axis=0) for p in range(2)], axis=1
+            [jnp.concatenate([part] * levels, axis=0) for part in wide], axis=1
         )
         return 0
 
@@ -144,19 +149,49 @@
 
     copies[1].wait()
     copies[2].wait()
+    copies[3].wait()
+    donor, kind = donor_ref[...], tile_ref[...]
+    listed = jnp.concatenate(
+        [donor & 15, donor >> 4, kind, jnp.zeros((2, blocks), jnp.int32)], axis=0
+    )
+    source = lax.broadcasted_iota(jnp.int32, (blocks, blocks), 0)
+    place = lax.broadcasted_iota(jnp.int32, (blocks, blocks), 1)
+    begin = jnp.zeros((blocks, blocks), jnp.int32)
+    for g in range(1, circles):
+        begin = jnp.where(place >= g * coarse, g * coarse, begin)
+    place = place - begin
+    half = coarse // 2
+    wanted = begin + jnp.where(place < half, place + half, coarse - 1 - place)
+    listed = jnp.dot(
+        listed.astype(F32).astype(BF16), one_hot(source == wanted), preferred_element_type=F32
+    )
+    columns = jnp.transpose(listed)
     own = side_by_side(field_ref)
-    blocks = own.shape[0]
-    listed = jnp.concatenate(
-        [donor_ref[...], tile_ref[...], jnp.zeros((4, blocks), jnp.int32)], axis=0
-    )
-    columns = jnp.transpose(listed.astype(F32))
+    kinds = kernels_ref.shape[0]
+    count = choice_ref.shape[1] // kinds
+    stacked = jnp.concatenate([kernels_ref[k] for k in range(kinds)], axis=1)
     lane = lax.broadcasted_iota(jnp.int32, (blocks, blocks), 1).astype(F32)
-    halo_lane = lax.broadcasted_iota(jnp.int32, hot_ref.shape[1:], 1).astype(F32) + float(blocks)
+    entry = lax.broadcasted_iota(jnp.int32, choice_ref.shape, 1).astype(F32)
+    arrival = [jnp.zeros((blocks, LANES), F32) for _ in range(levels)]
+    choice = jnp.zeros(choice_ref.shape, F32)
     for k in range(2):
-        donor = columns[:, k : k + 1]
-        own_ref[k] = jnp.dot(one_hot(lane == donor), own, preferred_element_type=F32)
-        hot_ref[k] = one_hot(halo_lane == donor)
-        kind_ref[k] = jnp.broadcast_to(columns[:, 2 + k : 3 + k], (blocks, LANES))
+        donor = columns[:, k : k + 1] + 16.0 * columns[:, 2 + k : 3 + k]
+        kind = columns[:, 4 + k : 5 + k]
+        code = jnp.where(donor >= float(blocks), donor - float(blocks) + float(count) * kind, -1.0)
+        choice = choice + jnp.where(entry == code, 1.0, 0.0)
+        picked = jnp.dot(one_hot(lane == donor), own, preferred_element_type=F32).astype(BF16)
+        kind = jnp.broadcast_to(kind, (blocks, LANES))
+        for l in range(levels):
+            every = jnp.dot(
+                picked[:, l * LANES : (l + 1) * LANES], stacked, preferred_element_type=F32
+            )
+            value = every[:, :LANES]
+            for q in range(1, kinds):
+                value = jnp.where(kind == float(q), every[:, q * LANES : (q + 1) * LANES], value)
+            arrival[l] = arrival[l] + value
+    choice_ref[...] = choice.astype(BF16)
+    for l in range(levels):
+        arrival_ref[l] = arrival[l]
 
     total = order_ref.shape[0]
     if total == lat * lev * 2 * circles:
@@ -168,7 +203,6 @@
         order_ref[...] = one_hot(col == target)
     else:
         order_ref[...] = jnp.zeros(order_ref.shape, BF16)
-    copies[3].wait()
     copies[4].wait()
 
 
@@ -185,13 +219,13 @@
 
 
 def transform_kernel(
-    lengths_ref, wave_ref, far_ref, near_ref, hot_ref, own_ref, kind_ref, kernels_ref, fine_ref,
+    lengths_ref, wave_ref, far_ref, near_ref, choice_ref, arrival_ref, kernels_ref, fine_ref,
     coarse_ref, out_ref, points_ref, coeff_ref, *, top_wave,
 ):
-    blocks = own_ref.shape[1]
-    levels = own_ref.shape[2] // LANES
+    levels, blocks, _ = arrival_ref.shape
     circles, tiles = fine_ref.shape[:2]
-    coarse = coarse_ref.shape[2]
+    coarse = blocks // circles
+    half = coarse // 2
     kinds = kernels_ref.shape[0]
     band = lax.axis_index("lat")
     even = lax.rem(band, 2) == 0
@@ -201,69 +235,95 @@
     far = jnp.where(at_end, jnp.zeros_like(far), far)
     halo = jnp.concatenate([jnp.where(even, far, near), jnp.where(even, near, far)], axis=0)
     stacked = jnp.concatenate([kernels_ref[k] for k in range(kinds)], axis=1)
-    arrival = [jnp.zeros((blocks, LANES), F32) for _ in range(levels)]
-    for k in range(2):
-        picked = jnp.dot(hot_ref[k], halo, preferred_element_type=F32)
-        picked = (picked + own_ref[k]).astype(BF16)
-        kind = kind_ref[k]
-        for l in range(levels):
-            every = jnp.dot(
-                picked[:, l * LANES : (l + 1) * LANES], stacked, preferred_element_type=F32
-            )
-            value = every[:, :LANES]
-            for q in range(1, kinds):
-                value = jnp.where(kind == float(q), every[:, q * LANES : (q + 1) * LANES], value)
-            arrival[l] = arrival[l] + value
-
-    position = lax.broadcasted_iota(jnp.int32, (coarse, LANES), 0) * LANES
-    position = position + lax.broadcasted_iota(jnp.int32, (coarse, LANES), 1)
+    high, low = [], []
+    for l in range(levels):
+        every = jnp.dot(
+            halo[:, l * LANES : (l + 1) * LANES], stacked, preferred_element_type=F32
+        )
+        every = jnp.concatenate(
+            [every[:, q * LANES : (q + 1) * LANES] for q in range(kinds)], axis=0
+        )
+        high.append(every.astype(BF16))
+        low.append((every - high[-1].astype(F32)).astype(BF16))
+    arrival = jnp.dot(
+        choice_ref[...], jnp.concatenate(high, axis=1), preferred_element_type=F32
+    ) + jnp.dot(choice_ref[...], jnp.concatenate(low, axis=1), preferred_element_type=F32)
+
+    distance = lax.broadcasted_iota(jnp.int32, (coarse, LANES), 0)
+    row = jnp.where(distance < half, distance + half, coarse - 1 - distance)
+    position = row * LANES + lax.broadcasted_iota(jnp.int32, (coarse, LANES), 1)
     for g in range(circles):
         inside = position < jnp.broadcast_to(lengths_ref[g : g + 1], (coarse, LANES))
-        parts = [arrival[l][g * coarse : (g + 1) * coarse] for l in range(levels)]
-        parts = [jnp.where(inside, part * part, 0.0) for part in parts]
-        points_ref[g] = jnp.concatenate(parts, axis=0).astype(BF16)
+        sums, differences = [], []
+        for l in range(levels):
+            rows = slice(g * coarse, (g + 1) * coarse)
+            part = arrival[rows, l * LANES : (l + 1) * LANES] + arrival_ref[l, rows]
+            part = jnp.where(inside, part * part, 0.0)
+            sums.append(part[:half] + part[half:])
+            differences.append(part[:half] - part[half:])
+        points_ref[g] = jnp.concatenate(sums + differences, axis=0).astype(BF16)
 
     height = 2 * circles
     lengths = lengths_ref[...]
     sine = lax.broadcasted_iota(jnp.int32, (height, LANES), 0) >= circles
-
-    def tile(t, _):
-        sums = [[] for _ in range(levels)]
+    sub = lax.broadcasted_iota(jnp.int32, (8, LANES), 0)
+
+    def level_sum(value, l):
+        first, last = l * half, (l + 1) * half
+        total = None
+        for at in range(first // 8 * 8, last, 8):
+            piece = value[at : at + 8]
+            if at < first:
+                piece = jnp.where(sub >= first - at, piece, 0.0)
+            if at + 8 > last:
+                piece = jnp.where(sub < last - at, piece, 0.0)
+            total = piece if total is None else total + piece
+        return total
+
+    def tile(t):
+        sums = [([], []) for _ in range(levels)]
         for g in range(circles):
             turned = jnp.dot(points_ref[g], fine_ref[g, t], preferred_element_type=F32)
+            both, apart = turned[: levels * half], turned[levels * half :]
             c, s = coarse_ref[g, t, :, :LANES], coarse_ref[g, t, :, LANES:]
+            real = both[:, :LANES] * c - apart[:, LANES:] * s
+            imag = both[:, LANES:] * c + apart[:, :LANES] * s
             for l in range(levels):
-                here = turned[l * coarse : (l + 1) * coarse]
-                a, b = here[:, :LANES], here[:, LANES:]
-                for value in (a * c - b * s, a * s + b * c):
-                    sums[l].append(jnp.sum(value.reshape(coarse // 8, 8, LANES), axis=0))
+                sums[l][0].append(level_sum(real, l))
+                sums[l][1].append(level_sum(imag, l))
         waves = jnp.broadcast_to(wave_ref[pl.ds(t, 1), :], (height, LANES))
         live = (waves >= 1) & (waves < top_wave) & (2 * waves < lengths)
+        found = []
         for l in range(levels):
-            ordered = sums[l][0::2] + sums[l][1::2]
+            ordered = sums[l][0] + sums[l][1]
             rows = [fold(ordered[i : i + 8]) for i in range(0, height, 8)]
             rows = jnp.concatenate(rows, axis=0)
-            coeff_ref[t, l * height : (l + 1) * height] = jnp.where(
-                live, jnp.where(sine, -rows, rows), 0.0
-            )
+            found.append(jnp.where(live, jnp.where(sine, -rows, rows), 0.0))
+        return jnp.concatenate(found, axis=0)
+
+    def stored(t, _):
+        coeff_ref[t] = tile(t)
         return 0
 
-    lax.fori_loop(0, tiles, tile, 0, unroll=circles * tiles <= 64)
-
-    devices, height, _ = out_ref.shape
+    devices, chunk_rows, _ = out_ref.shape
     width = tiles * LANES // devices
-    packs = coeff_ref.shape[1] // height
+    packs = coeff_ref.shape[1] // chunk_rows
     step = LANES // packs
-    lane = lax.broadcasted_iota(jnp.int32, (height, LANES), 1)
+    lane = lax.broadcasted_iota(jnp.int32, (chunk_rows, LANES), 1)
+    if circles * tiles <= 64:
+        coeffs = [tile(t) for t in range(tiles)]
+    else:
+        lax.fori_loop(0, tiles, stored, 0)
+        coeffs = [coeff_ref.at[t] for t in range(tiles)]
     for d in range(devices):
         t, shift = divmod(d * width, LANES)
-        chunk = jnp.zeros((height, LANES), F32)
+        chunk = jnp.zeros((chunk_rows, LANES), F32)
         for p in range(packs):
-            rows = slice(p * height, (p + 1) * height)
+            rows = slice(p * chunk_rows, (p + 1) * chunk_rows)
             at = p * step
-            value = pltpu.roll(coeff_ref[t, rows], (at - shift) % LANES, 1)
+            value = pltpu.roll(coeffs[t][rows], (at - shift) % LANES, 1)
             if shift + width > LANES:
-                after = pltpu.roll(coeff_ref[t + 1, rows], (at - shift) % LANES, 1)
+                after = pltpu.roll(coeffs[t + 1][rows], (at - shift) % LANES, 1)
                 value = jnp.where(lane < at + LANES - shift, value, after)
             chunk = value if p == 0 else jnp.where(lane < at, chunk, value)
         out_ref[d] = chunk.astype(BF16)
@@ -381,20 +441,19 @@
     total = devices * 2 * own if direct else 16
     entries = own * tiles * (LANES + coarse) * 2 * LANES
     donors, kinds = donor_index.T, tile_choice.T
-    fine, wide, limits, hot, own_part, kind, kernels, functions, order = pl.pallas_call(
+    fine, wide, limits, choice, own_part, kernels, functions, order = pl.pallas_call(
         functools.partial(table_kernel, lat=lat, lev=lev),
         out_shape=(
             jax.ShapeDtypeStruct((own, tiles, LANES, 2 * LANES), BF16),
-            jax.ShapeDtypeStruct((own, tiles, coarse, 2 * LANES), F32),
+            jax.ShapeDtypeStruct((own, tiles, levels * coarse // 2, 2 * LANES), F32),
             jax.ShapeDtypeStruct((slots, LANES), jnp.int32),
-            jax.ShapeDtypeStruct((2, blocks, 2 * send_count), BF16),
-            jax.ShapeDtypeStruct((2, blocks, levels * LANES), F32),
-            jax.ShapeDtypeStruct((2, blocks, LANES), F32),
+            jax.ShapeDtypeStruct((blocks, kernel_tiles.shape[0] * 2 * send_count), BF16),
+            jax.ShapeDtypeStruct((levels, blocks, LANES), F32),
             like(kernel_tiles),
             like(legendre),
             jax.ShapeDtypeStruct((total, total), BF16),
         ),
-        in_specs=[VMEM] * 3 + [HBM] * 5, out_specs=(VMEM,) * 9,
+        in_specs=[VMEM] * 3 + [HBM] * 5, out_specs=(VMEM,) * 8,
         scratch_shapes=[
             pltpu.SMEM(slot_wave.shape, jnp.int32),
             pltpu.VMEM(donors.shape, jnp.int32),
@@ -412,13 +471,13 @@
     coeffs = pl.pallas_call(
         functools.partial(transform_kernel, top_wave=top_wave),
         out_shape=jax.ShapeDtypeStruct((devices, rows // packs, LANES), BF16),
-        in_specs=[VMEM] * 10, out_specs=VMEM,
+        in_specs=[VMEM] * 9, out_specs=VMEM,
         scratch_shapes=[
             pltpu.VMEM((own, levels * coarse, LANES), BF16),
             pltpu.VMEM((tiles, rows, LANES), F32),
         ],
         compiler_params=params(40), name="transform",
-    )(lengths, waves, far, near, hot, own_part, kind, kernels, fine, wide)
+    )(lengths, waves, far, near, choice, own_part, kernels, fine, wide)
     arrived = lax.all_to_all(coeffs, ("lat", "lev"), 0, 0, tiled=True)
 
     outputs = lev * levels * 2

time: 23.5 us -> 24 us (1.021)
  Pallas kernels: 6.78 us -> 7.32 us
    pallas_call x1, Pallas kernels: 2.39 us -> 3.24 us  [body(): pl.pallas_call(functools.partial(table_kernel, lat=lat, lev=lev), out_sha...]
    pallas_call x1, Pallas kernels: 1.56 us -> 1.25 us  [body(): pl.pallas_call(functools.partial(transform_kernel, top_wave=top_wave), ou...]
  transfers between devices with their start and end apart: 2 -> 2, of which waited for: 0 -> 0; matrix products, arithmetic and copies ran while one was open for 0% -> 0% of each run, Pallas kernels for 10% -> 14%
where the time goes in v5:
time: 24 us; the launch traced here: 23.9 us
  blocking collectives  11.9 us (50%)
  Pallas kernels  7.32 us (30%)
  starting transfers between devices  4.55 us (19%)
    all_to_all x1, blocking collectives, body(): arrived = lax.all_to_all(coeffs, ('lat', 'lev'), 0, 0, tiled=True)  11.9 us
    ppermute x1, starting transfers between devices, body(): near = lax.ppermute(to_near, 'lat', [(i, i ^ 1) for i in range(lat)])  4.03 us
    pallas_call x1, Pallas kernels, body(): pl.pallas_call(functools.partial(table_kernel, lat=lat, lev=lev), out_sha...  3.24 us
    pallas_call x1, Pallas kernels, body(): pl.pallas_call(functools.partial(legendre_kernel, packs=packs), out_shape...  1.68 us
    pallas_call x1, Pallas kernels, body(): pl.pallas_call(functools.partial(transform_kernel, top_wave=top_wave), ou...  1.25 us
    pallas_call x1, Pallas kernels, body(): pl.pallas_call(outgoing_kernel, out_shape=(halo, halo, like(grid_field),...  1.15 us
    ppermute x1, starting transfers between devices, body(): far = lax.ppermute(to_far, ('lat', 'lev'), other_neighbours(lat, lev))  0.52 us
  transfers between devices with their start and end apart: 2, of which 0 were waited for; matrix products, arithmetic and copies ran while one was open for 0% of the time, Pallas kernels for 14%

profile of v5, /device:TPU:0, one launch (start us, length us, event | category | flops | bytes accessed | tf_op | source)
XLA Modules:
  0.0 23.9 jit_solution(6054754521460477517)
XLA Ops:
  0.0 1.2 %outgoing.1 = (bf16[32,256]{1,0:T(8,128)(2,1)S(1)}, bf16[32,256]{1,0:T(8,128)(2,1)S(1)}, bf16[2,160,128]{2,1,0:T(8,128)(2,1)S(1)}, s32[8,128]{1,0:T(8,128)S(1)}, s32[10,128]{1,0:T(8,128)S(1)}) custom-call(s32[1,2,32]{2,1,0:T(2,128)} %send_hbm.1, bf16[2,160,128]{2,1,0:T(8,128)(2,1)} %field_hbm.1, s32[32]{0:T(128)} %length_hbm.1, s32[10,128]{1,0:T(8,128)} %bitcast.8), custom_call_target="tpu_custom_call" | custom-call | tf_op jit(solution)/shard_map/outgoing/pallas_call | solution.py:423
  1.2 0.5 %collective-permute-start = (bf16[32,256]{1,0:T(8,128)(2,1)S(1)}, bf16[32,256]{1,0:T(8,128)(2,1)S(1)}, u32[]{:S(2)}, u32[]{:S(2)}) collective-permute-start(bf16[32,256]{1,0:T(8,128)(2,1)S(1)} %get-tuple-element.22), channel_id=1, source_target_pairs={{4,8},{5,9},{6,10},{7,11},{12,16},{13,17},{14,18},{15,19},{20,24},... | collective-permute-start | bytes 49160 | tf_op jit(solution)/shard_map/ppermute | solution.py:437
  1.7 4.0 %collective-permute-start.1 = (bf16[32,256]{1,0:T(8,128)(2,1)S(1)}, bf16[32,256]{1,0:T(8,128)(2,1)S(1)}, u32[]{:S(2)}, u32[]{:S(2)}) collective-permute-start(bf16[32,256]{1,0:T(8,128)(2,1)S(1)} %get-tuple-element.23), channel_id=1, source_target_pairs={{0,4},{4,0},{8,12},{12,8},{16,20},{20,16},{24,28},{28,24},{1,5},{5... | collective-permute-start | bytes 49160 | tf_op jit(solution)/shard_map/ppermute | solution.py:436
  5.7 3.2 %tables.1 = (bf16[4,10,128,256]{3,2,1,0:T(8,128)(2,1)S(1)}, f32[4,10,40,256]{3,2,1,0:T(8,128)S(1)}, s32[40,128]{1,0:T(8,128)S(1)}, bf16[160,512]{1,0:T(8,128)(2,...) custom-call(s32[8,128]{1,0:T(8,128)S(1)} %get-tuple-element.18.lengt, ...), custom_call_target="tpu_custom_call" | custom-call | flops 13762560 | bytes 5160960 | tf_op jit(solution)/shard_map/tables/pallas_call | solution.py:444
  9.0 0.0 collective-permute-done.far_ref
  9.0 0.0 collective-permute-done.1.near_ref
  9.0 1.3 %transform.1 = bf16[32,8,128]{2,1,0:T(8,128)(2,1)S(1)} custom-call(s32[8,128]{1,0:T(8,128)S(1)} %get-tuple-element.18.lengths_ref, s32[10,128]{1,0:T(8,128)S(1)} %get-tuple-element.19.wave_ref, bf16[32,256]{1,0:T(8,128)(2,1)S(1)} %collective-permute-done.far_ref, bf16[32,256]{1,0:T(8,128)(2,1)S(1)} %collective-permute-done.1.near_ref, ...), custom_call_target="tpu_custom_call" | custom-call | tf_op jit(solution)/shard_map/transform/pallas_call | solution.py:471
  10.2 11.9 %all_to_all.5 = bf16[32,8,128]{2,1,0:T(8,128)(2,1)S(1)} all-to-all(bf16[32,8,128]{2,1,0:T(8,128)(2,1)S(1)} %transform.1), channel_id=1, replica_groups=mesh['lat'=8,'lev'=4] {'lat','lev'}, dimensions={0} | all-to-all | bytes 131072 | tf_op jit(solution)/shard_map/all_to_all | solution.py:481
  22.2 1.7 %legendre.1 = bf16[16,40,1280]{2,1,0:T(8,128)(2,1)} custom-call(s32[40,128]{1,0:T(8,128)S(1)} %get-tuple-element.21.limits_ref, bf16[256,128]{1,0:T(8,128)(2,1)S(1)} %bitcast.7, bf16[256,256]{1,0:T(8,128)(2,1)S(1)} %get-tuple-element.29.order_ref, bf16[1280,1280]{1,0:T(8,128)(2,1)S(1)} %bitcast.6), custom_call_target="tpu_custom_call" | custom-call | tf_op jit(solution)/shard_map/legendre/pallas_call | solution.py:486
Async XLA Ops:
  1.2 7.8 %collective-permute-start = (bf16[32,256]{1,0:T(8,128)(2,1)S(1)}, bf16[32,256]{1,0:T(8,128)(2,1)S(1)}, u32[]{:S(2)}, u32[]{:S(2)}) collective-permute-start(bf16[32,256]{1,0:T(8,128)(2,1)S(1)} %get-tuple-element.22), channel_id=1, source_target_pairs={{4,8},{5,9},{6,10},{7,11},{12,16},{13,17},{14,18},{15,19},{20,24},... | collective-permute-start | bytes 49160 | tf_op jit(solution)/shard_map/ppermute | solution.py:437
  1.7 7.3 %collective-permute-start.1 = (bf16[32,256]{1,0:T(8,128)(2,1)S(1)}, bf16[32,256]{1,0:T(8,128)(2,1)S(1)}, u32[]{:S(2)}, u32[]{:S(2)}) collective-permute-start(bf16[32,256]{1,0:T(8,128)(2,1)S(1)} %get-tuple-element.23), channel_id=1, source_target_pairs={{0,4},{4,0},{8,12},{12,8},{16,20},{20,16},{24,28},{28,24},{1,5},{5... | collective-permute-start | bytes 49160 | tf_op jit(solution)/shard_map/ppermute | solution.py:436

commit v6 on v5

--- a/solution.py
+++ b/solution.py
@@ -30,11 +30,13 @@
 
 
 def outgoing_kernel(
-    send_hbm, field_hbm, length_hbm, wave_hbm, far_ref, near_ref, field_ref, lengths_ref, wave_ref,
+    send_hbm, field_hbm, length_hbm, wave_hbm, donor_hbm, tile_hbm,
+    far_ref, near_ref, field_ref, lengths_ref, wave_ref, donor_ref, tile_ref,
     send_ref, length_ref, sems,
 ):
     pairs = (
-        (send_hbm, send_ref), (field_hbm, field_ref), (length_hbm, length_ref), (wave_hbm, wave_ref)
+        (send_hbm, send_ref), (field_hbm, field_ref), (length_hbm, length_ref), (wave_hbm, wave_ref),
+        (donor_hbm, donor_ref), (tile_hbm, tile_ref),
     )
     copies = [pltpu.make_async_copy(*pair, sems.at[i]) for i, pair in enumerate(pairs)]
     for copy in copies:
@@ -60,22 +62,26 @@
     for i in range(2 * circles):
         length = length_ref[band * circles + i % circles]
         lengths_ref[i : i + 1] = jnp.full((1, LANES), length, jnp.int32)
-    copies[3].wait()
+    for copy in copies[3:]:
+        copy.wait()
+
+
+SINE = (0.07761395, -0.59827207, 2.55007494, -5.16770998, 3.14159264)
+COSINE = (0.21953804, -1.33180992, 4.05840238, -4.93479245, 0.99999995)
+ROUND = 1.5 * 2.0**23
 
 
 def turn(steps, waves, length, inverse):
     phase = steps * waves
-    rest = phase - jnp.round(phase * inverse) * length
+    rest = phase - ((phase * inverse + ROUND) - ROUND) * length
     f = rest * inverse
     x = f * f
-    s = math.pi ** 11 / -math.factorial(11)
-    for k in (9, 7, 5, 3, 1):
-        s = s * x + (-1) ** (k // 2) * math.pi**k / math.factorial(k)
+    s, c = SINE[0], COSINE[0]
+    for p, q in zip(SINE[1:], COSINE[1:]):
+        s, c = s * x + p, c * x + q
     s = s * f
-    c = math.pi ** 10 / -math.factorial(10)
-    for k in (8, 6, 4, 2, 0):
-        c = c * x + (-1) ** (k // 2) * math.pi**k / math.factorial(k)
-    return 1.0 - 2.0 * (s * s), 2.0 * (s * c)
+    twice = s + s
+    return 1.0 - twice * s, twice * c
 
 
 def log(n):
@@ -87,123 +93,123 @@
 
 
 def table_kernel(
-    lengths_ref, wave_ref, field_ref, slot_hbm, donor_hbm, tile_hbm, kernels_hbm, legendre_hbm,
-    fine_ref, coarse_ref, limits_ref, choice_ref, arrival_ref, kernels_ref, legendre_ref, order_ref,
-    slot_ref, donor_ref, tile_ref, sems, *, lat, lev,
+    lengths_ref, wave_ref, field_ref, donor_ref, tile_ref, slot_hbm, kernels_hbm,
+    fine_ref, coarse_ref, limits_ref, choice_ref, arrival_ref, kernels_ref, order_ref,
+    slot_ref, sems, *, lat, lev,
 ):
     circles, tiles = fine_ref.shape[:2]
     levels, blocks, _ = field_ref.shape
     coarse = blocks // circles
-    pairs = (
-        (slot_hbm, slot_ref), (donor_hbm, donor_ref), (tile_hbm, tile_ref),
-        (kernels_hbm, kernels_ref), (legendre_hbm, legendre_ref),
-    )
+    half = coarse // 2
+    pairs = ((slot_hbm, slot_ref), (kernels_hbm, kernels_ref))
     copies = [pltpu.make_async_copy(*pair, sems.at[i]) for i, pair in enumerate(pairs)]
     for copy in copies:
         copy.start()
-    step = lax.broadcasted_iota(jnp.int32, (8, LANES), 0).astype(F32)
-
-    def doubled(base, factor_of, groups):
+    row = lax.broadcasted_iota(jnp.int32, (8, LANES), 0)
+    near_step = (row + LANES // 2 * (coarse - 1)).astype(F32)
+    far_step = (row * LANES + LANES // 2).astype(F32)
+    hop_step = jnp.left_shift(8, jnp.where(row < 4, row, row - 4 + log(LANES))).astype(F32)
+
+    def doubled(base, hops, groups):
         out = [base]
         while len(out) < groups:
-            out += [times(e, factor_of(len(out))) for e in out[: groups - len(out)]]
-        return out
-
-    def one(index, _):
-        g, t = index // tiles, lax.rem(index, tiles)
+            k = log(len(out))
+            hop = tuple(jnp.broadcast_to(x[k : k + 1], (8, LANES)) for x in hops)
+            out += [times(e, hop) for e in out[: groups - len(out)]]
+        return [jnp.concatenate(part, axis=0) for part in zip(*out)]
+
+    def circle(g):
         length = jnp.broadcast_to(lengths_ref[pl.ds(g, 1)], (8, LANES)).astype(F32)
-        inverse = 1.0 / length
+        return length, 1.0 / length
+
+    def table(g, t, length, inverse):
         waves = jnp.broadcast_to(wave_ref[pl.ds(t, 1), :], (8, LANES)).astype(F32)
-        hop_steps = jnp.left_shift(8, lax.broadcasted_iota(jnp.int32, (8, LANES), 0)).astype(F32)
-        hops = turn(hop_steps, waves, length, inverse)
-        far = turn(hop_steps * float(LANES), waves, length, inverse)
-
-        def hop(table):
-            def factor(groups):
-                k = groups.bit_length() - 1
-                return tuple(jnp.broadcast_to(x[k : k + 1], (8, LANES)) for x in table)
-
-            return factor
-
-        middle = float(LANES // 2 * (coarse - 1))
-        fine = doubled(turn(step + middle, waves, length, inverse), hop(hops), LANES // 8)
-        fine_ref[g, t] = jnp.concatenate(
-            [jnp.concatenate([e[p] for e in fine], axis=0) for p in range(2)], axis=1
-        ).astype(BF16)
-        start = turn(step * float(LANES) + float(LANES // 2), waves, length, inverse)
-        half = coarse // 2
-        wide = doubled(start, hop(far), -(-half // 8))
-        wide = [jnp.concatenate([e[p] for e in wide], axis=0)[:half] for p in range(2)]
+        hops = turn(hop_step, waves, length, inverse)
+        fine = doubled(turn(near_step, waves, length, inverse), hops, LANES // 8)
+        fine_ref[g, t] = jnp.concatenate(fine, axis=1).astype(BF16)
+        wide = doubled(
+            turn(far_step, waves, length, inverse), tuple(x[4:] for x in hops), -(-half // 8)
+        )
         coarse_ref[g, t] = jnp.concatenate(
-            [jnp.concatenate([part] * levels, axis=0) for part in wide], axis=1
+            [jnp.concatenate([part[:half]] * levels, axis=0) for part in wide], axis=1
         )
+
+    def looped(index, _):
+        table(index // tiles, lax.rem(index, tiles), *circle(index // tiles))
         return 0
 
-    lax.fori_loop(0, circles * tiles, one, 0, unroll=2)
-
-    copies[0].wait()
+    place = lax.broadcasted_iota(jnp.int32, (8, blocks), 1)
+    begin = jnp.zeros((8, blocks), jnp.int32)
+    for g in range(1, circles):
+        begin = jnp.where(place >= g * coarse, g * coarse, begin)
+    place = place - begin
+    wanted = begin + jnp.where(place < half, place + half, coarse - 1 - place)
+    source = lax.broadcasted_iota(jnp.int32, (blocks, blocks), 0)
+    donor = donor_ref[...]
+    listed = jnp.concatenate(
+        [donor & 15, donor >> 4, tile_ref[...], jnp.zeros((2, blocks), jnp.int32)], axis=0
+    )
+    listed = jnp.dot(
+        listed.astype(F32).astype(BF16), one_hot(source == wanted[0:1]), preferred_element_type=F32
+    )
+    columns = jnp.transpose(listed)
+    own = side_by_side(field_ref)
+    kinds = kernels_ref.shape[0]
+    count = choice_ref.shape[1] // kinds
+    lane = lax.broadcasted_iota(jnp.int32, (blocks, blocks), 1).astype(F32)
+    entry = lax.broadcasted_iota(jnp.int32, choice_ref.shape, 1).astype(F32)
+    choice, picked, kind = None, [], []
+    for k in range(2):
+        donor = columns[:, k : k + 1] + 16.0 * columns[:, 2 + k : 3 + k]
+        tile = columns[:, 4 + k : 5 + k]
+        code = jnp.where(donor >= float(blocks), donor - float(blocks) + float(count) * tile, -1.0)
+        chosen = jnp.where(entry == code, 1.0, 0.0)
+        choice = chosen if k == 0 else choice + chosen
+        picked.append(
+            jnp.dot(one_hot(lane == donor), own, preferred_element_type=F32).astype(BF16)
+        )
+        kind.append(jnp.broadcast_to(tile, (blocks, LANES)))
+    choice_ref[...] = choice.astype(BF16)
+
+    unrolled = circles * tiles <= 64
+    if unrolled:
+        for g in range(circles):
+            for t in range(tiles):
+                table(g, t, *circle(g))
+    else:
+        lax.fori_loop(0, circles * tiles, looped, 0, unroll=2)
+
+    for copy in copies:
+        copy.wait()
+    stacked = jnp.concatenate([kernels_ref[k] for k in range(kinds)], axis=1)
+    for l in range(levels):
+        total = None
+        for k in range(2):
+            every = jnp.dot(
+                picked[k][:, l * LANES : (l + 1) * LANES], stacked, preferred_element_type=F32
+            )
+            value = every[:, :LANES]
+            for q in range(1, kinds):
+                value = jnp.where(kind[k] == float(q), every[:, q * LANES : (q + 1) * LANES], value)
+            total = value if k == 0 else total + value
+        arrival_ref[l] = total
+
+
     slots = limits_ref.shape[0]
     first = (lax.axis_index("lat") * lev + lax.axis_index("lev")) * slots
     for s in range(slots):
         limits_ref[s : s + 1] = jnp.full((1, LANES), slot_ref[first + s], jnp.int32)
 
-    copies[1].wait()
-    copies[2].wait()
-    copies[3].wait()
-    donor, kind = donor_ref[...], tile_ref[...]
-    listed = jnp.concatenate(
-        [donor & 15, donor >> 4, kind, jnp.zeros((2, blocks), jnp.int32)], axis=0
-    )
-    source = lax.broadcasted_iota(jnp.int32, (blocks, blocks), 0)
-    place = lax.broadcasted_iota(jnp.int32, (blocks, blocks), 1)
-    begin = jnp.zeros((blocks, blocks), jnp.int32)
-    for g in range(1, circles):
-        begin = jnp.where(place >= g * coarse, g * coarse, begin)
-    place = place - begin
-    half = coarse // 2
-    wanted = begin + jnp.where(place < half, place + half, coarse - 1 - place)
-    listed = jnp.dot(
-        listed.astype(F32).astype(BF16), one_hot(source == wanted), preferred_element_type=F32
-    )
-    columns = jnp.transpose(listed)
-    own = side_by_side(field_ref)
-    kinds = kernels_ref.shape[0]
-    count = choice_ref.shape[1] // kinds
-    stacked = jnp.concatenate([kernels_ref[k] for k in range(kinds)], axis=1)
-    lane = lax.broadcasted_iota(jnp.int32, (blocks, blocks), 1).astype(F32)
-    entry = lax.broadcasted_iota(jnp.int32, choice_ref.shape, 1).astype(F32)
-    arrival = [jnp.zeros((blocks, LANES), F32) for _ in range(levels)]
-    choice = jnp.zeros(choice_ref.shape, F32)
-    for k in range(2):
-        donor = columns[:, k : k + 1] + 16.0 * columns[:, 2 + k : 3 + k]
-        kind = columns[:, 4 + k : 5 + k]
-        code = jnp.where(donor >= float(blocks), donor - float(blocks) + float(count) * kind, -1.0)
-        choice = choice + jnp.where(entry == code, 1.0, 0.0)
-        picked = jnp.dot(one_hot(lane == donor), own, preferred_element_type=F32).astype(BF16)
-        kind = jnp.broadcast_to(kind, (blocks, LANES))
-        for l in range(levels):
-            every = jnp.dot(
-                picked[:, l * LANES : (l + 1) * LANES], stacked, preferred_element_type=F32
-            )
-            value = every[:, :LANES]
-            for q in range(1, kinds):
-                value = jnp.where(kind == float(q), every[:, q * LANES : (q + 1) * LANES], value)
-            arrival[l] = arrival[l] + value
-    choice_ref[...] = choice.astype(BF16)
-    for l in range(levels):
-        arrival_ref[l] = arrival[l]
-
     total = order_ref.shape[0]
     if total == lat * lev * 2 * circles:
+        at = lax.broadcasted_iota(jnp.int32, (8, total), 1)
+        outer = (at >> log(circles)) & (lat - 1)
+        group = at >> log(lat * circles)
+        source = (outer << log(circles * 2 * lev)) | (group << log(circles)) | (at & (circles - 1))
         row = lax.broadcasted_iota(jnp.int32, (total, total), 0)
-        col = lax.broadcasted_iota(jnp.int32, (total, total), 1)
-        group = (row >> log(circles)) & (2 * lev - 1)
-        outer = row >> log(circles * 2 * lev)
-        target = (group << log(lat * circles)) | (outer << log(circles)) | (row & (circles - 1))
-        order_ref[...] = one_hot(col == target)
+        order_ref[...] = one_hot(row == source[0:1])
     else:
         order_ref[...] = jnp.zeros(order_ref.shape, BF16)
-    copies[4].wait()
 
 
 def fold(parts):
@@ -235,19 +241,25 @@
     far = jnp.where(at_end, jnp.zeros_like(far), far)
     halo = jnp.concatenate([jnp.where(even, far, near), jnp.where(even, near, far)], axis=0)
     stacked = jnp.concatenate([kernels_ref[k] for k in range(kinds)], axis=1)
-    high, low = [], []
-    for l in range(levels):
-        every = jnp.dot(
-            halo[:, l * LANES : (l + 1) * LANES], stacked, preferred_element_type=F32
-        )
-        every = jnp.concatenate(
-            [every[:, q * LANES : (q + 1) * LANES] for q in range(kinds)], axis=0
-        )
-        high.append(every.astype(BF16))
-        low.append((every - high[-1].astype(F32)).astype(BF16))
-    arrival = jnp.dot(
-        choice_ref[...], jnp.concatenate(high, axis=1), preferred_element_type=F32
-    ) + jnp.dot(choice_ref[...], jnp.concatenate(low, axis=1), preferred_element_type=F32)
+    rows = jnp.concatenate(
+        [halo[:, l * LANES : (l + 1) * LANES] for l in range(levels)], axis=0
+    )
+    every = jnp.dot(rows, stacked, preferred_element_type=F32)
+    count = halo.shape[0]
+    every = jnp.concatenate(
+        [
+            jnp.concatenate(
+                [every[l * count : (l + 1) * count, q * LANES : (q + 1) * LANES] for q in range(kinds)],
+                axis=0,
+            )
+            for l in range(levels)
+        ],
+        axis=1,
+    )
+    high = every.astype(BF16)
+    low = (every - high.astype(F32)).astype(BF16)
+    arrival = jnp.dot(choice_ref[...], high, preferred_element_type=F32)
+    arrival = arrival + jnp.dot(choice_ref[...], low, preferred_element_type=F32)
 
     distance = lax.broadcasted_iota(jnp.int32, (coarse, LANES), 0)
     row = jnp.where(distance < half, distance + half, coarse - 1 - distance)
@@ -420,19 +432,21 @@
         return pltpu.with_memory_space_constraint(x, pltpu.HBM)
 
     halo = jax.ShapeDtypeStruct((send_count, levels * LANES), BF16)
-    to_far, to_near, field, lengths, waves = pl.pallas_call(
+    donors, kinds = donor_index.T, tile_choice.T
+    to_far, to_near, field, lengths, waves, donors, kinds = pl.pallas_call(
         outgoing_kernel,
         out_shape=(
-            halo, halo, like(grid_field), jax.ShapeDtypeStruct((2 * own, LANES), jnp.int32), like(waves)
+            halo, halo, like(grid_field), jax.ShapeDtypeStruct((2 * own, LANES), jnp.int32),
+            like(waves), like(donors), like(kinds),
         ),
-        in_specs=[HBM] * 4, out_specs=(VMEM,) * 5,
+        in_specs=[HBM] * 6, out_specs=(VMEM,) * 7,
         scratch_shapes=[
             pltpu.VMEM(send_blocks.shape, jnp.int32),
             pltpu.SMEM(circle_len.shape, jnp.int32),
-            pltpu.SemaphoreType.DMA((4,)),
+            pltpu.SemaphoreType.DMA((6,)),
         ],
         compiler_params=params(4), name="outgoing",
-    )(*map(in_hbm, (send_blocks, grid_field, circle_len, waves)))
+    )(*map(in_hbm, (send_blocks, grid_field, circle_len, waves, donors, kinds)))
     near = lax.ppermute(to_near, "lat", [(i, i ^ 1) for i in range(lat)])
     far = lax.ppermute(to_far, ("lat", "lev"), other_neighbours(lat, lev))
 
@@ -440,8 +454,7 @@
     direct = direct and 2 * slots <= LANES and lev & (lev - 1) == 0
     total = devices * 2 * own if direct else 16
     entries = own * tiles * (LANES + coarse) * 2 * LANES
-    donors, kinds = donor_index.T, tile_choice.T
-    fine, wide, limits, choice, own_part, kernels, functions, order = pl.pallas_call(
+    fine, wide, limits, choice, own_part, kernels, order = pl.pallas_call(
         functools.partial(table_kernel, lat=lat, lev=lev),
         out_shape=(
             jax.ShapeDtypeStruct((own, tiles, LANES, 2 * LANES), BF16),
@@ -450,19 +463,16 @@
             jax.ShapeDtypeStruct((blocks, kernel_tiles.shape[0] * 2 * send_count), BF16),
             jax.ShapeDtypeStruct((levels, blocks, LANES), F32),
             like(kernel_tiles),
-            like(legendre),
             jax.ShapeDtypeStruct((total, total), BF16),
         ),
-        in_specs=[VMEM] * 3 + [HBM] * 5, out_specs=(VMEM,) * 8,
+        in_specs=[VMEM] * 5 + [HBM] * 2, out_specs=(VMEM,) * 7,
         scratch_shapes=[
             pltpu.SMEM(slot_wave.shape, jnp.int32),
-            pltpu.VMEM(donors.shape, jnp.int32),
-            pltpu.VMEM(donors.shape, jnp.int32),
-            pltpu.SemaphoreType.DMA((5,)),
+            pltpu.SemaphoreType.DMA((2,)),
         ],
         compiler_params=params(32), name="tables",
         cost_estimate=pl.CostEstimate(flops=8 * entries, bytes_accessed=3 * entries, transcendentals=0),
-    )(lengths, waves, field, *map(in_hbm, (slot_wave, donors, kinds, kernel_tiles, legendre)))
+    )(lengths, waves, field, donors, kinds, *map(in_hbm, (slot_wave, kernel_tiles)))
 
     rows = levels * 2 * own
     packs = 1
@@ -496,14 +506,14 @@
             limits,
             arrived.reshape(devices * height, LANES),
             order,
-            functions.reshape(slots * circles, top_wave),
+            legendre.reshape(slots * circles, top_wave),
         )
         return spectra.reshape(outputs // 2, 2, slots, top_wave)
 
     gathered = arrived.reshape(lat, lev, height, packs, LANES // packs)[..., :slots]
     gathered = gathered.swapaxes(2, 3).reshape(lat, lev, levels, 2, own, slots)
     gathered = gathered.transpose(1, 2, 3, 0, 4, 5).reshape(outputs // 2, 2, circles, slots)
-    spectra = jnp.einsum("lcgs,sgn->lcsn", gathered, functions, preferred_element_type=F32)
+    spectra = jnp.einsum("lcgs,sgn->lcsn", gathered, legendre, preferred_element_type=F32)
     first_slot = (lax.axis_index("lat") * lev + lax.axis_index("lev")) * slots
     mine = lax.dynamic_slice_in_dim(slot_wave, first_slot, slots)
     allowed = jnp.arange(top_wave, dtype=jnp.int32)[None, :] >= mine[:, None]

time: 24 us -> 23.2 us (0.967)
  Pallas kernels: 7.32 us -> 6.49 us
    pallas_call x1, Pallas kernels: 3.24 us -> 2.4 us  [body(): pl.pallas_call(functools.partial(table_kernel, lat=lat, lev=lev), out_sha...]
  transfers between devices with their start and end apart: 2 -> 2, of which waited for: 0 -> 0; matrix products, arithmetic and copies ran while one was open for 0% -> 0% of each run, Pallas kernels for 14% -> 10%
where the time goes in v6:
time: 23.2 us; the launch traced here: 23 us
  blocking collectives  11.9 us (51%)
  Pallas kernels  6.49 us (28%)
  starting transfers between devices  4.55 us (20%)
    all_to_all x1, blocking collectives, body(): arrived = lax.all_to_all(coeffs, ('lat', 'lev'), 0, 0, tiled=True)  11.9 us
    ppermute x1, starting transfers between devices, body(): near = lax.ppermute(to_near, 'lat', [(i, i ^ 1) for i in range(lat)])  4.03 us
    pallas_call x1, Pallas kernels, body(): pl.pallas_call(functools.partial(table_kernel, lat=lat, lev=lev), out_sha...  2.4 us
    pallas_call x1, Pallas kernels, body(): pl.pallas_call(functools.partial(legendre_kernel, packs=packs), out_shape...  1.69 us
    pallas_call x1, Pallas kernels, body(): pl.pallas_call(functools.partial(transform_kernel, top_wave=top_wave), ou...  1.22 us
    pallas_call x1, Pallas kernels, body(): pl.pallas_call(outgoing_kernel, out_shape=(halo, halo, like(grid_field),...  1.17 us
    ppermute x1, starting transfers between devices, body(): far = lax.ppermute(to_far, ('lat', 'lev'), other_neighbours(lat, lev))  0.52 us
  transfers between devices with their start and end apart: 2, of which 0 were waited for; matrix products, arithmetic and copies ran while one was open for 0% of the time, Pallas kernels for 10%

profile of v6, /device:TPU:0, one launch (start us, length us, event | category | flops | bytes accessed | tf_op | source)
XLA Modules:
  0.0 23.0 jit_solution(11319437525233179594)
XLA Ops:
  0.0 1.2 %outgoing.1 = (bf16[32,256]{1,0:T(8,128)(2,1)S(1)}, bf16[32,256]{1,0:T(8,128)(2,1)S(1)}, bf16[2,160,128]{2,1,0:T(8,128)(2,1)S(1)}, s32[8,128]{1,0:T(8,128)S(1)},...) custom-call(s32[1,2,32]{2,1,0:T(2,128)} %send_hbm.1, bf16[2,160,128]{2,1,0:T(8,128)(2,1)} %field_hbm.1, ...), custom_call_target="tpu_custom_call" | custom-call | tf_op jit(solution)/shard_map/outgoing/pallas_call | solution.py:436
  1.2 0.5 %collective-permute-start = (bf16[32,256]{1,0:T(8,128)(2,1)S(1)}, bf16[32,256]{1,0:T(8,128)(2,1)S(1)}, u32[]{:S(2)}, u32[]{:S(2)}) collective-permute-start(bf16[32,256]{1,0:T(8,128)(2,1)S(1)} %get-tuple-element.25), channel_id=1, source_target_pairs={{4,8},{5,9},{6,10},{7,11},{12,16},{13,17},{14,18},{15,19},{20,24},... | collective-permute-start | bytes 49160 | tf_op jit(solution)/shard_map/ppermute | solution.py:451
  1.7 4.0 %collective-permute-start.1 = (bf16[32,256]{1,0:T(8,128)(2,1)S(1)}, bf16[32,256]{1,0:T(8,128)(2,1)S(1)}, u32[]{:S(2)}, u32[]{:S(2)}) collective-permute-start(bf16[32,256]{1,0:T(8,128)(2,1)S(1)} %get-tuple-element.26), channel_id=1, source_target_pairs={{0,4},{4,0},{8,12},{12,8},{16,20},{20,16},{24,28},{28,24},{1,5},{5... | collective-permute-start | bytes 49160 | tf_op jit(solution)/shard_map/ppermute | solution.py:450
  5.7 2.4 %tables.1 = (bf16[4,10,128,256]{3,2,1,0:T(8,128)(2,1)S(1)}, f32[4,10,40,256]{3,2,1,0:T(8,128)S(1)}, s32[40,128]{1,0:T(8,128)S(1)}, bf16[160,512]{1,0:T(8,128)(2,...) custom-call(s32[8,128]{1,0:T(8,128)S(1)} %get-tuple-element.19.lengths_ref, ...), custom_call_target="tpu_custom_call" | custom-call | flops 13762560 | bytes 5160960 | tf_op jit(solution)/shard_map/tables/pallas_call | solution.py:457
  8.1 0.0 copy-start
  8.2 0.0 collective-permute-done.far_ref
  8.2 0.0 collective-permute-done.1.near_ref
  8.2 1.2 %transform.1 = bf16[32,8,128]{2,1,0:T(8,128)(2,1)S(1)} custom-call(s32[8,128]{1,0:T(8,128)S(1)} %get-tuple-element.19.lengths_ref, s32[10,128]{1,0:T(8,128)S(1)} %get-tuple-element.20.wave_ref, bf16[32,256]{1,0:T(8,128)(2,1)S(1)} %collective-permute-done.far_ref, bf16[32,256]{1,0:T(8,128)(2,1)S(1)} %collective-permute-done.1.near_ref, ...), custom_call_target="tpu_custom_call" | custom-call | tf_op jit(solution)/shard_map/transform/pallas_call | solution.py:481
  9.4 11.9 %all_to_all.5 = bf16[32,8,128]{2,1,0:T(8,128)(2,1)S(1)} all-to-all(bf16[32,8,128]{2,1,0:T(8,128)(2,1)S(1)} %transform.1), channel_id=1, replica_groups=mesh['lat'=8,'lev'=4] {'lat','lev'}, dimensions={0} | all-to-all | bytes 131072 | tf_op jit(solution)/shard_map/all_to_all | solution.py:491
  21.4 0.0 copy-done
  21.4 1.7 %legendre.1 = bf16[16,40,1280]{2,1,0:T(8,128)(2,1)} custom-call(s32[40,128]{1,0:T(8,128)S(1)} %get-tuple-element.24.limits_ref, bf16[256,128]{1,0:T(8,128)(2,1)S(1)} %bitcast.7, bf16[256,256]{1,0:T(8,128)(2,1)S(1)} %get-tuple-element.32.order_ref, bf16[1280,1280]{1,0:T(8,128)(2,1)S(1)} %bitcast.6), custom_call_target="tpu_custom_call" | custom-call | tf_op jit(solution)/shard_map/legendre/pallas_call | solution.py:496
Async XLA Ops:
  1.2 7.0 %collective-permute-start = (bf16[32,256]{1,0:T(8,128)(2,1)S(1)}, bf16[32,256]{1,0:T(8,128)(2,1)S(1)}, u32[]{:S(2)}, u32[]{:S(2)}) collective-permute-start(bf16[32,256]{1,0:T(8,128)(2,1)S(1)} %get-tuple-element.25), channel_id=1, source_target_pairs={{4,8},{5,9},{6,10},{7,11},{12,16},{13,17},{14,18},{15,19},{20,24},... | collective-permute-start | bytes 49160 | tf_op jit(solution)/shard_map/ppermute | solution.py:451
  1.7 6.5 %collective-permute-start.1 = (bf16[32,256]{1,0:T(8,128)(2,1)S(1)}, bf16[32,256]{1,0:T(8,128)(2,1)S(1)}, u32[]{:S(2)}, u32[]{:S(2)}) collective-permute-start(bf16[32,256]{1,0:T(8,128)(2,1)S(1)} %get-tuple-element.26), channel_id=1, source_target_pairs={{0,4},{4,0},{8,12},{12,8},{16,20},{20,16},{24,28},{28,24},{1,5},{5... | collective-permute-start | bytes 49160 | tf_op jit(solution)/shard_map/ppermute | solution.py:450
  8.1 13.2 %copy-start = (bf16[40,32,1280]{2,1,0:T(8,128)(2,1)S(1)}, bf16[40,32,1280]{2,1,0:T(8,128)(2,1)}, u32[]{:S(2)}) copy-start(bf16[40,32,1280]{2,1,0:T(8,128)(2,1)} %param.15) | copy-start | bytes 9830404

commit v7 on v6

--- a/solution.py
+++ b/solution.py
@@ -30,13 +30,13 @@
 
 
 def outgoing_kernel(
-    send_hbm, field_hbm, length_hbm, wave_hbm, donor_hbm, tile_hbm,
-    far_ref, near_ref, field_ref, lengths_ref, wave_ref, donor_ref, tile_ref,
+    send_hbm, field_hbm, length_hbm, wave_hbm, donor_hbm, tile_hbm, kernels_hbm,
+    far_ref, near_ref, field_ref, lengths_ref, wave_ref, donor_ref, tile_ref, kernels_ref,
     send_ref, length_ref, sems,
 ):
     pairs = (
         (send_hbm, send_ref), (field_hbm, field_ref), (length_hbm, length_ref), (wave_hbm, wave_ref),
-        (donor_hbm, donor_ref), (tile_hbm, tile_ref),
+        (donor_hbm, donor_ref), (tile_hbm, tile_ref), (kernels_hbm, kernels_ref),
     )
     copies = [pltpu.make_async_copy(*pair, sems.at[i]) for i, pair in enumerate(pairs)]
     for copy in copies:
@@ -92,19 +92,43 @@
     return a[0] * b[0] - a[1] * b[1], a[0] * b[1] + a[1] * b[0]
 
 
+def folded_order(array, coarse):
+    half, count = coarse // 2, coarse // 8
+    assert coarse % 8 == 0 and half % 8 == 4
+    sub = lax.broadcasted_iota(jnp.int32, (8, array.shape[1]), 0)
+
+    def reverse(v):
+        v = pltpu.roll(v, 4, 0)
+        for h in (2, 1):
+            v = jnp.where((sub & h) == 0, pltpu.roll(v, 8 - h, 0), pltpu.roll(v, h, 0))
+        return v
+
+    out = []
+    for begin in range(0, array.shape[0], coarse):
+        rows = [array[begin + 8 * i : begin + 8 * i + 8] for i in range(count)]
+        swapped = {i: pltpu.roll(rows[i], 4, 0) for i in range(half // 8, count)}
+        for i in range(count):
+            q = (8 * i + half) // 8
+            if 8 * i + 8 <= half:
+                out.append(jnp.where(sub < 4, swapped[q], swapped[q + 1]))
+            elif 8 * i < half:
+                out.append(jnp.where(sub < 4, swapped[q], reverse(rows[count - 1 - i])))
+            else:
+                out.append(reverse(rows[count - 1 - i]))
+    return jnp.concatenate(out, axis=0)
+
+
 def table_kernel(
-    lengths_ref, wave_ref, field_ref, donor_ref, tile_ref, slot_hbm, kernels_hbm,
-    fine_ref, coarse_ref, limits_ref, choice_ref, arrival_ref, kernels_ref, order_ref,
-    slot_ref, sems, *, lat, lev,
+    lengths_ref, wave_ref, field_ref, donor_ref, tile_ref, kernels_ref, slot_hbm,
+    fine_ref, coarse_ref, limits_ref, choice_ref, arrival_ref, order_ref,
+    slot_ref, sem, *, lat, lev,
 ):
     circles, tiles = fine_ref.shape[:2]
     levels, blocks, _ = field_ref.shape
     coarse = blocks // circles
     half = coarse // 2
-    pairs = ((slot_hbm, slot_ref), (kernels_hbm, kernels_ref))
-    copies = [pltpu.make_async_copy(*pair, sems.at[i]) for i, pair in enumerate(pairs)]
-    for copy in copies:
-        copy.start()
+    fetch = pltpu.make_async_copy(slot_hbm, slot_ref, sem)
+    fetch.start()
     row = lax.broadcasted_iota(jnp.int32, (8, LANES), 0)
     near_step = (row + LANES // 2 * (coarse - 1)).astype(F32)
     far_step = (row * LANES + LANES // 2).astype(F32)
@@ -138,21 +162,10 @@
         table(index // tiles, lax.rem(index, tiles), *circle(index // tiles))
         return 0
 
-    place = lax.broadcasted_iota(jnp.int32, (8, blocks), 1)
-    begin = jnp.zeros((8, blocks), jnp.int32)
-    for g in range(1, circles):
-        begin = jnp.where(place >= g * coarse, g * coarse, begin)
-    place = place - begin
-    wanted = begin + jnp.where(place < half, place + half, coarse - 1 - place)
-    source = lax.broadcasted_iota(jnp.int32, (blocks, blocks), 0)
-    donor = donor_ref[...]
     listed = jnp.concatenate(
-        [donor & 15, donor >> 4, tile_ref[...], jnp.zeros((2, blocks), jnp.int32)], axis=0
-    )
-    listed = jnp.dot(
-        listed.astype(F32).astype(BF16), one_hot(source == wanted[0:1]), preferred_element_type=F32
-    )
-    columns = jnp.transpose(listed)
+        [donor_ref[...], tile_ref[...], jnp.zeros((4, blocks), jnp.int32)], axis=0
+    )
+    columns = folded_order(jnp.transpose(listed.astype(F32)), coarse)
     own = side_by_side(field_ref)
     kinds = kernels_ref.shape[0]
     count = choice_ref.shape[1] // kinds
@@ -160,8 +173,8 @@
     entry = lax.broadcasted_iota(jnp.int32, choice_ref.shape, 1).astype(F32)
     choice, picked, kind = None, [], []
     for k in range(2):
-        donor = columns[:, k : k + 1] + 16.0 * columns[:, 2 + k : 3 + k]
-        tile = columns[:, 4 + k : 5 + k]
+        donor = columns[:, k : k + 1]
+        tile = columns[:, 2 + k : 3 + k]
         code = jnp.where(donor >= float(blocks), donor - float(blocks) + float(count) * tile, -1.0)
         chosen = jnp.where(entry == code, 1.0, 0.0)
         choice = chosen if k == 0 else choice + chosen
@@ -171,16 +184,6 @@
         kind.append(jnp.broadcast_to(tile, (blocks, LANES)))
     choice_ref[...] = choice.astype(BF16)
 
-    unrolled = circles * tiles <= 64
-    if unrolled:
-        for g in range(circles):
-            for t in range(tiles):
-                table(g, t, *circle(g))
-    else:
-        lax.fori_loop(0, circles * tiles, looped, 0, unroll=2)
-
-    for copy in copies:
-        copy.wait()
     stacked = jnp.concatenate([kernels_ref[k] for k in range(kinds)], axis=1)
     for l in range(levels):
         total = None
@@ -194,7 +197,15 @@
             total = value if k == 0 else total + value
         arrival_ref[l] = total
 
-
+    unrolled = circles * tiles <= 64
+    if unrolled:
+        for g in range(circles):
+            for t in range(tiles):
+                table(g, t, *circle(g))
+    else:
+        lax.fori_loop(0, circles * tiles, looped, 0, unroll=2)
+
+    fetch.wait()
     slots = limits_ref.shape[0]
     first = (lax.axis_index("lat") * lev + lax.axis_index("lev")) * slots
     for s in range(slots):
@@ -433,20 +444,22 @@
 
     halo = jax.ShapeDtypeStruct((send_count, levels * LANES), BF16)
     donors, kinds = donor_index.T, tile_choice.T
-    to_far, to_near, field, lengths, waves, donors, kinds = pl.pallas_call(
+    to_far, to_near, field, lengths, waves, donors, kinds, kernels = pl.pallas_call(
         outgoing_kernel,
         out_shape=(
             halo, halo, like(grid_field), jax.ShapeDtypeStruct((2 * own, LANES), jnp.int32),
-            like(waves), like(donors), like(kinds),
+            like(waves), like(donors), like(kinds), like(kernel_tiles),
         ),
-        in_specs=[HBM] * 6, out_specs=(VMEM,) * 7,
+        in_specs=[HBM] * 7, out_specs=(VMEM,) * 8,
         scratch_shapes=[
             pltpu.VMEM(send_blocks.shape, jnp.int32),
             pltpu.SMEM(circle_len.shape, jnp.int32),
-            pltpu.SemaphoreType.DMA((6,)),
+            pltpu.SemaphoreType.DMA((7,)),
         ],
         compiler_params=params(4), name="outgoing",
-    )(*map(in_hbm, (send_blocks, grid_field, circle_len, waves, donors, kinds)))
+    )(
+        *map(in_hbm, (send_blocks, grid_field, circle_len, waves, donors, kinds, kernel_tiles))
+    )
     near = lax.ppermute(to_near, "lat", [(i, i ^ 1) for i in range(lat)])
     far = lax.ppermute(to_far, ("lat", "lev"), other_neighbours(lat, lev))
 
@@ -454,7 +467,7 @@
     direct = direct and 2 * slots <= LANES and lev & (lev - 1) == 0
     total = devices * 2 * own if direct else 16
     entries = own * tiles * (LANES + coarse) * 2 * LANES
-    fine, wide, limits, choice, own_part, kernels, order = pl.pallas_call(
+    fine, wide, limits, choice, own_part, order = pl.pallas_call(
         functools.partial(table_kernel, lat=lat, lev=lev),
         out_shape=(
             jax.ShapeDtypeStruct((own, tiles, LANES, 2 * LANES), BF16),
@@ -462,17 +475,16 @@
             jax.ShapeDtypeStruct((slots, LANES), jnp.int32),
             jax.ShapeDtypeStruct((blocks, kernel_tiles.shape[0] * 2 * send_count), BF16),
             jax.ShapeDtypeStruct((levels, blocks, LANES), F32),
-            like(kernel_tiles),
             jax.ShapeDtypeStruct((total, total), BF16),
         ),
-        in_specs=[VMEM] * 5 + [HBM] * 2, out_specs=(VMEM,) * 7,
+        in_specs=[VMEM] * 6 + [HBM], out_specs=(VMEM,) * 6,
         scratch_shapes=[
             pltpu.SMEM(slot_wave.shape, jnp.int32),
-            pltpu.SemaphoreType.DMA((2,)),
+            pltpu.SemaphoreType.DMA,
         ],
         compiler_params=params(32), name="tables",
         cost_estimate=pl.CostEstimate(flops=8 * entries, bytes_accessed=3 * entries, transcendentals=0),
-    )(lengths, waves, field, donors, kinds, *map(in_hbm, (slot_wave, kernel_tiles)))
+    )(lengths, waves, field, donors, kinds, kernels, in_hbm(slot_wave))
 
     rows = levels * 2 * own
     packs = 1

time: 23.2 us -> 23.1 us (level)
  Pallas kernels: 6.49 us -> 6.02 us
  blocking collectives: 11.9 us -> 12.3 us
    pallas_call x1, Pallas kernels: 2.4 us -> 1.93 us  [body(): pl.pallas_call(functools.partial(table_kernel, lat=lat, lev=lev), out_sha...]
    all_to_all x1, blocking collectives: 11.9 us -> 12.3 us  [body(): arrived = lax.all_to_all(coeffs, ('lat', 'lev'), 0, 0, tiled=True)]
  transfers between devices with their start and end apart: 2 -> 2, of which waited for: 0 -> 0; matrix products, arithmetic and copies ran while one was open for 0% -> 0% of each run, Pallas kernels for 10% -> 8%
where the time goes in v7:
time: 23.1 us; the launch traced here: 23 us
  blocking collectives  12.3 us (53%)
  Pallas kernels  6.02 us (26%)
  starting transfers between devices  4.55 us (20%)
    all_to_all x1, blocking collectives, body(): arrived = lax.all_to_all(coeffs, ('lat', 'lev'), 0, 0, tiled=True)  12.3 us
    ppermute x1, starting transfers between devices, body(): near = lax.ppermute(to_near, 'lat', [(i, i ^ 1) for i in range(lat)])  4.03 us
    pallas_call x1, Pallas kernels, body(): pl.pallas_call(functools.partial(table_kernel, lat=lat, lev=lev), out_sha...  1.93 us
    pallas_call x1, Pallas kernels, body(): pl.pallas_call(functools.partial(legendre_kernel, packs=packs), out_shape...  1.68 us
    pallas_call x1, Pallas kernels, body(): pl.pallas_call(functools.partial(transform_kernel, top_wave=top_wave), ou...  1.23 us
    pallas_call x1, Pallas kernels, body(): pl.pallas_call(outgoing_kernel, out_shape=(halo, halo, like(grid_field),...  1.18 us
    ppermute x1, starting transfers between devices, body(): far = lax.ppermute(to_far, ('lat', 'lev'), other_neighbours(lat, lev))  0.52 us
  transfers between devices with their start and end apart: 2, of which 0 were waited for; matrix products, arithmetic and copies ran while one was open for 0% of the time, Pallas kernels for 8%

profile of v7, /device:TPU:0, one launch (start us, length us, event | category | flops | bytes accessed | tf_op | source)
XLA Modules:
  0.0 23.0 jit_solution(18185776971717551362)
XLA Ops:
  0.0 1.2 %outgoing.1 = (bf16[32,256]{1,0:T(8,128)(2,1)S(1)}, bf16[32,256]{1,0:T(8,128)(2,1)S(1)}, bf16[2,160,128]{2,1,0:T(8,128)(2,1)S(1)}, s32[8,128]{1,0:T(8,128)S(1)},...) custom-call(s32[1,2,32]{2,1,0:T(2,128)} %send_hbm.1, ...), custom_call_target="tpu_custom_call" | custom-call | tf_op jit(solution)/shard_map/outgoing/pallas_call | solution.py:447
  1.2 0.5 %collective-permute-start = (bf16[32,256]{1,0:T(8,128)(2,1)S(1)}, bf16[32,256]{1,0:T(8,128)(2,1)S(1)}, u32[]{:S(2)}, u32[]{:S(2)}) collective-permute-start(bf16[32,256]{1,0:T(8,128)(2,1)S(1)} %get-tuple-element.26), channel_id=1, source_target_pairs={{4,8},{5,9},{6,10},{7,11},{12,16},{13,17},{14,18},{15,19},{20,24},... | collective-permute-start | bytes 49160 | tf_op jit(solution)/shard_map/ppermute | solution.py:464
  1.7 4.0 %collective-permute-start.1 = (bf16[32,256]{1,0:T(8,128)(2,1)S(1)}, bf16[32,256]{1,0:T(8,128)(2,1)S(1)}, u32[]{:S(2)}, u32[]{:S(2)}) collective-permute-start(bf16[32,256]{1,0:T(8,128)(2,1)S(1)} %get-tuple-element.27), channel_id=1, source_target_pairs={{0,4},{4,0},{8,12},{12,8},{16,20},{20,16},{24,28},{28,24},{1,5},{5... | collective-permute-start | bytes 49160 | tf_op jit(solution)/shard_map/ppermute | solution.py:463
  5.7 1.9 %tables.1 = (bf16[4,10,128,256]{3,2,1,0:T(8,128)(2,1)S(1)}, f32[4,10,40,256]{3,2,1,0:T(8,128)S(1)}, s32[40,128]{1,0:T(8,128)S(1)}, bf16[160,512]{1,0:T(8,128)(2,...) custom-call(s32[8,128]{1,0:T(8,128)S(1)} %get-tuple-element.19.lengths_ref, ...), custom_call_target="tpu_custom_call" | custom-call | flops 13762560 | bytes 5160960 | tf_op jit(solution)/shard_map/tables/pallas_call | solution.py:470
  7.7 0.0 copy-start
  7.7 0.0 collective-permute-done.far_ref
  7.7 0.0 collective-permute-done.1.near_ref
  7.7 1.2 %transform.1 = bf16[32,8,128]{2,1,0:T(8,128)(2,1)S(1)} custom-call(s32[8,128]{1,0:T(8,128)S(1)} %get-tuple-element.19.lengths_ref, s32[10,128]{1,0:T(8,128)S(1)} %get-tuple-element.20.wave_ref, bf16[32,256]{1,0:T(8,128)(2,1)S(1)} %collective-permute-done.far_ref, bf16[32,256]{1,0:T(8,128)(2,1)S(1)} %collective-permute-done.1.near_ref, ...), custom_call_target="tpu_custom_call" | custom-call | tf_op jit(solution)/shard_map/transform/pallas_call | solution.py:493
  8.9 12.3 %all_to_all.5 = bf16[32,8,128]{2,1,0:T(8,128)(2,1)S(1)} all-to-all(bf16[32,8,128]{2,1,0:T(8,128)(2,1)S(1)} %transform.1), channel_id=1, replica_groups=mesh['lat'=8,'lev'=4] {'lat','lev'}, dimensions={0} | all-to-all | bytes 131072 | tf_op jit(solution)/shard_map/all_to_all | solution.py:503
  21.3 0.0 copy-done
  21.3 1.7 %legendre.1 = bf16[16,40,1280]{2,1,0:T(8,128)(2,1)} custom-call(s32[40,128]{1,0:T(8,128)S(1)} %get-tuple-element.25.limits_ref, bf16[256,128]{1,0:T(8,128)(2,1)S(1)} %bitcast.7, bf16[256,256]{1,0:T(8,128)(2,1)S(1)} %get-tuple-element.32.order_ref, bf16[1280,1280]{1,0:T(8,128)(2,1)S(1)} %bitcast.6), custom_call_target="tpu_custom_call" | custom-call | tf_op jit(solution)/shard_map/legendre/pallas_call | solution.py:508
Async XLA Ops:
  1.2 6.5 %collective-permute-start = (bf16[32,256]{1,0:T(8,128)(2,1)S(1)}, bf16[32,256]{1,0:T(8,128)(2,1)S(1)}, u32[]{:S(2)}, u32[]{:S(2)}) collective-permute-start(bf16[32,256]{1,0:T(8,128)(2,1)S(1)} %get-tuple-element.26), channel_id=1, source_target_pairs={{4,8},{5,9},{6,10},{7,11},{12,16},{13,17},{14,18},{15,19},{20,24},... | collective-permute-start | bytes 49160 | tf_op jit(solution)/shard_map/ppermute | solution.py:464
  1.7 6.0 %collective-permute-start.1 = (bf16[32,256]{1,0:T(8,128)(2,1)S(1)}, bf16[32,256]{1,0:T(8,128)(2,1)S(1)}, u32[]{:S(2)}, u32[]{:S(2)}) collective-permute-start(bf16[32,256]{1,0:T(8,128)(2,1)S(1)} %get-tuple-element.27), channel_id=1, source_target_pairs={{0,4},{4,0},{8,12},{12,8},{16,20},{20,16},{24,28},{28,24},{1,5},{5... | collective-permute-start | bytes 49160 | tf_op jit(solution)/shard_map/ppermute | solution.py:463
  7.7 13.6 %copy-start = (bf16[40,32,1280]{2,1,0:T(8,128)(2,1)S(1)}, bf16[40,32,1280]{2,1,0:T(8,128)(2,1)}, u32[]{:S(2)}) copy-start(bf16[40,32,1280]{2,1,0:T(8,128)(2,1)} %param.15) | copy-start | bytes 9830404

commit v8 on v7

--- a/solution.py
+++ b/solution.py
@@ -120,7 +120,7 @@
 
 def table_kernel(
     lengths_ref, wave_ref, field_ref, donor_ref, tile_ref, kernels_ref, slot_hbm,
-    fine_ref, coarse_ref, limits_ref, choice_ref, arrival_ref, order_ref,
+    fine_ref, coarse_ref, limits_ref, far_choice_ref, near_choice_ref, arrival_ref, order_ref,
     slot_ref, sem, *, lat, lev,
 ):
     circles, tiles = fine_ref.shape[:2]
@@ -168,22 +168,27 @@
     columns = folded_order(jnp.transpose(listed.astype(F32)), coarse)
     own = side_by_side(field_ref)
     kinds = kernels_ref.shape[0]
-    count = choice_ref.shape[1] // kinds
+    count = far_choice_ref.shape[1] // kinds
+    even = lax.rem(lax.axis_index("lat"), 2) == 0
     lane = lax.broadcasted_iota(jnp.int32, (blocks, blocks), 1).astype(F32)
-    entry = lax.broadcasted_iota(jnp.int32, choice_ref.shape, 1).astype(F32)
-    choice, picked, kind = None, [], []
+    entry = lax.broadcasted_iota(jnp.int32, far_choice_ref.shape, 1).astype(F32)
+    far_choice, near_choice, picked, kind = [], [], [], []
     for k in range(2):
         donor = columns[:, k : k + 1]
         tile = columns[:, 2 + k : 3 + k]
-        code = jnp.where(donor >= float(blocks), donor - float(blocks) + float(count) * tile, -1.0)
-        chosen = jnp.where(entry == code, 1.0, 0.0)
-        choice = chosen if k == 0 else choice + chosen
+        place = donor - float(blocks)
+        above = place >= float(count)
+        code = jnp.where(above, place - float(count), place) + float(count) * tile
+        code = jnp.where(place >= 0.0, code, -1.0)
+        is_far = jnp.logical_xor(above, even)
+        far_choice.append(jnp.where(entry == jnp.where(is_far, code, -1.0), 1.0, 0.0))
+        near_choice.append(jnp.where(entry == jnp.where(is_far, -1.0, code), 1.0, 0.0))
         picked.append(
             jnp.dot(one_hot(lane == donor), own, preferred_element_type=F32).astype(BF16)
         )
         kind.append(jnp.broadcast_to(tile, (blocks, LANES)))
-    choice_ref[...] = choice.astype(BF16)
-
+    far_choice_ref[...] = (far_choice[0] + far_choice[1]).astype(BF16)
+    near_choice_ref[...] = (near_choice[0] + near_choice[1]).astype(BF16)
     stacked = jnp.concatenate([kernels_ref[k] for k in range(kinds)], axis=1)
     for l in range(levels):
         total = None
@@ -195,7 +200,7 @@
             for q in range(1, kinds):
                 value = jnp.where(kind[k] == float(q), every[:, q * LANES : (q + 1) * LANES], value)
             total = value if k == 0 else total + value
-        arrival_ref[l] = total
+        arrival_ref[:, l * LANES : (l + 1) * LANES] = total
 
     unrolled = circles * tiles <= 64
     if unrolled:
@@ -235,28 +240,14 @@
     return parts[0]
 
 
-def transform_kernel(
-    lengths_ref, wave_ref, far_ref, near_ref, choice_ref, arrival_ref, kernels_ref, fine_ref,
-    coarse_ref, out_ref, points_ref, coeff_ref, *, top_wave,
-):
-    levels, blocks, _ = arrival_ref.shape
-    circles, tiles = fine_ref.shape[:2]
-    coarse = blocks // circles
-    half = coarse // 2
+def from_halo(halo, kernels_ref, choice):
     kinds = kernels_ref.shape[0]
-    band = lax.axis_index("lat")
-    even = lax.rem(band, 2) == 0
-
-    near, far = near_ref[...], far_ref[...]
-    at_end = (band == 0) | (band == lax.axis_size("lat") - 1)
-    far = jnp.where(at_end, jnp.zeros_like(far), far)
-    halo = jnp.concatenate([jnp.where(even, far, near), jnp.where(even, near, far)], axis=0)
+    count, levels = halo.shape[0], halo.shape[1] // LANES
     stacked = jnp.concatenate([kernels_ref[k] for k in range(kinds)], axis=1)
     rows = jnp.concatenate(
         [halo[:, l * LANES : (l + 1) * LANES] for l in range(levels)], axis=0
     )
     every = jnp.dot(rows, stacked, preferred_element_type=F32)
-    count = halo.shape[0]
     every = jnp.concatenate(
         [
             jnp.concatenate(
@@ -269,8 +260,29 @@
     )
     high = every.astype(BF16)
     low = (every - high.astype(F32)).astype(BF16)
-    arrival = jnp.dot(choice_ref[...], high, preferred_element_type=F32)
-    arrival = arrival + jnp.dot(choice_ref[...], low, preferred_element_type=F32)
+    return jnp.dot(choice, high, preferred_element_type=F32) + jnp.dot(
+        choice, low, preferred_element_type=F32
+    )
+
+
+def far_kernel(far_ref, choice_ref, kernels_ref, own_ref, arrival_ref):
+    band = lax.axis_index("lat")
+    at_end = (band == 0) | (band == lax.axis_size("lat") - 1)
+    far = far_ref[...]
+    far = jnp.where(at_end, jnp.zeros_like(far), far)
+    arrival_ref[...] = own_ref[...] + from_halo(far, kernels_ref, choice_ref[...])
+
+
+def transform_kernel(
+    lengths_ref, wave_ref, near_ref, choice_ref, arrival_ref, kernels_ref, fine_ref,
+    coarse_ref, out_ref, points_ref, coeff_ref, *, top_wave,
+):
+    blocks = arrival_ref.shape[0]
+    levels = arrival_ref.shape[1] // LANES
+    circles, tiles = fine_ref.shape[:2]
+    coarse = blocks // circles
+    half = coarse // 2
+    arrival = arrival_ref[...] + from_halo(near_ref[...], kernels_ref, choice_ref[...])
 
     distance = lax.broadcasted_iota(jnp.int32, (coarse, LANES), 0)
     row = jnp.where(distance < half, distance + half, coarse - 1 - distance)
@@ -280,7 +292,7 @@
         sums, differences = [], []
         for l in range(levels):
             rows = slice(g * coarse, (g + 1) * coarse)
-            part = arrival[rows, l * LANES : (l + 1) * LANES] + arrival_ref[l, rows]
+            part = arrival[rows, l * LANES : (l + 1) * LANES]
             part = jnp.where(inside, part * part, 0.0)
             sums.append(part[:half] + part[half:])
             differences.append(part[:half] - part[half:])
@@ -467,17 +479,20 @@
     direct = direct and 2 * slots <= LANES and lev & (lev - 1) == 0
     total = devices * 2 * own if direct else 16
     entries = own * tiles * (LANES + coarse) * 2 * LANES
-    fine, wide, limits, choice, own_part, order = pl.pallas_call(
+    choice = jax.ShapeDtypeStruct((blocks, kernel_tiles.shape[0] * send_count), BF16)
+    arrival = jax.ShapeDtypeStruct((blocks, levels * LANES), F32)
+    fine, wide, limits, far_choice, near_choice, own_part, order = pl.pallas_call(
         functools.partial(table_kernel, lat=lat, lev=lev),
         out_shape=(
             jax.ShapeDtypeStruct((own, tiles, LANES, 2 * LANES), BF16),
             jax.ShapeDtypeStruct((own, tiles, levels * coarse // 2, 2 * LANES), F32),
             jax.ShapeDtypeStruct((slots, LANES), jnp.int32),
-            jax.ShapeDtypeStruct((blocks, kernel_tiles.shape[0] * 2 * send_count), BF16),
-            jax.ShapeDtypeStruct((levels, blocks, LANES), F32),
+            choice,
+            choice,
+            arrival,
             jax.ShapeDtypeStruct((total, total), BF16),
         ),
-        in_specs=[VMEM] * 6 + [HBM], out_specs=(VMEM,) * 6,
+        in_specs=[VMEM] * 6 + [HBM], out_specs=(VMEM,) * 7,
         scratch_shapes=[
             pltpu.SMEM(slot_wave.shape, jnp.int32),
             pltpu.SemaphoreType.DMA,
@@ -490,16 +505,20 @@
     packs = 1
     while rows % (16 * packs) == 0 and 2 * packs * slots <= LANES:
         packs *= 2
+    arrival = pl.pallas_call(
+        far_kernel, out_shape=arrival, in_specs=[VMEM] * 4, out_specs=VMEM,
+        compiler_params=params(8), name="far_part",
+    )(far, far_choice, kernels, own_part)
     coeffs = pl.pallas_call(
         functools.partial(transform_kernel, top_wave=top_wave),
         out_shape=jax.ShapeDtypeStruct((devices, rows // packs, LANES), BF16),
-        in_specs=[VMEM] * 9, out_specs=VMEM,
+        in_specs=[VMEM] * 8, out_specs=VMEM,
         scratch_shapes=[
             pltpu.VMEM((own, levels * coarse, LANES), BF16),
             pltpu.VMEM((tiles, rows, LANES), F32),
         ],
         compiler_params=params(40), name="transform",
-    )(lengths, waves, far, near, choice, own_part, kernels, fine, wide)
+    )(lengths, waves, near, near_choice, arrival, kernels, fine, wide)
     arrived = lax.all_to_all(coeffs, ("lat", "lev"), 0, 0, tiled=True)
 
     outputs = lev * levels * 2

time: 23.1 us -> 23 us (level)
  blocking collectives: 12.3 us -> 12 us
    pallas_call x0 -> x1, Pallas kernels: none -> 0.36 us  [body(): pl.pallas_call(far_kernel, out_shape=arrival, in_specs=[VMEM] * 4, out_sp...]
    all_to_all x1, blocking collectives: 12.3 us -> 12 us  [body(): arrived = lax.all_to_all(coeffs, ('lat', 'lev'), 0, 0, tiled=True)]
  transfers between devices with their start and end apart: 2 -> 2, of which waited for: 0 -> 0; matrix products, arithmetic and copies ran while one was open for 0% -> 0% of each run, Pallas kernels for 8% -> 10%
where the time goes in v8:
time: 23 us; the launch traced here: 22.8 us
  blocking collectives  12 us (52%)
  Pallas kernels  6.22 us (27%)
  starting transfers between devices  4.55 us (20%)
    all_to_all x1, blocking collectives, body(): arrived = lax.all_to_all(coeffs, ('lat', 'lev'), 0, 0, tiled=True)  12 us
    ppermute x1, starting transfers between devices, body(): near = lax.ppermute(to_near, 'lat', [(i, i ^ 1) for i in range(lat)])  4.03 us
    pallas_call x1, Pallas kernels, body(): pl.pallas_call(functools.partial(table_kernel, lat=lat, lev=lev), out_sha...  1.91 us
    pallas_call x1, Pallas kernels, body(): pl.pallas_call(functools.partial(legendre_kernel, packs=packs), out_shape...  1.68 us
    pallas_call x1, Pallas kernels, body(): pl.pallas_call(outgoing_kernel, out_shape=(halo, halo, like(grid_field),...  1.18 us
    pallas_call x1, Pallas kernels, body(): pl.pallas_call(functools.partial(transform_kernel, top_wave=top_wave), ou...  1.08 us
    ppermute x1, starting transfers between devices, body(): far = lax.ppermute(to_far, ('lat', 'lev'), other_neighbours(lat, lev))  0.52 us
  transfers between devices with their start and end apart: 2, of which 0 were waited for; matrix products, arithmetic and copies ran while one was open for 0% of the time, Pallas kernels for 10%

profile of v8, /device:TPU:0, one launch (start us, length us, event | category | flops | bytes accessed | tf_op | source)
XLA Modules:
  0.0 22.8 jit_solution(18197183847476189385)
XLA Ops:
  0.0 1.2 %outgoing.1 = (bf16[32,256]{1,0:T(8,128)(2,1)S(1)}, bf16[32,256]{1,0:T(8,128)(2,1)S(1)}, bf16[2,160,128]{2,1,0:T(8,128)(2,1)S(1)}, s32[8,128]{1,0:T(8,128)S(1)},...) custom-call(s32[1,2,32]{2,1,0:T(2,128)} %send_hbm.1, ...), custom_call_target="tpu_custom_call" | custom-call | tf_op jit(solution)/shard_map/outgoing/pallas_call | solution.py:459
  1.2 0.5 %collective-permute-start.1 = (bf16[32,256]{1,0:T(8,128)(2,1)S(1)}, bf16[32,256]{1,0:T(8,128)(2,1)S(1)}, u32[]{:S(2)}, u32[]{:S(2)}) collective-permute-start(bf16[32,256]{1,0:T(8,128)(2,1)S(1)} %get-tuple-element.29), channel_id=1, source_target_pairs={{4,8},{5,9},{6,10},{7,11},{12,16},{13,17},{14,18},{15,19},{20,24},... | collective-permute-start | bytes 49160 | tf_op jit(solution)/shard_map/ppermute | solution.py:476
  1.7 4.0 %collective-permute-start = (bf16[32,256]{1,0:T(8,128)(2,1)S(1)}, bf16[32,256]{1,0:T(8,128)(2,1)S(1)}, u32[]{:S(2)}, u32[]{:S(2)}) collective-permute-start(bf16[32,256]{1,0:T(8,128)(2,1)S(1)} %get-tuple-element.27), channel_id=1, source_target_pairs={{0,4},{4,0},{8,12},{12,8},{16,20},{20,16},{24,28},{28,24},{1,5},{5... | collective-permute-start | bytes 49160 | tf_op jit(solution)/shard_map/ppermute | solution.py:475
  5.7 1.9 %tables.1 = (bf16[4,10,128,256]{3,2,1,0:T(8,128)(2,1)S(1)}, f32[4,10,40,256]{3,2,1,0:T(8,128)S(1)}, s32[40,128]{1,0:T(8,128)S(1)}, bf16[160,256]{1,0:T(8,128)(2,...) custom-call(s32[8,128]{1,0:T(8,128)S(1)} %get-tuple-element.20.lengths_ref, ...), custom_call_target="tpu_custom_call" | custom-call | flops 13762560 | bytes 5160960 | tf_op jit(solution)/shard_map/tables/pallas_call | solution.py:484
  7.7 0.0 collective-permute-done.1.far_ref
  7.7 0.4 %far_part.1.arrival_ref = f32[160,256]{1,0:T(8,128)S(1)} custom-call(bf16[32,256]{1,0:T(8,128)(2,1)S(1)} %collective-permute-done.1.far_ref, bf16[160,256]{1,0:T(8,128)(2,1)S(1)} %get-tuple-element.30.choice_ref, bf16[8,128,128]{2,1,0:T(8,128)(2,1)S(1)} %get-tuple-element.25.kernels_ref, f32[160,256]{1,0:T(8,128)S(1)} %get-tuple-element.31.own_ref), custom_call_target="tpu_custom_call" | custom-call | tf_op jit(solution)/shard_map/far_part/pallas_call | solution.py:508
  8.0 0.0 copy-start
  8.1 0.0 collective-permute-done.near_ref
  8.1 1.1 %transform.1 = bf16[32,8,128]{2,1,0:T(8,128)(2,1)S(1)} custom-call(s32[8,128]{1,0:T(8,128)S(1)} %get-tuple-element.20.lengths_ref, s32[10,128]{1,0:T(8,128)S(1)} %get-tuple-element.21.wave_ref, bf16[32,256]{1,0:T(8,128)(2,1)S(1)} %collective-permute-done.near_ref, bf16[160,256]{1,0:T(8,128)(2,1)S(1)} %get-tuple-element.28.choice_ref, ...), custom_call_target="tpu_custom_call" | custom-call | tf_op jit(solution)/shard_map/transform/pallas_call | solution.py:512
  9.2 12.0 %all_to_all.5 = bf16[32,8,128]{2,1,0:T(8,128)(2,1)S(1)} all-to-all(bf16[32,8,128]{2,1,0:T(8,128)(2,1)S(1)} %transform.1), channel_id=1, replica_groups=mesh['lat'=8,'lev'=4] {'lat','lev'}, dimensions={0} | all-to-all | bytes 131072 | tf_op jit(solution)/shard_map/all_to_all | solution.py:522
  21.1 0.0 copy-done
  21.1 1.7 %legendre.1 = bf16[16,40,1280]{2,1,0:T(8,128)(2,1)} custom-call(s32[40,128]{1,0:T(8,128)S(1)} %get-tuple-element.26.limits_ref, bf16[256,128]{1,0:T(8,128)(2,1)S(1)} %bitcast.7, bf16[256,256]{1,0:T(8,128)(2,1)S(1)} %get-tuple-element.34.order_ref, bf16[1280,1280]{1,0:T(8,128)(2,1)S(1)} %bitcast.6), custom_call_target="tpu_custom_call" | custom-call | tf_op jit(solution)/shard_map/legendre/pallas_call | solution.py:527
Async XLA Ops:
  1.2 6.5 %collective-permute-start.1 = (bf16[32,256]{1,0:T(8,128)(2,1)S(1)}, bf16[32,256]{1,0:T(8,128)(2,1)S(1)}, u32[]{:S(2)}, u32[]{:S(2)}) collective-permute-start(bf16[32,256]{1,0:T(8,128)(2,1)S(1)} %get-tuple-element.29), channel_id=1, source_target_pairs={{4,8},{5,9},{6,10},{7,11},{12,16},{13,17},{14,18},{15,19},{20,24},... | collective-permute-start | bytes 49160 | tf_op jit(solution)/shard_map/ppermute | solution.py:476
  1.7 6.3 %collective-permute-start = (bf16[32,256]{1,0:T(8,128)(2,1)S(1)}, bf16[32,256]{1,0:T(8,128)(2,1)S(1)}, u32[]{:S(2)}, u32[]{:S(2)}) collective-permute-start(bf16[32,256]{1,0:T(8,128)(2,1)S(1)} %get-tuple-element.27), channel_id=1, source_target_pairs={{0,4},{4,0},{8,12},{12,8},{16,20},{20,16},{24,28},{28,24},{1,5},{5... | collective-permute-start | bytes 49160 | tf_op jit(solution)/shard_map/ppermute | solution.py:475
  8.0 13.1 %copy-start = (bf16[40,32,1280]{2,1,0:T(8,128)(2,1)S(1)}, bf16[40,32,1280]{2,1,0:T(8,128)(2,1)}, u32[]{:S(2)}) copy-start(bf16[40,32,1280]{2,1,0:T(8,128)(2,1)} %param.15) | copy-start | bytes 9830404

commit v9 on v8

--- a/solution.py
+++ b/solution.py
@@ -41,21 +41,18 @@
     copies = [pltpu.make_async_copy(*pair, sems.at[i]) for i, pair in enumerate(pairs)]
     for copy in copies:
         copy.start()
-    copies[0].wait()
-    copies[1].wait()
     band = lax.axis_index("lat")
     even = lax.rem(band, 2) == 0
+    blocks, count = field_ref.shape[1], send_ref.shape[2]
+    rows = lax.broadcasted_iota(jnp.int32, (blocks, count), 0)
+    copies[0].wait()
+    below, above = send_ref[0, 0:1, :], send_ref[0, 1:2, :]
+    far_hot = jnp.transpose(jnp.where(rows == jnp.where(even, below, above), 1.0, 0.0)).astype(BF16)
+    near_hot = jnp.transpose(jnp.where(rows == jnp.where(even, above, below), 1.0, 0.0)).astype(BF16)
+    copies[1].wait()
     own = side_by_side(field_ref)
-    blocks, count = own.shape[0], send_ref.shape[2]
-    rows = lax.broadcasted_iota(jnp.int32, (blocks, count), 0)
-    below, above = send_ref[0, 0:1, :], send_ref[0, 1:2, :]
-    for ref, listed in (
-        (far_ref, jnp.where(even, below, above)),
-        (near_ref, jnp.where(even, above, below)),
-    ):
-        picked = lax.dot_general(
-            one_hot(rows == listed), own, CONTRACT_ROWS, preferred_element_type=F32
-        )
+    for ref, hot in ((far_ref, far_hot), (near_ref, near_hot)):
+        picked = jnp.dot(hot, own, preferred_element_type=F32)
         ref[...] = picked.astype(BF16)
     copies[2].wait()
     circles = lengths_ref.shape[0] // 2
@@ -132,34 +129,43 @@
     row = lax.broadcasted_iota(jnp.int32, (8, LANES), 0)
     near_step = (row + LANES // 2 * (coarse - 1)).astype(F32)
     far_step = (row * LANES + LANES // 2).astype(F32)
-    hop_step = jnp.left_shift(8, jnp.where(row < 4, row, row - 4 + log(LANES))).astype(F32)
-
-    def doubled(base, hops, groups):
-        out = [base]
+    hop_step = jnp.where((row & 1) == 0, 8, 8 * LANES).astype(F32)
+    group = 4 if circles % 4 == 0 else 1
+
+    def stepped(base, hop, groups):
+        out = [base, times(base, hop)]
+        twice = hop[0] + hop[0]
         while len(out) < groups:
-            k = log(len(out))
-            hop = tuple(jnp.broadcast_to(x[k : k + 1], (8, LANES)) for x in hops)
-            out += [times(e, hop) for e in out[: groups - len(out)]]
-        return [jnp.concatenate(part, axis=0) for part in zip(*out)]
-
-    def circle(g):
-        length = jnp.broadcast_to(lengths_ref[pl.ds(g, 1)], (8, LANES)).astype(F32)
-        return length, 1.0 / length
-
-    def table(g, t, length, inverse):
+            out.append(tuple(twice * x - y for x, y in zip(out[-1], out[-2])))
+        return [jnp.concatenate(part, axis=0) for part in zip(*out[:groups])]
+
+    def lengths_of(first):
+        each = [
+            jnp.broadcast_to(lengths_ref[pl.ds(first + i, 1)], (8, LANES)) for i in range(group)
+        ]
+        mixed = each[0]
+        for i in range(1, group):
+            mixed = jnp.where(row >= 2 * i, each[i], mixed)
+        return [(x.astype(F32), 1.0 / x.astype(F32)) for x in (*each, mixed)]
+
+    def table(first, t, scales):
         waves = jnp.broadcast_to(wave_ref[pl.ds(t, 1), :], (8, LANES)).astype(F32)
-        hops = turn(hop_step, waves, length, inverse)
-        fine = doubled(turn(near_step, waves, length, inverse), hops, LANES // 8)
-        fine_ref[g, t] = jnp.concatenate(fine, axis=1).astype(BF16)
-        wide = doubled(
-            turn(far_step, waves, length, inverse), tuple(x[4:] for x in hops), -(-half // 8)
-        )
-        coarse_ref[g, t] = jnp.concatenate(
-            [jnp.concatenate([part[:half]] * levels, axis=0) for part in wide], axis=1
-        )
+        hops = turn(hop_step, waves, *scales[group])
+        for i in range(group):
+            near_hop, far_hop = (
+                tuple(jnp.broadcast_to(x[k : k + 1], (8, LANES)) for x in hops)
+                for k in (2 * i, 2 * i + 1)
+            )
+            fine = stepped(turn(near_step, waves, *scales[i]), near_hop, LANES // 8)
+            fine_ref[first + i, t] = jnp.concatenate(fine, axis=1).astype(BF16)
+            wide = stepped(turn(far_step, waves, *scales[i]), far_hop, -(-half // 8))
+            coarse_ref[first + i, t] = jnp.concatenate(
+                [jnp.concatenate([part[:half]] * levels, axis=0) for part in wide], axis=1
+            )
 
     def looped(index, _):
-        table(index // tiles, lax.rem(index, tiles), *circle(index // tiles))
+        first = index // tiles * group
+        table(first, lax.rem(index, tiles), lengths_of(first))
         return 0
 
     listed = jnp.concatenate(
@@ -202,13 +208,13 @@
             total = value if k == 0 else total + value
         arrival_ref[:, l * LANES : (l + 1) * LANES] = total
 
-    unrolled = circles * tiles <= 64
-    if unrolled:
-        for g in range(circles):
+    if circles * tiles <= 64:
+        for first in range(0, circles, group):
+            scales = lengths_of(first)
             for t in range(tiles):
-                table(g, t, *circle(g))
+                table(first, t, scales)
     else:
-        lax.fori_loop(0, circles * tiles, looped, 0, unroll=2)
+        lax.fori_loop(0, circles // group * tiles, looped, 0)
 
     fetch.wait()
     slots = limits_ref.shape[0]

time: 23 us -> 22.9 us (level)
  Pallas kernels: 6.22 us -> 5.94 us
  transfers between devices with their start and end apart: 2 -> 2, of which waited for: 0 -> 0; matrix products, arithmetic and copies ran while one was open for 0% -> 0% of each run, Pallas kernels for 10% -> 9%
where the time goes in v9:
time: 22.9 us; the launch traced here: 22.8 us
  blocking collectives  12.2 us (53%)
  Pallas kernels  5.94 us (26%)
  starting transfers between devices  4.55 us (20%)
    all_to_all x1, blocking collectives, body(): arrived = lax.all_to_all(coeffs, ('lat', 'lev'), 0, 0, tiled=True)  12.2 us
    ppermute x1, starting transfers between devices, body(): near = lax.ppermute(to_near, 'lat', [(i, i ^ 1) for i in range(lat)])  4.03 us
    pallas_call x1, Pallas kernels, body(): pl.pallas_call(functools.partial(table_kernel, lat=lat, lev=lev), out_sha...  1.69 us
    pallas_call x1, Pallas kernels, body(): pl.pallas_call(functools.partial(legendre_kernel, packs=packs), out_shape...  1.68 us
    pallas_call x1, Pallas kernels, body(): pl.pallas_call(outgoing_kernel, out_shape=(halo, halo, like(grid_field),...  1.13 us
    pallas_call x1, Pallas kernels, body(): pl.pallas_call(functools.partial(transform_kernel, top_wave=top_wave), ou...  1.08 us
    ppermute x1, starting transfers between devices, body(): far = lax.ppermute(to_far, ('lat', 'lev'), other_neighbours(lat, lev))  0.52 us
  transfers between devices with their start and end apart: 2, of which 0 were waited for; matrix products, arithmetic and copies ran while one was open for 0% of the time, Pallas kernels for 9%

profile of v9, /device:TPU:0, one launch (start us, length us, event | category | flops | bytes accessed | tf_op | source)
XLA Modules:
  0.0 22.8 jit_solution(16820165773540856358)
XLA Ops:
  0.0 1.1 %outgoing.1 = (bf16[32,256]{1,0:T(8,128)(2,1)S(1)}, bf16[32,256]{1,0:T(8,128)(2,1)S(1)}, bf16[2,160,128]{2,1,0:T(8,128)(2,1)S(1)}, s32[8,128]{1,0:T(8,128)S(1)},...) custom-call(s32[1,2,32]{2,1,0:T(2,128)} %send_hbm.1, ...), custom_call_target="tpu_custom_call" | custom-call | tf_op jit(solution)/shard_map/outgoing/pallas_call | solution.py:465
  1.1 0.5 %collective-permute-start.1 = (bf16[32,256]{1,0:T(8,128)(2,1)S(1)}, bf16[32,256]{1,0:T(8,128)(2,1)S(1)}, u32[]{:S(2)}, u32[]{:S(2)}) collective-permute-start(bf16[32,256]{1,0:T(8,128)(2,1)S(1)} %get-tuple-element.29), channel_id=1, source_target_pairs={{4,8},{5,9},{6,10},{7,11},{12,16},{13,17},{14,18},{15,19},{20,24},... | collective-permute-start | bytes 49160 | tf_op jit(solution)/shard_map/ppermute | solution.py:482
  1.7 4.0 %collective-permute-start = (bf16[32,256]{1,0:T(8,128)(2,1)S(1)}, bf16[32,256]{1,0:T(8,128)(2,1)S(1)}, u32[]{:S(2)}, u32[]{:S(2)}) collective-permute-start(bf16[32,256]{1,0:T(8,128)(2,1)S(1)} %get-tuple-element.27), channel_id=1, source_target_pairs={{0,4},{4,0},{8,12},{12,8},{16,20},{20,16},{24,28},{28,24},{1,5},{5... | collective-permute-start | bytes 49160 | tf_op jit(solution)/shard_map/ppermute | solution.py:481
  5.7 1.7 %tables.1 = (bf16[4,10,128,256]{3,2,1,0:T(8,128)(2,1)S(1)}, f32[4,10,40,256]{3,2,1,0:T(8,128)S(1)}, s32[40,128]{1,0:T(8,128)S(1)}, bf16[160,256]{1,0:T(8,128)(2,...) custom-call(s32[8,128]{1,0:T(8,128)S(1)} %get-tuple-element.20.lengths_ref, ...), custom_call_target="tpu_custom_call" | custom-call | flops 13762560 | bytes 5160960 | tf_op jit(solution)/shard_map/tables/pallas_call | solution.py:490
  7.4 0.0 collective-permute-done.1.far_ref
  7.4 0.4 %far_part.1.arrival_ref = f32[160,256]{1,0:T(8,128)S(1)} custom-call(bf16[32,256]{1,0:T(8,128)(2,1)S(1)} %collective-permute-done.1.far_ref, bf16[160,256]{1,0:T(8,128)(2,1)S(1)} %get-tuple-element.30.choice_ref, bf16[8,128,128]{2,1,0:T(8,128)(2,1)S(1)} %get-tuple-element.25.kernels_ref, f32[160,256]{1,0:T(8,128)S(1)} %get-tuple-element.31.own_ref), custom_call_target="tpu_custom_call" | custom-call | tf_op jit(solution)/shard_map/far_part/pallas_call | solution.py:514
  7.8 0.0 copy-start
  7.8 0.0 collective-permute-done.near_ref
  7.8 1.1 %transform.1 = bf16[32,8,128]{2,1,0:T(8,128)(2,1)S(1)} custom-call(s32[8,128]{1,0:T(8,128)S(1)} %get-tuple-element.20.lengths_ref, s32[10,128]{1,0:T(8,128)S(1)} %get-tuple-element.21.wave_ref, bf16[32,256]{1,0:T(8,128)(2,1)S(1)} %collective-permute-done.near_ref, bf16[160,256]{1,0:T(8,128)(2,1)S(1)} %get-tuple-element.28.choice_ref, ...), custom_call_target="tpu_custom_call" | custom-call | tf_op jit(solution)/shard_map/transform/pallas_call | solution.py:518
  8.9 12.2 %all_to_all.5 = bf16[32,8,128]{2,1,0:T(8,128)(2,1)S(1)} all-to-all(bf16[32,8,128]{2,1,0:T(8,128)(2,1)S(1)} %transform.1), channel_id=1, replica_groups=mesh['lat'=8,'lev'=4] {'lat','lev'}, dimensions={0} | all-to-all | bytes 131072 | tf_op jit(solution)/shard_map/all_to_all | solution.py:528
  21.1 0.0 copy-done
  21.1 1.7 %legendre.1 = bf16[16,40,1280]{2,1,0:T(8,128)(2,1)} custom-call(s32[40,128]{1,0:T(8,128)S(1)} %get-tuple-element.26.limits_ref, bf16[256,128]{1,0:T(8,128)(2,1)S(1)} %bitcast.7, bf16[256,256]{1,0:T(8,128)(2,1)S(1)} %get-tuple-element.34.order_ref, bf16[1280,1280]{1,0:T(8,128)(2,1)S(1)} %bitcast.6), custom_call_target="tpu_custom_call" | custom-call | tf_op jit(solution)/shard_map/legendre/pallas_call | solution.py:533
Async XLA Ops:
  1.1 6.3 %collective-permute-start.1 = (bf16[32,256]{1,0:T(8,128)(2,1)S(1)}, bf16[32,256]{1,0:T(8,128)(2,1)S(1)}, u32[]{:S(2)}, u32[]{:S(2)}) collective-permute-start(bf16[32,256]{1,0:T(8,128)(2,1)S(1)} %get-tuple-element.29), channel_id=1, source_target_pairs={{4,8},{5,9},{6,10},{7,11},{12,16},{13,17},{14,18},{15,19},{20,24},... | collective-permute-start | bytes 49160 | tf_op jit(solution)/shard_map/ppermute | solution.py:482
  1.7 6.1 %collective-permute-start = (bf16[32,256]{1,0:T(8,128)(2,1)S(1)}, bf16[32,256]{1,0:T(8,128)(2,1)S(1)}, u32[]{:S(2)}, u32[]{:S(2)}) collective-permute-start(bf16[32,256]{1,0:T(8,128)(2,1)S(1)} %get-tuple-element.27), channel_id=1, source_target_pairs={{0,4},{4,0},{8,12},{12,8},{16,20},{20,16},{24,28},{28,24},{1,5},{5... | collective-permute-start | bytes 49160 | tf_op jit(solution)/shard_map/ppermute | solution.py:481
  7.8 13.3 %copy-start = (bf16[40,32,1280]{2,1,0:T(8,128)(2,1)S(1)}, bf16[40,32,1280]{2,1,0:T(8,128)(2,1)}, u32[]{:S(2)}) copy-start(bf16[40,32,1280]{2,1,0:T(8,128)(2,1)} %param.15) | copy-start | bytes 9830404

commit v10 on v9

--- a/solution.py
+++ b/solution.py
@@ -65,12 +65,11 @@
 
 SINE = (0.07761395, -0.59827207, 2.55007494, -5.16770998, 3.14159264)
 COSINE = (0.21953804, -1.33180992, 4.05840238, -4.93479245, 0.99999995)
-ROUND = 1.5 * 2.0**23
 
 
 def turn(steps, waves, length, inverse):
     phase = steps * waves
-    rest = phase - ((phase * inverse + ROUND) - ROUND) * length
+    rest = phase - jnp.floor(phase * inverse + 0.5) * length
     f = rest * inverse
     x = f * f
     s, c = SINE[0], COSINE[0]

time: 22.9 us -> 22.9 us (level)
  no operation moved by 1% of the time
where the time goes in v10:
time: 22.9 us; the launch traced here: 22.8 us
  blocking collectives  12.2 us (53%)
  Pallas kernels  5.94 us (26%)
  starting transfers between devices  4.55 us (20%)
    all_to_all x1, blocking collectives, body(): arrived = lax.all_to_all(coeffs, ('lat', 'lev'), 0, 0, tiled=True)  12.2 us
    ppermute x1, starting transfers between devices, body(): near = lax.ppermute(to_near, 'lat', [(i, i ^ 1) for i in range(lat)])  4.03 us
    pallas_call x1, Pallas kernels, body(): pl.pallas_call(functools.partial(table_kernel, lat=lat, lev=lev), out_sha...  1.69 us
    pallas_call x1, Pallas kernels, body(): pl.pallas_call(functools.partial(legendre_kernel, packs=packs), out_shape...  1.68 us
    pallas_call x1, Pallas kernels, body(): pl.pallas_call(outgoing_kernel, out_shape=(halo, halo, like(grid_field),...  1.13 us
    pallas_call x1, Pallas kernels, body(): pl.pallas_call(functools.partial(transform_kernel, top_wave=top_wave), ou...  1.08 us
    ppermute x1, starting transfers between devices, body(): far = lax.ppermute(to_far, ('lat', 'lev'), other_neighbours(lat, lev))  0.52 us
  transfers between devices with their start and end apart: 2, of which 0 were waited for; matrix products, arithmetic and copies ran while one was open for 0% of the time, Pallas kernels for 9%

profile of v10, /device:TPU:0, one launch (start us, length us, event | category | flops | bytes accessed | tf_op | source)
XLA Modules:
  0.0 22.8 jit_solution(6285196996984920053)
XLA Ops:
  0.0 1.1 %outgoing.1 = (bf16[32,256]{1,0:T(8,128)(2,1)S(1)}, bf16[32,256]{1,0:T(8,128)(2,1)S(1)}, bf16[2,160,128]{2,1,0:T(8,128)(2,1)S(1)}, s32[8,128]{1,0:T(8,128)S(1)},...) custom-call(s32[1,2,32]{2,1,0:T(2,128)} %send_hbm.1, ...), custom_call_target="tpu_custom_call" | custom-call | tf_op jit(solution)/shard_map/outgoing/pallas_call | solution.py:464
  1.1 0.5 %collective-permute-start.1 = (bf16[32,256]{1,0:T(8,128)(2,1)S(1)}, bf16[32,256]{1,0:T(8,128)(2,1)S(1)}, u32[]{:S(2)}, u32[]{:S(2)}) collective-permute-start(bf16[32,256]{1,0:T(8,128)(2,1)S(1)} %get-tuple-element.29), channel_id=1, source_target_pairs={{4,8},{5,9},{6,10},{7,11},{12,16},{13,17},{14,18},{15,19},{20,24},... | collective-permute-start | bytes 49160 | tf_op jit(solution)/shard_map/ppermute | solution.py:481
  1.7 4.0 %collective-permute-start = (bf16[32,256]{1,0:T(8,128)(2,1)S(1)}, bf16[32,256]{1,0:T(8,128)(2,1)S(1)}, u32[]{:S(2)}, u32[]{:S(2)}) collective-permute-start(bf16[32,256]{1,0:T(8,128)(2,1)S(1)} %get-tuple-element.27), channel_id=1, source_target_pairs={{0,4},{4,0},{8,12},{12,8},{16,20},{20,16},{24,28},{28,24},{1,5},{5... | collective-permute-start | bytes 49160 | tf_op jit(solution)/shard_map/ppermute | solution.py:480
  5.7 1.7 %tables.1 = (bf16[4,10,128,256]{3,2,1,0:T(8,128)(2,1)S(1)}, f32[4,10,40,256]{3,2,1,0:T(8,128)S(1)}, s32[40,128]{1,0:T(8,128)S(1)}, bf16[160,256]{1,0:T(8,128)(2,...) custom-call(s32[8,128]{1,0:T(8,128)S(1)} %get-tuple-element.20.lengths_ref, ...), custom_call_target="tpu_custom_call" | custom-call | flops 13762560 | bytes 5160960 | tf_op jit(solution)/shard_map/tables/pallas_call | solution.py:489
  7.4 0.0 collective-permute-done.1.far_ref
  7.4 0.4 %far_part.1.arrival_ref = f32[160,256]{1,0:T(8,128)S(1)} custom-call(bf16[32,256]{1,0:T(8,128)(2,1)S(1)} %collective-permute-done.1.far_ref, bf16[160,256]{1,0:T(8,128)(2,1)S(1)} %get-tuple-element.30.choice_ref, bf16[8,128,128]{2,1,0:T(8,128)(2,1)S(1)} %get-tuple-element.25.kernels_ref, f32[160,256]{1,0:T(8,128)S(1)} %get-tuple-element.31.own_ref), custom_call_target="tpu_custom_call" | custom-call | tf_op jit(solution)/shard_map/far_part/pallas_call | solution.py:513
  7.8 0.0 copy-start
  7.8 0.0 collective-permute-done.near_ref
  7.8 1.1 %transform.1 = bf16[32,8,128]{2,1,0:T(8,128)(2,1)S(1)} custom-call(s32[8,128]{1,0:T(8,128)S(1)} %get-tuple-element.20.lengths_ref, s32[10,128]{1,0:T(8,128)S(1)} %get-tuple-element.21.wave_ref, bf16[32,256]{1,0:T(8,128)(2,1)S(1)} %collective-permute-done.near_ref, bf16[160,256]{1,0:T(8,128)(2,1)S(1)} %get-tuple-element.28.choice_ref, ...), custom_call_target="tpu_custom_call" | custom-call | tf_op jit(solution)/shard_map/transform/pallas_call | solution.py:517
  8.9 12.2 %all_to_all.5 = bf16[32,8,128]{2,1,0:T(8,128)(2,1)S(1)} all-to-all(bf16[32,8,128]{2,1,0:T(8,128)(2,1)S(1)} %transform.1), channel_id=1, replica_groups=mesh['lat'=8,'lev'=4] {'lat','lev'}, dimensions={0} | all-to-all | bytes 131072 | tf_op jit(solution)/shard_map/all_to_all | solution.py:527
  21.1 0.0 copy-done
  21.1 1.7 %legendre.1 = bf16[16,40,1280]{2,1,0:T(8,128)(2,1)} custom-call(s32[40,128]{1,0:T(8,128)S(1)} %get-tuple-element.26.limits_ref, bf16[256,128]{1,0:T(8,128)(2,1)S(1)} %bitcast.7, bf16[256,256]{1,0:T(8,128)(2,1)S(1)} %get-tuple-element.34.order_ref, bf16[1280,1280]{1,0:T(8,128)(2,1)S(1)} %bitcast.6), custom_call_target="tpu_custom_call" | custom-call | tf_op jit(solution)/shard_map/legendre/pallas_call | solution.py:532
Async XLA Ops:
  1.1 6.2 %collective-permute-start.1 = (bf16[32,256]{1,0:T(8,128)(2,1)S(1)}, bf16[32,256]{1,0:T(8,128)(2,1)S(1)}, u32[]{:S(2)}, u32[]{:S(2)}) collective-permute-start(bf16[32,256]{1,0:T(8,128)(2,1)S(1)} %get-tuple-element.29), channel_id=1, source_target_pairs={{4,8},{5,9},{6,10},{7,11},{12,16},{13,17},{14,18},{15,19},{20,24},... | collective-permute-start | bytes 49160 | tf_op jit(solution)/shard_map/ppermute | solution.py:481
  1.7 6.1 %collective-permute-start = (bf16[32,256]{1,0:T(8,128)(2,1)S(1)}, bf16[32,256]{1,0:T(8,128)(2,1)S(1)}, u32[]{:S(2)}, u32[]{:S(2)}) collective-permute-start(bf16[32,256]{1,0:T(8,128)(2,1)S(1)} %get-tuple-element.27), channel_id=1, source_target_pairs={{0,4},{4,0},{8,12},{12,8},{16,20},{20,16},{24,28},{28,24},{1,5},{5... | collective-permute-start | bytes 49160 | tf_op jit(solution)/shard_map/ppermute | solution.py:480
  7.8 13.3 %copy-start = (bf16[40,32,1280]{2,1,0:T(8,128)(2,1)S(1)}, bf16[40,32,1280]{2,1,0:T(8,128)(2,1)}, u32[]{:S(2)}) copy-start(bf16[40,32,1280]{2,1,0:T(8,128)(2,1)} %param.15) | copy-start | bytes 9830404

commit v11 on v10

--- a/solution.py
+++ b/solution.py
@@ -292,6 +292,8 @@
     distance = lax.broadcasted_iota(jnp.int32, (coarse, LANES), 0)
     row = jnp.where(distance < half, distance + half, coarse - 1 - distance)
     position = row * LANES + lax.broadcasted_iota(jnp.int32, (coarse, LANES), 1)
+    unrolled = circles * tiles <= 64
+    points = []
     for g in range(circles):
         inside = position < jnp.broadcast_to(lengths_ref[g : g + 1], (coarse, LANES))
         sums, differences = [], []
@@ -301,7 +303,9 @@
             part = jnp.where(inside, part * part, 0.0)
             sums.append(part[:half] + part[half:])
             differences.append(part[:half] - part[half:])
-        points_ref[g] = jnp.concatenate(sums + differences, axis=0).astype(BF16)
+        points.append(jnp.concatenate(sums + differences, axis=0).astype(BF16))
+        if not unrolled:
+            points_ref[g] = points[g]
 
     height = 2 * circles
     lengths = lengths_ref[...]
@@ -323,7 +327,8 @@
     def tile(t):
         sums = [([], []) for _ in range(levels)]
         for g in range(circles):
-            turned = jnp.dot(points_ref[g], fine_ref[g, t], preferred_element_type=F32)
+            rows = points[g] if unrolled else points_ref[g]
+            turned = jnp.dot(rows, fine_ref[g, t], preferred_element_type=F32)
             both, apart = turned[: levels * half], turned[levels * half :]
             c, s = coarse_ref[g, t, :, :LANES], coarse_ref[g, t, :, LANES:]
             real = both[:, :LANES] * c - apart[:, LANES:] * s
@@ -350,7 +355,7 @@
     packs = coeff_ref.shape[1] // chunk_rows
     step = LANES // packs
     lane = lax.broadcasted_iota(jnp.int32, (chunk_rows, LANES), 1)
-    if circles * tiles <= 64:
+    if unrolled:
         coeffs = [tile(t) for t in range(tiles)]
     else:
         lax.fori_loop(0, tiles, stored, 0)

time: 22.9 us -> 22.9 us (level)
  no operation moved by 1% of the time
where the time goes in v11:
time: 22.9 us; the launch traced here: 22.8 us
  blocking collectives  12.2 us (53%)
  Pallas kernels  5.94 us (26%)
  starting transfers between devices  4.55 us (20%)
    all_to_all x1, blocking collectives, body(): arrived = lax.all_to_all(coeffs, ('lat', 'lev'), 0, 0, tiled=True)  12.2 us
    ppermute x1, starting transfers between devices, body(): near = lax.ppermute(to_near, 'lat', [(i, i ^ 1) for i in range(lat)])  4.03 us
    pallas_call x1, Pallas kernels, body(): pl.pallas_call(functools.partial(table_kernel, lat=lat, lev=lev), out_sha...  1.69 us
    pallas_call x1, Pallas kernels, body(): pl.pallas_call(functools.partial(legendre_kernel, packs=packs), out_shape...  1.68 us
    pallas_call x1, Pallas kernels, body(): pl.pallas_call(outgoing_kernel, out_shape=(halo, halo, like(grid_field),...  1.13 us
    pallas_call x1, Pallas kernels, body(): pl.pallas_call(functools.partial(transform_kernel, top_wave=top_wave), ou...  1.08 us
    ppermute x1, starting transfers between devices, body(): far = lax.ppermute(to_far, ('lat', 'lev'), other_neighbours(lat, lev))  0.52 us
  transfers between devices with their start and end apart: 2, of which 0 were waited for; matrix products, arithmetic and copies ran while one was open for 0% of the time, Pallas kernels for 9%

profile of v11, /device:TPU:0, one launch (start us, length us, event | category | flops | bytes accessed | tf_op | source)
XLA Modules:
  0.0 22.8 jit_solution(1224103155137814698)
XLA Ops:
  0.0 1.1 %outgoing.1 = (bf16[32,256]{1,0:T(8,128)(2,1)S(1)}, bf16[32,256]{1,0:T(8,128)(2,1)S(1)}, bf16[2,160,128]{2,1,0:T(8,128)(2,1)S(1)}, s32[8,128]{1,0:T(8,128)S(1)},...) custom-call(s32[1,2,32]{2,1,0:T(2,128)} %send_hbm.1, ...), custom_call_target="tpu_custom_call" | custom-call | tf_op jit(solution)/shard_map/outgoing/pallas_call | solution.py:469
  1.1 0.5 %collective-permute-start.1 = (bf16[32,256]{1,0:T(8,128)(2,1)S(1)}, bf16[32,256]{1,0:T(8,128)(2,1)S(1)}, u32[]{:S(2)}, u32[]{:S(2)}) collective-permute-start(bf16[32,256]{1,0:T(8,128)(2,1)S(1)} %get-tuple-element.29), channel_id=1, source_target_pairs={{4,8},{5,9},{6,10},{7,11},{12,16},{13,17},{14,18},{15,19},{20,24},... | collective-permute-start | bytes 49160 | tf_op jit(solution)/shard_map/ppermute | solution.py:486
  1.7 4.0 %collective-permute-start = (bf16[32,256]{1,0:T(8,128)(2,1)S(1)}, bf16[32,256]{1,0:T(8,128)(2,1)S(1)}, u32[]{:S(2)}, u32[]{:S(2)}) collective-permute-start(bf16[32,256]{1,0:T(8,128)(2,1)S(1)} %get-tuple-element.27), channel_id=1, source_target_pairs={{0,4},{4,0},{8,12},{12,8},{16,20},{20,16},{24,28},{28,24},{1,5},{5... | collective-permute-start | bytes 49160 | tf_op jit(solution)/shard_map/ppermute | solution.py:485
  5.7 1.7 %tables.1 = (bf16[4,10,128,256]{3,2,1,0:T(8,128)(2,1)S(1)}, f32[4,10,40,256]{3,2,1,0:T(8,128)S(1)}, s32[40,128]{1,0:T(8,128)S(1)}, bf16[160,256]{1,0:T(8,128)(2,...) custom-call(s32[8,128]{1,0:T(8,128)S(1)} %get-tuple-element.20.lengths_ref, ...), custom_call_target="tpu_custom_call" | custom-call | flops 13762560 | bytes 5160960 | tf_op jit(solution)/shard_map/tables/pallas_call | solution.py:494
  7.4 0.0 collective-permute-done.1.far_ref
  7.4 0.4 %far_part.1.arrival_ref = f32[160,256]{1,0:T(8,128)S(1)} custom-call(bf16[32,256]{1,0:T(8,128)(2,1)S(1)} %collective-permute-done.1.far_ref, bf16[160,256]{1,0:T(8,128)(2,1)S(1)} %get-tuple-element.30.choice_ref, bf16[8,128,128]{2,1,0:T(8,128)(2,1)S(1)} %get-tuple-element.25.kernels_ref, f32[160,256]{1,0:T(8,128)S(1)} %get-tuple-element.31.own_ref), custom_call_target="tpu_custom_call" | custom-call | tf_op jit(solution)/shard_map/far_part/pallas_call | solution.py:518
  7.8 0.0 copy-start
  7.8 0.0 collective-permute-done.near_ref
  7.8 1.1 %transform.1 = bf16[32,8,128]{2,1,0:T(8,128)(2,1)S(1)} custom-call(s32[8,128]{1,0:T(8,128)S(1)} %get-tuple-element.20.lengths_ref, s32[10,128]{1,0:T(8,128)S(1)} %get-tuple-element.21.wave_ref, bf16[32,256]{1,0:T(8,128)(2,1)S(1)} %collective-permute-done.near_ref, bf16[160,256]{1,0:T(8,128)(2,1)S(1)} %get-tuple-element.28.choice_ref, ...), custom_call_target="tpu_custom_call" | custom-call | tf_op jit(solution)/shard_map/transform/pallas_call | solution.py:522
  8.9 12.2 %all_to_all.5 = bf16[32,8,128]{2,1,0:T(8,128)(2,1)S(1)} all-to-all(bf16[32,8,128]{2,1,0:T(8,128)(2,1)S(1)} %transform.1), channel_id=1, replica_groups=mesh['lat'=8,'lev'=4] {'lat','lev'}, dimensions={0} | all-to-all | bytes 131072 | tf_op jit(solution)/shard_map/all_to_all | solution.py:532
  21.1 0.0 copy-done
  21.1 1.7 %legendre.1 = bf16[16,40,1280]{2,1,0:T(8,128)(2,1)} custom-call(s32[40,128]{1,0:T(8,128)S(1)} %get-tuple-element.26.limits_ref, bf16[256,128]{1,0:T(8,128)(2,1)S(1)} %bitcast.7, bf16[256,256]{1,0:T(8,128)(2,1)S(1)} %get-tuple-element.34.order_ref, bf16[1280,1280]{1,0:T(8,128)(2,1)S(1)} %bitcast.6), custom_call_target="tpu_custom_call" | custom-call | tf_op jit(solution)/shard_map/legendre/pallas_call | solution.py:537
Async XLA Ops:
  1.1 6.2 %collective-permute-start.1 = (bf16[32,256]{1,0:T(8,128)(2,1)S(1)}, bf16[32,256]{1,0:T(8,128)(2,1)S(1)}, u32[]{:S(2)}, u32[]{:S(2)}) collective-permute-start(bf16[32,256]{1,0:T(8,128)(2,1)S(1)} %get-tuple-element.29), channel_id=1, source_target_pairs={{4,8},{5,9},{6,10},{7,11},{12,16},{13,17},{14,18},{15,19},{20,24},... | collective-permute-start | bytes 49160 | tf_op jit(solution)/shard_map/ppermute | solution.py:486
  1.7 6.1 %collective-permute-start = (bf16[32,256]{1,0:T(8,128)(2,1)S(1)}, bf16[32,256]{1,0:T(8,128)(2,1)S(1)}, u32[]{:S(2)}, u32[]{:S(2)}) collective-permute-start(bf16[32,256]{1,0:T(8,128)(2,1)S(1)} %get-tuple-element.27), channel_id=1, source_target_pairs={{0,4},{4,0},{8,12},{12,8},{16,20},{20,16},{24,28},{28,24},{1,5},{5... | collective-permute-start | bytes 49160 | tf_op jit(solution)/shard_map/ppermute | solution.py:485
  7.8 13.3 %copy-start = (bf16[40,32,1280]{2,1,0:T(8,128)(2,1)S(1)}, bf16[40,32,1280]{2,1,0:T(8,128)(2,1)}, u32[]{:S(2)}) copy-start(bf16[40,32,1280]{2,1,0:T(8,128)(2,1)} %param.15) | copy-start | bytes 9830404

commit v12 on v11

--- a/solution.py
+++ b/solution.py
@@ -411,9 +411,8 @@
     lane = lax.broadcasted_iota(jnp.int32, (8, wide), 1)
     limits = [limits_ref[8 * k : 8 * k + 8] for k in range(slots // 8)]
     limits = [jnp.concatenate([m, m], axis=1) for m in limits]
-    copies = []
-    for n in range(0, top_wave, wide):
-        sums = [
+    def products(n):
+        return [
             jnp.dot(
                 spread[k],
                 legendre_ref[8 * k * circles : 8 * (k + 1) * circles, n : n + wide],
@@ -421,6 +420,11 @@
             )
             for k in range(slots // 8)
         ]
+
+    copies = []
+    later = products(0)
+    for n in range(0, top_wave, wide):
+        sums, later = later, products(n + wide) if n + wide < top_wave else None
         keep = [lane + n >= m for m in limits]
         for o in range(outputs):
             out_ref[o, :, n : n + wide] = jnp.concatenate(

time: 22.9 us -> 22.9 us (level)
  no operation moved by 1% of the time
where the time goes in v12:
time: 22.9 us; the launch traced here: 22.8 us
  blocking collectives  12.2 us (53%)
  Pallas kernels  5.94 us (26%)
  starting transfers between devices  4.55 us (20%)
    all_to_all x1, blocking collectives, body(): arrived = lax.all_to_all(coeffs, ('lat', 'lev'), 0, 0, tiled=True)  12.2 us
    ppermute x1, starting transfers between devices, body(): near = lax.ppermute(to_near, 'lat', [(i, i ^ 1) for i in range(lat)])  4.03 us
    pallas_call x1, Pallas kernels, body(): pl.pallas_call(functools.partial(table_kernel, lat=lat, lev=lev), out_sha...  1.69 us
    pallas_call x1, Pallas kernels, body(): pl.pallas_call(functools.partial(legendre_kernel, packs=packs), out_shape...  1.68 us
    pallas_call x1, Pallas kernels, body(): pl.pallas_call(outgoing_kernel, out_shape=(halo, halo, like(grid_field),...  1.13 us
    pallas_call x1, Pallas kernels, body(): pl.pallas_call(functools.partial(transform_kernel, top_wave=top_wave), ou...  1.08 us
    ppermute x1, starting transfers between devices, body(): far = lax.ppermute(to_far, ('lat', 'lev'), other_neighbours(lat, lev))  0.52 us
  transfers between devices with their start and end apart: 2, of which 0 were waited for; matrix products, arithmetic and copies ran while one was open for 0% of the time, Pallas kernels for 9%

profile of v12, /device:TPU:0, one launch (start us, length us, event | category | flops | bytes accessed | tf_op | source)
XLA Modules:
  0.0 22.8 jit_solution(8241060847668130735)
XLA Ops:
  0.0 1.1 %outgoing.1 = (bf16[32,256]{1,0:T(8,128)(2,1)S(1)}, bf16[32,256]{1,0:T(8,128)(2,1)S(1)}, bf16[2,160,128]{2,1,0:T(8,128)(2,1)S(1)}, s32[8,128]{1,0:T(8,128)S(1)},...) custom-call(s32[1,2,32]{2,1,0:T(2,128)} %send_hbm.1, ...), custom_call_target="tpu_custom_call" | custom-call | tf_op jit(solution)/shard_map/outgoing/pallas_call | solution.py:473
  1.1 0.5 %collective-permute-start.1 = (bf16[32,256]{1,0:T(8,128)(2,1)S(1)}, bf16[32,256]{1,0:T(8,128)(2,1)S(1)}, u32[]{:S(2)}, u32[]{:S(2)}) collective-permute-start(bf16[32,256]{1,0:T(8,128)(2,1)S(1)} %get-tuple-element.29), channel_id=1, source_target_pairs={{4,8},{5,9},{6,10},{7,11},{12,16},{13,17},{14,18},{15,19},{20,24},... | collective-permute-start | bytes 49160 | tf_op jit(solution)/shard_map/ppermute | solution.py:490
  1.7 4.0 %collective-permute-start = (bf16[32,256]{1,0:T(8,128)(2,1)S(1)}, bf16[32,256]{1,0:T(8,128)(2,1)S(1)}, u32[]{:S(2)}, u32[]{:S(2)}) collective-permute-start(bf16[32,256]{1,0:T(8,128)(2,1)S(1)} %get-tuple-element.27), channel_id=1, source_target_pairs={{0,4},{4,0},{8,12},{12,8},{16,20},{20,16},{24,28},{28,24},{1,5},{5... | collective-permute-start | bytes 49160 | tf_op jit(solution)/shard_map/ppermute | solution.py:489
  5.7 1.7 %tables.1 = (bf16[4,10,128,256]{3,2,1,0:T(8,128)(2,1)S(1)}, f32[4,10,40,256]{3,2,1,0:T(8,128)S(1)}, s32[40,128]{1,0:T(8,128)S(1)}, bf16[160,256]{1,0:T(8,128)(2,...) custom-call(s32[8,128]{1,0:T(8,128)S(1)} %get-tuple-element.20.lengths_ref, ...), custom_call_target="tpu_custom_call" | custom-call | flops 13762560 | bytes 5160960 | tf_op jit(solution)/shard_map/tables/pallas_call | solution.py:498
  7.4 0.0 collective-permute-done.1.far_ref
  7.4 0.4 %far_part.1.arrival_ref = f32[160,256]{1,0:T(8,128)S(1)} custom-call(bf16[32,256]{1,0:T(8,128)(2,1)S(1)} %collective-permute-done.1.far_ref, bf16[160,256]{1,0:T(8,128)(2,1)S(1)} %get-tuple-element.30.choice_ref, bf16[8,128,128]{2,1,0:T(8,128)(2,1)S(1)} %get-tuple-element.25.kernels_ref, f32[160,256]{1,0:T(8,128)S(1)} %get-tuple-element.31.own_ref), custom_call_target="tpu_custom_call" | custom-call | tf_op jit(solution)/shard_map/far_part/pallas_call | solution.py:522
  7.8 0.0 copy-start
  7.8 0.0 collective-permute-done.near_ref
  7.8 1.1 %transform.1 = bf16[32,8,128]{2,1,0:T(8,128)(2,1)S(1)} custom-call(s32[8,128]{1,0:T(8,128)S(1)} %get-tuple-element.20.lengths_ref, s32[10,128]{1,0:T(8,128)S(1)} %get-tuple-element.21.wave_ref, bf16[32,256]{1,0:T(8,128)(2,1)S(1)} %collective-permute-done.near_ref, bf16[160,256]{1,0:T(8,128)(2,1)S(1)} %get-tuple-element.28.choice_ref, ...), custom_call_target="tpu_custom_call" | custom-call | tf_op jit(solution)/shard_map/transform/pallas_call | solution.py:526
  8.9 12.2 %all_to_all.5 = bf16[32,8,128]{2,1,0:T(8,128)(2,1)S(1)} all-to-all(bf16[32,8,128]{2,1,0:T(8,128)(2,1)S(1)} %transform.1), channel_id=1, replica_groups=mesh['lat'=8,'lev'=4] {'lat','lev'}, dimensions={0} | all-to-all | bytes 131072 | tf_op jit(solution)/shard_map/all_to_all | solution.py:536
  21.1 0.0 copy-done
  21.1 1.7 %legendre.1 = bf16[16,40,1280]{2,1,0:T(8,128)(2,1)} custom-call(s32[40,128]{1,0:T(8,128)S(1)} %get-tuple-element.26.limits_ref, bf16[256,128]{1,0:T(8,128)(2,1)S(1)} %bitcast.7, bf16[256,256]{1,0:T(8,128)(2,1)S(1)} %get-tuple-element.34.order_ref, bf16[1280,1280]{1,0:T(8,128)(2,1)S(1)} %bitcast.6), custom_call_target="tpu_custom_call" | custom-call | tf_op jit(solution)/shard_map/legendre/pallas_call | solution.py:541
Async XLA Ops:
  1.1 6.2 %collective-permute-start.1 = (bf16[32,256]{1,0:T(8,128)(2,1)S(1)}, bf16[32,256]{1,0:T(8,128)(2,1)S(1)}, u32[]{:S(2)}, u32[]{:S(2)}) collective-permute-start(bf16[32,256]{1,0:T(8,128)(2,1)S(1)} %get-tuple-element.29), channel_id=1, source_target_pairs={{4,8},{5,9},{6,10},{7,11},{12,16},{13,17},{14,18},{15,19},{20,24},... | collective-permute-start | bytes 49160 | tf_op jit(solution)/shard_map/ppermute | solution.py:490
  1.7 6.1 %collective-permute-start = (bf16[32,256]{1,0:T(8,128)(2,1)S(1)}, bf16[32,256]{1,0:T(8,128)(2,1)S(1)}, u32[]{:S(2)}, u32[]{:S(2)}) collective-permute-start(bf16[32,256]{1,0:T(8,128)(2,1)S(1)} %get-tuple-element.27), channel_id=1, source_target_pairs={{0,4},{4,0},{8,12},{12,8},{16,20},{20,16},{24,28},{28,24},{1,5},{5... | collective-permute-start | bytes 49160 | tf_op jit(solution)/shard_map/ppermute | solution.py:489
  7.8 13.3 %copy-start = (bf16[40,32,1280]{2,1,0:T(8,128)(2,1)S(1)}, bf16[40,32,1280]{2,1,0:T(8,128)(2,1)}, u32[]{:S(2)}) copy-start(bf16[40,32,1280]{2,1,0:T(8,128)(2,1)} %param.15) | copy-start | bytes 9830404
